TPU v7x, 128 devices: a whole 4x4x4 slice. The times are simulated.
128 devices in a mesh: seq: 16 (over y, x), head: 8 (over z, core).
Axes of the slice: x: 4, y: 4, z: 4, core: 2. Of those that a mesh axis runs over, the one named last changes fastest.
Arguments:
- token_ids: int32 [2, 24], replicated, may hold values from 0 to 64127
- lengths: int32 [24], replicated, may hold values from 4096 to 16384, as said below
- embedding: bfloat16 [64128, 8192], P('head', 'seq'), may hold values from -100 to 100
- norm_gain: bfloat16 [8192], P('seq'), may hold values from 0.099609375 to 1.8984375
- w_qkv: bfloat16 [8192, 8, 1280], P('seq', 'head'), may hold values from -0.0625 to 0.0625
- k_cache: bfloat16 [24, 8, 16384, 128], P(None, 'head', 'seq'), may hold values from -110 to 110
- v_cache: bfloat16 [24, 8, 16384, 128], P(None, 'head', 'seq'), may hold values from -24 to 24
- w_out: bfloat16 [8, 1024, 8192], P('head', None, 'seq'), may hold values from -0.0625 to 0.0625
Outputs:
- attn_out: bfloat16 [2, 24, 8192], P(None, None, 'seq')
Inputs may be any that keep to these rules, and one draw needn't show every extreme that they name: `lengths`: at least one sequence has 16384 cached positions.
All inputs are finite; a program needn't handle non-finite values.
Results may differ from a plain program's by a relative error of at most 0.012.
The roundings to bfloat16 on the way count: a program that leaves them out, or rounds other values in their place, can miss the bound.
Values may be sent and summed in bfloat16 or wider, within the bound.
No kernel may reach another device: no remote copies, remote signals or barrier semaphores. Data moves between devices by JAX's collectives and lax.ppermute only.
A program may use at most 128 MiB of HBM per device.

v0:
```python
import jax
import jax.numpy as jnp
from jax import lax
from jax.sharding import PartitionSpec as P

D = 8192


rope_base = 500000.0
epsilon = 1e-05
negative = -1e30


def rope_tables(positions, head_dim):
    half_dim = head_dim // 2
    exponent = jnp.arange(half_dim, dtype=jnp.float32) * (2.0 / head_dim)
    frequency = jnp.power(jnp.float32(rope_base), -exponent)
    angles = positions.astype(jnp.float32)[:, None] * frequency[None, :]
    return (jnp.cos(angles), jnp.sin(angles))


def rotate(block, cosine, sine_part):
    half_dim = block.shape[-1] // 2
    first_half = block[..., :half_dim]
    second_half = block[..., half_dim:]
    return jnp.concatenate(
        [
            first_half * cosine - second_half * sine_part,
            second_half * cosine + first_half * sine_part,
        ],
        axis=-1,
    )


def finish(summed, squares, positions, group, head_dim):
    count_rows = summed.shape[0]
    normed = summed * lax.rsqrt(squares / D + epsilon)
    normed = normed.reshape(count_rows, -1, group + 2, head_dim)
    cosine, sine_part = rope_tables(positions, head_dim)
    query_rows = rotate(
        normed[:, :, :group], cosine[:, None, None, :], sine_part[:, None, None, :]
    ) * head_dim ** (-0.5)
    new_key = rotate(normed[:, :, group], cosine[:, None, :], sine_part[:, None, :])
    new_value = normed[:, :, group + 1]
    return (
        query_rows.astype(jnp.bfloat16),
        new_key.astype(jnp.bfloat16),
        new_value.astype(jnp.bfloat16),
    )


def body(token_ids, lengths, embedding, norm_gain, w_qkv, k_cache, v_cache, w_out):
    vocab_dev = embedding.shape[0]
    kv_dev = w_qkv.shape[1]
    head_dim = k_cache.shape[3]
    group = w_out.shape[1] // head_dim
    cache_dev = k_cache.shape[2]
    row_count = lengths.shape[0]
    flat_ids = token_ids.reshape(-1) - lax.axis_index("head") * vocab_dev
    inside = (flat_ids >= 0) & (flat_ids < vocab_dev)
    picked = jnp.take(embedding, jnp.clip(flat_ids, 0, vocab_dev - 1), axis=0)
    picked = jnp.where(inside[:, None], picked.astype(jnp.float32), 0.0)
    gathered = lax.psum(picked.astype(jnp.bfloat16), "head")
    widened = gathered.astype(jnp.float32)
    squares = jnp.sum(widened * widened, axis=1, keepdims=True)
    scaled = (widened * norm_gain.astype(jnp.float32)[None, :]).astype(jnp.bfloat16)
    partial_value = jnp.dot(
        scaled, w_qkv.reshape(w_qkv.shape[0], -1), preferred_element_type=jnp.float32
    )
    positions = (lengths[None, :] + jnp.arange(2, dtype=jnp.int32)[:, None]).reshape(-1)
    summed, total_squares = lax.psum((partial_value, squares), "seq")
    query_rows, new_key, new_value = finish(summed, total_squares, positions, group, head_dim)
    query_rows = (
        query_rows.reshape(2, row_count, kv_dev, group, head_dim)
        .transpose(1, 2, 0, 3, 4)
        .reshape(row_count, kv_dev, 2 * group, head_dim)
    )
    new_key = new_key.reshape(2, row_count, kv_dev, head_dim).transpose(1, 2, 0, 3)
    new_value = new_value.reshape(2, row_count, kv_dev, head_dim).transpose(1, 2, 0, 3)
    cache_positions = lax.axis_index("seq") * cache_dev + jnp.arange(cache_dev, dtype=jnp.int32)
    visible = (cache_positions[None, :] < lengths[:, None])[:, None, None, :]
    scores = jnp.einsum("rgqd,rgpd->rgqp", query_rows, k_cache, preferred_element_type=jnp.float32)
    masked = jnp.where(visible, scores, negative)
    local_top = jnp.max(masked, axis=3, keepdims=True)
    exponentials = jnp.where(visible, jnp.exp(masked - local_top), 0.0)
    local_sum = jnp.sum(exponentials, axis=3, keepdims=True)
    partial_out = jnp.einsum(
        "rgqp,rgpd->rgqd",
        exponentials.astype(jnp.bfloat16),
        v_cache,
        preferred_element_type=jnp.float32,
    )
    merged_top = lax.pmax(local_top, "seq")
    factor = jnp.exp(local_top - merged_top)
    merged_out, merged_sum = lax.psum((partial_out * factor, local_sum * factor), "seq")
    step_of_query = jnp.arange(2 * group, dtype=jnp.int32) // group
    allowed = (jnp.arange(2, dtype=jnp.int32)[None, :] <= step_of_query[:, None])[None, None]
    new_scores = jnp.einsum(
        "rgqd,rgsd->rgqs", query_rows, new_key, preferred_element_type=jnp.float32
    )
    new_masked = jnp.where(allowed, new_scores, negative)
    overall = jnp.maximum(merged_top, jnp.max(new_masked, axis=3, keepdims=True))
    old_scale = jnp.exp(merged_top - overall)
    new_weights = jnp.where(allowed, jnp.exp(new_masked - overall), 0.0)
    numerator = merged_out * old_scale + jnp.einsum(
        "rgqs,rgsd->rgqd",
        new_weights.astype(jnp.bfloat16),
        new_value,
        preferred_element_type=jnp.float32,
    )
    denominator = merged_sum * old_scale + jnp.sum(new_weights, axis=3, keepdims=True)
    attention = (numerator / denominator).astype(jnp.bfloat16)
    attention = (
        attention.reshape(row_count, kv_dev, 2, group, head_dim)
        .transpose(2, 0, 1, 3, 4)
        .reshape(2 * row_count, kv_dev * group * head_dim)
    )
    terms = jnp.dot(
        attention, w_out.reshape(kv_dev * group * head_dim, -1), preferred_element_type=jnp.float32
    )
    projected = lax.psum(terms, "head")
    return projected.astype(jnp.bfloat16).reshape(2, row_count, -1)


def solution(mesh):
    return jax.shard_map(
        body,
        mesh=mesh,
        in_specs=(
            P(),
            P(),
            P("head", "seq"),
            P("seq"),
            P("seq", "head", None),
            P(None, "head", "seq", None),
            P(None, "head", "seq", None),
            P("head", None, "seq"),
        ),
        out_specs=P(None, None, "seq"),
        check_vma=False,
    )
```

profile of v0, /device:TPU:1, one launch (start us, length us, event | category | flops | bytes accessed | tf_op | source)
XLA Modules:
  0.0 390.8 jit_solution(4361056466421666420)
XLA Ops:
  6.5 0.0 copy-start
  6.5 0.0 copy-start.2
  6.5 0.0 all-reduce.3.cloned.1.call-start
  6.5 0.8 compare_and_fusion.1
  7.3 0.7 subtract_clamp_fusion
  8.0 0.1 min.18
  8.1 0.1 min.16
  8.2 0.1 and.35
  8.3 0.7 convert_element_type.77
  9.0 5.1 %gather_fusion = bf16[48,512]{1,0:T(8,128)(2,1)S(1)} fusion(bf16[8016,512]{1,0:T(8,128)(2,1)} %param.10, s32[1024]{0:T(1024)S(1)} %pad_clamp_fusion), kind=kCustom, calls=%fused_computation | custom fusion | bytes 98496 | tf_op jit(solution)/shard_map/jit(_take)/gather | solution.py:61
  14.0 0.1 select_convert_fusion
  14.1 25.3 %psum.42 = bf16[48,512]{1,0:T(8,128)(2,1)S(1)} all-reduce(bf16[48,512]{1,0:T(8,128)(2,1)S(1)} %select_convert_fusion), channel_id=1, replica_groups=mesh['seq'=16,'head'=8] {'head'}, use_global_device_ids=true, to_apply=%region_0.1 | all-reduce | flops 24576 | bytes 98304 | tf_op jit(solution)/shard_map/psum | solution.py:63
  39.4 0.0 copy-done
  39.4 1.0 fusion.4
  40.4 0.0 all-reduce.3.cloned.1.call-update
  40.5 0.0 all-reduce.5.cloned.1.call-start
  40.5 0.1 fusion.27
  40.6 0.0 copy-done.2
  40.7 0.1 broadcast_compare_fusion
  40.8 33.6 %psum.44 = f32[48,1]{0,1:T(1,128)S(1)} all-reduce(f32[48,1]{0,1:T(1,128)S(1)} %bitcast.110), channel_id=1, replica_groups=mesh['seq'=16,'head'=8] {'seq'}, use_global_device_ids=true, to_apply=%region_3.4 | all-reduce | flops 48 | bytes 384 | tf_op jit(solution)/shard_map/psum | solution.py:71
  74.4 0.1 convert_element_type.80
  74.5 0.2 multiply_cosine_fusion.1
  74.6 50.5 %all-reduce.3.cloned.1.call-done = f32[48,1280]{1,0:T(8,128)} async-done(((f32[48,1280]{1,0:T(8,128)}), f32[48,1280]{1,0:T(8,128)}) %all-reduce.3.cloned.1.call-update) | async-done | bytes 245776 | tf_op jit(solution)/shard_map/psum | solution.py:71
  125.1 1.0 broadcast_multiply_fusion
  126.2 0.2 fusion.40
  126.5 0.1 multiply_subtract_fusion
  126.6 4.7 %select_reduce_fusion = (f32[24,16]{1,0:T(8,128)S(1)}, f32[24,16,1024]{2,1,0:T(8,128)S(1)}) fusion(pred[24,1024]{1,0:T(8,128)(4,1)S(1)} %broadcast_compare_fusion, bf16[24,1,1024,128]{3,2,1,0:T(8,128)(2,1)} %param.13, f32[2,24,1,8,64]{4,3,1,0,2:T(8,128)S(1)} %bitcast.102, f32[2,24,1,8,64]{4,3,1,0,2:T(8,128)S(1)} %bitcast.100), kind=kOutput, calls=%fused_computation.6 | convolution fusion | flops 101596800 | bytes 8087040 | tf_op jit(solution)/shard_map/rgqd,rgpd->rgqp/dot_general | solution.py:82
  131.2 58.2 %pmax.7 = f32[24,1,16,1]{2,0,3,1:T(8,128)S(1)} all-reduce(f32[24,1,16,1]{2,0,3,1:T(8,128)S(1)} %bitcast.105), channel_id=1, replica_groups=mesh['seq'=16,'head'=8] {'seq'}, use_global_device_ids=true, to_apply=%region_5.6 | all-reduce | flops 384 | bytes 3072 | tf_op jit(solution)/shard_map/pmax | solution.py:93
  189.4 0.5 fusion.6
  189.9 0.3 fusion.60
  190.2 55.6 %psum.46 = f32[24,1,16,1]{2,0,3,1:T(8,128)S(1)} all-reduce(f32[24,1,16,1]{2,0,3,1:T(8,128)S(1)} %get-tuple-element.11), channel_id=1, replica_groups=mesh['seq'=16,'head'=8] {'seq'}, use_global_device_ids=true, to_apply=%region_9.10 | all-reduce | flops 384 | bytes 3072 | tf_op jit(solution)/shard_map/psum | solution.py:95
  245.8 4.6 %fusion.13 = f32[24,1,16,128]{3,2,0,1:T(8,128)} fusion(bf16[24,1,1024,128]{3,2,1,0:T(8,128)(2,1)} %param.14, f32[24,16,1024]{2,1,0:T(8,128)S(1)} %get-tuple-element.17, f32[24,16]{1,0:T(8,128)S(1)} %get-tuple-element.16, pred[24,1024]{1,0:T(8,128)(4,1)S(1)} %broadcast_compare_fusion, f32[24,16]{1,0:T(8,128)S(1)} %get-tuple-element.12), kind=kOutput, calls=%fused_computation.15 | convolution fusion | flops 102285312 | bytes 8088576 | tf_op jit(solution)/shard_map/rgqp,rgpd->rgqd/dot_general | solution.py:87
  250.5 0.0 copy-start.1
  250.5 0.0 all-reduce.5.cloned.1.call-update
  250.5 0.1 fusion.52
  250.6 107.5 %all-reduce.5.cloned.1.call-done = f32[24,1,16,128]{3,2,0,1:T(8,128)} async-done(((f32[24,1,16,128]{3,2,0,1:T(8,128)}), f32[24,1,16,128]{3,2,0,1:T(8,128)}) %all-reduce.5.cloned.1.call-update) | async-done | bytes 196624 | tf_op jit(solution)/shard_map/psum | solution.py:95
  358.1 1.2 fusion.17
  359.3 0.0 copy-done.1
  359.3 0.3 fusion.18
  359.6 24.3 %psum.47 = bf16[48,512]{1,0:T(8,128)(2,1)} all-reduce(f32[48,512]{1,0:T(8,128)S(1)} %fusion.18), channel_id=1, replica_groups=mesh['seq'=16,'head'=8] {'head'}, use_global_device_ids=true, to_apply=%region_11.12 | all-reduce | flops 24576 | bytes 147456 | tf_op jit(solution)/shard_map/psum | solution.py:121
  (18 shorter events, 0.2 us)
Async XLA Ops:
  6.5 32.9 %copy-start = (bf16[512,1,1280]{2,0,1:T(8,128)(2,1)S(1)}, bf16[512,1,1280]{2,0,1:T(8,128)(2,1)}, u32[]{:S(2)}) copy-start(bf16[512,1,1280]{2,0,1:T(8,128)(2,1)} %param.12) | copy-start | bytes 3932164
  6.5 34.1 %copy-start.2 = (s32[24]{0:T(128)S(1)}, s32[24]{0:T(128)}, u32[]{:S(2)}) copy-start(s32[24]{0:T(128)} %param.9) | copy-start | bytes 292
  6.5 118.6 %all-reduce.3.cloned.1.call-start = ((), (), s32[]{:S(2)}) async-start(), calls=%async_computation | async-start | bytes 491520 | tf_op jit(solution)/shard_map/psum | solution.py:71
  40.5 317.6 %all-reduce.5.cloned.1.call-start = ((), (), s32[]{:S(2)}) async-start(), calls=%async_computation.1 | async-start | bytes 393216 | tf_op jit(solution)/shard_map/psum | solution.py:95
  250.5 108.8 %copy-start.1 = (bf16[1,1024,512]{2,1,0:T(8,128)(2,1)S(1)}, bf16[1,1024,512]{2,1,0:T(8,128)(2,1)}, u32[]{:S(2)}) copy-start(bf16[1,1024,512]{2,1,0:T(8,128)(2,1)} %param.15) | copy-start | bytes 3145732
Sparse Core Ops, SparseCore 0:
  40.6 84.4 all-reduce.2
  250.6 107.4 all-reduce.4
where the time goes:
time: 393 us; the launch traced here: 391 us
  blocking collectives  197 us (50%)
  waiting for transfers between devices  158 us (40%)
  between operations  13.6 us (3%)
  matrix products  12 us (3%)
  local copies, waits for them, and re-layouts  5.51 us (1%)
  other arithmetic  4.57 us (1%)
    psum x1, waiting for transfers between devices, body(): lax.psum((partial_out * factor, local_sum * factor), 'seq')  108 us
    pmax x1, blocking collectives, body(): merged_top = lax.pmax(local_top, 'seq')  58.2 us
    psum x1, blocking collectives, body(): lax.psum((partial_out * factor, local_sum * factor), 'seq')  55.6 us
    psum x1, waiting for transfers between devices, body(): summed, total_squares = lax.psum((partial_value, squares), 'seq')  50.5 us
    psum x1, blocking collectives, body(): summed, total_squares = lax.psum((partial_value, squares), 'seq')  33.6 us
    psum x1, blocking collectives, body(): gathered = lax.psum(picked.astype(jnp.bfloat16), 'head')  25.3 us
    psum x1, blocking collectives, body(): projected = lax.psum(terms, 'head')  24.3 us
  transfers between devices with their start and end apart: 2, of which 2 were waited for; matrix products, arithmetic and copies ran while one was open for 0% of the time, Pallas kernels for 0%

commit v1 on v0

v1 whole, which is shorter than its diff:
```python
import functools

import jax
import jax.numpy as jnp
from jax import lax
from jax.experimental import pallas as pl
from jax.experimental.pallas import tpu as pltpu
from jax.sharding import PartitionSpec as P

D = 8192
TILE = 16
LANES = 128
SUB = 8

rope_base = 500000.0
epsilon = 1e-05
negative = -1e30

VMEM = pl.BlockSpec(memory_space=pltpu.VMEM)
SMEM = pl.BlockSpec(memory_space=pltpu.SMEM)
ANY = pl.BlockSpec(memory_space=pl.ANY)


def in_vmem(array):
    return pltpu.with_memory_space_constraint(array, pltpu.VMEM)


def in_hbm(array):
    return pltpu.with_memory_space_constraint(array, pltpu.HBM)


def call(kernel, name, out, in_specs, scratch=(), limit=4):
    return pl.pallas_call(
        kernel,
        out_shape=jax.ShapeDtypeStruct(*out),
        in_specs=in_specs,
        out_specs=VMEM,
        scratch_shapes=list(scratch),
        compiler_params=pltpu.CompilerParams(vmem_limit_bytes=limit << 20),
        name=name,
    )


def swap(array, axis_name):
    return lax.all_to_all(array, axis_name, 0, 0, tiled=True)


SEQ_MASKS = (1, 3, 4, 12)


def place_of(me, source):
    differ = me ^ source
    return differ ^ ((differ >> 1) & 5)


def rope_frequency(head_dim):
    exponent = jnp.arange(head_dim // 2, dtype=jnp.float32) * (2.0 / head_dim)
    frequency = jnp.power(jnp.float32(rope_base), -exponent)
    return jnp.concatenate([frequency, frequency])[None, :]


def cos_sin(angles):
    turn = jnp.floor(angles * 0.6366197723675814 + 0.5)
    rest = ((angles - turn * 1.5703125) - turn * 0.00048351287841796875) - turn * 3.13916478589249e-07
    square = rest * rest
    sine = ((-1.9515295891e-4 * square + 8.3321608736e-3) * square - 1.6666654611e-1) * square
    sine = sine * rest + rest
    cosine = (2.443315711809948e-5 * square - 1.388731625493765e-3) * square
    cosine = (cosine + 4.166664568298827e-2) * square * square - 0.5 * square + 1.0
    quarter = turn.astype(jnp.int32) & 3
    odd = (quarter & 1) == 1
    first, second = jnp.where(odd, sine, cosine), jnp.where(odd, cosine, sine)
    return (
        jnp.where((quarter == 1) | (quarter == 2), -first, first),
        jnp.where(quarter >= 2, -second, second),
    )


def pick_kernel(
    cache_dev, ids_ref, lengths_ref, frequency_ref, table_ref, far_w_ref,
    x_ref, rope_ref, limits_ref, w_ref, held, sem, w_sem,
):
    vocab_dev, feat = table_ref.shape
    steps, rows = ids_ref.shape
    tokens = steps * rows
    first = lax.axis_index("head") * vocab_dev
    places = []
    for i in range(tokens):
        local = ids_ref[i // rows, i % rows] - first
        inside = (local >= 0) & (local < vocab_dev)
        local = jnp.clip(local, 0, vocab_dev - 1)
        within = local & (TILE - 1)
        pltpu.make_async_copy(
            table_ref.at[pl.ds(pl.multiple_of(local - within, TILE), TILE)],
            held.at[pl.ds(i * TILE, TILE)],
            sem,
        ).start()
        places.append(jnp.where(inside, i * TILE + within, -1))
    w_copy = pltpu.make_async_copy(far_w_ref, w_ref, w_sem)
    w_copy.start()

    me = lax.axis_index("seq")
    near = LANES // (2 * SUB)
    sub = lax.broadcasted_iota(jnp.int32, (SUB, LANES), 0)
    lane = lax.broadcasted_iota(jnp.int32, (SUB, LANES), 1)
    position = jnp.zeros((SUB, LANES), jnp.int32)
    limits = jnp.zeros((SUB, LANES), jnp.int32)
    for g in range(rows // near):
        position = jnp.where(sub == g, lengths_ref[g * near + me // 2] + me % 2, position)
        for r in range(near):
            here = (sub == g) & (lane // (2 * SUB) == r)
            limits = jnp.where(here, lengths_ref[g * near + r], limits)
    limits_ref[...] = limits - me * cache_dev
    cosine, sine = cos_sin(position.astype(jnp.float32) * frequency_ref[...])
    rope_ref[:SUB] = cosine
    rope_ref[SUB:] = jnp.where(lane < LANES // 2, -sine, sine)

    row = lax.broadcasted_iota(jnp.int32, (tokens, 1), 0)
    choice = jnp.full((tokens, 1), -1, jnp.int32)
    for i in range(tokens):
        choice = jnp.where(row == i, places[i], choice)
    column = lax.broadcasted_iota(jnp.int32, (tokens, tokens * TILE), 1)
    select = jnp.where(column == choice, 1.0, 0.0).astype(jnp.bfloat16)
    pltpu.make_async_copy(table_ref.at[pl.ds(0, tokens * TILE)], held, sem).wait()
    picked = jnp.dot(select, held[...], preferred_element_type=jnp.float32)
    x_ref[...] = picked.astype(jnp.bfloat16)
    w_copy.wait()


def project_kernel(x_ref, gain_ref, w_ref, out_ref):
    tokens = x_ref.shape[0]
    count, own, width = out_ref.shape
    width -= LANES
    row = lax.broadcasted_iota(jnp.int32, (count * SUB, tokens), 0)
    column = lax.broadcasted_iota(jnp.int32, (count * SUB, tokens), 1)
    owner, k = row // SUB, row % SUB
    token = (owner % 2) * (tokens // 2) + owner // 2 + (count // 2) * k
    spread = jnp.where((column == token) & (k < own), 1.0, 0.0).astype(jnp.bfloat16)
    x = jnp.dot(spread, x_ref[...], preferred_element_type=jnp.float32)
    squares = jnp.sum(x * x, axis=1, keepdims=True)
    scaled = (x * gain_ref[...]).astype(jnp.bfloat16)
    partial = jnp.dot(scaled, w_ref[...], preferred_element_type=jnp.float32)
    squares = jnp.broadcast_to(squares, (count * SUB, LANES))
    for j in range(count):
        out_ref[j, :, :width] = partial[j * SUB : j * SUB + own]
        out_ref[j, :, width:] = squares[j * SUB : j * SUB + own]


def finish_kernel(parts_ref, rope_ref, out_ref):
    _, own, width = parts_ref.shape
    head_dim = out_ref.shape[1]
    summed = parts_ref[0]
    for j in range(1, parts_ref.shape[0]):
        summed = summed + parts_ref[j]
    scale = lax.rsqrt(summed[:, width - LANES :] / D + epsilon)
    cosine, sine_part = rope_ref[:own], rope_ref[SUB : SUB + own]
    group = (width - LANES) // head_dim - 2
    blocks = []
    for b in range(group + 2):
        block = summed[:, b * head_dim : (b + 1) * head_dim] * scale
        if b <= group:
            block = block * cosine + pltpu.roll(block, head_dim // 2, 1) * sine_part
        if b < group:
            block = block * head_dim ** (-0.5)
        blocks.append(block)
    rows = [blocks[b][k : k + 1] for k in range(own) for b in range(group)]
    rows += [blocks[group], blocks[group + 1]]
    rows.append(jnp.zeros((out_ref.shape[0] - own * (group + 2), head_dim), jnp.float32))
    out_ref[...] = jnp.concatenate(rows, axis=0).astype(jnp.bfloat16)


def attend_kernel(
    limits_ref, first_ref, second_ref, k_ref, v_ref, out_ref, rows_ref, scores_ref
):
    row_count, cache_dev, head_dim = k_ref.shape
    count = rows_ref.shape[0]
    rows_ref[: count // 2] = first_ref[...]
    rows_ref[count // 2 :] = second_ref[...]
    per_row = 2 * SUB
    near = LANES // per_row
    groups = row_count // near
    chunk = 256
    me = lax.axis_index("seq")
    lane = lax.broadcasted_iota(jnp.int32, (1, LANES), 1)
    position = lax.broadcasted_iota(jnp.int32, (chunk, LANES), 0)
    slot = lax.broadcasted_iota(jnp.int32, (LANES, LANES), 0)
    rows = [rows_ref[place_of(me, j)].astype(jnp.float32) for j in range(count)]
    new_keys = jnp.concatenate([part[groups * SUB :] for part in rows], axis=0)
    new_values = pltpu.roll(new_keys, LANES - groups, 0).astype(jnp.bfloat16)
    new_keys = new_keys.astype(jnp.bfloat16)
    tops, totals = [], []
    for g in range(groups):
        turned = jnp.concatenate([part[g * SUB : (g + 1) * SUB] for part in rows], axis=0).T
        blocks = [
            jnp.where(lane // per_row == r, turned, 0.0).astype(jnp.bfloat16) for r in range(near)
        ]
        weights = jnp.concatenate(blocks, axis=0)
        limit = limits_ref[g : g + 1]

        fresh = jnp.dot(new_keys, turned.astype(jnp.bfloat16), preferred_element_type=jnp.float32)
        seen = (
            (slot % SUB == g)
            & (slot // per_row == lane // per_row)
            & (slot // SUB <= lane // SUB)
            & (me == 0)
        )
        fresh = jnp.where(seen, fresh, negative)
        top = jnp.max(fresh, axis=0, keepdims=True)
        for c in range(cache_dev // chunk):
            keys = jnp.concatenate(
                [k_ref[g * near + r, pl.ds(c * chunk, chunk)] for r in range(near)], axis=1
            )
            scores = jnp.dot(keys, weights, preferred_element_type=jnp.float32)
            scores = jnp.where(position < limit - c * chunk, scores, negative)
            scores_ref[g, pl.ds(c * chunk, chunk)] = scores
            top = jnp.maximum(top, jnp.max(scores, axis=0, keepdims=True))

        fresh = jnp.exp(fresh - top)
        total = jnp.sum(fresh, axis=0, keepdims=True)
        parts = []
        for c in range(cache_dev // chunk):
            weight = jnp.exp(scores_ref[g, pl.ds(c * chunk, chunk)] - top)
            total = total + jnp.sum(weight, axis=0, keepdims=True)
            parts.append(weight.astype(jnp.bfloat16).T)
        parts = jnp.concatenate(parts, axis=1)
        value = []
        for r in range(0, near, 2):
            both = jnp.dot(
                parts[r * per_row : (r + 2) * per_row],
                jnp.concatenate([v_ref[g * near + r], v_ref[g * near + r + 1]], axis=1),
                preferred_element_type=jnp.float32,
            )
            value += [both[:per_row, :head_dim], both[per_row:, head_dim:]]
        value = jnp.concatenate(value, axis=0) + jnp.dot(
            fresh.T.astype(jnp.bfloat16), new_values, preferred_element_type=jnp.float32
        )
        for j in range(count):
            out_ref[j, pl.ds(g * SUB, SUB)] = value[j * SUB : (j + 1) * SUB]
        tops.append(top)
        totals.append(total)
    spare = jnp.zeros((SUB - 2 * groups, LANES), jnp.float32)
    stats = jnp.concatenate(tops + totals + [spare], axis=0)
    for j in range(count):
        turn = (LANES - SUB * j) % LANES
        out_ref[j, pl.ds(groups * SUB, SUB)] = pltpu.roll(stats, turn, 1) if turn else stats


def merge_kernel(parts_ref, out_ref):
    count, rows, head_dim = parts_ref.shape
    groups = rows // SUB - 1
    stats = parts_ref[:, groups * SUB :]
    top = stats[0]
    for j in range(1, count):
        top = jnp.maximum(top, stats[j])
    factors = [jnp.exp(stats[j] - top) for j in range(count)]
    denominator = factors[0] * pltpu.roll(stats[0], SUB - groups, 0)
    for j in range(1, count):
        denominator = denominator + factors[j] * pltpu.roll(stats[j], SUB - groups, 0)
    shares = jnp.concatenate([factor / denominator for factor in factors], axis=0).T[:SUB]
    merged = []
    for g in range(groups):
        total = jnp.zeros((SUB, head_dim), jnp.float32)
        for j in range(count):
            column = j * SUB + g
            total = total + parts_ref[j, pl.ds(g * SUB, SUB)] * shares[:, column : column + 1]
        merged.append(total)
    out_ref[...] = jnp.concatenate(merged, axis=1).astype(jnp.bfloat16)


def output_kernel(first_ref, second_ref, w_ref, out_ref, attention_ref, held):
    count, heads, width = attention_ref.shape
    attention_ref[: count // 2] = first_ref[...]
    attention_ref[count // 2 :] = second_ref[...]
    head_dim = width // (out_ref.shape[0] // count)
    me = lax.axis_index("seq")
    for j in range(count):
        part = attention_ref[place_of(me, j)].astype(jnp.float32)
        for g in range(width // head_dim):
            held[g, pl.ds(j * heads, heads)] = part[:, g * head_dim : (g + 1) * head_dim]
    left = jnp.concatenate(
        [
            jnp.concatenate(
                [
                    held[g, pl.ds(step * heads + i, count // 2, stride=2 * heads)]
                    for i in range(heads)
                ],
                axis=1,
            )
            for step in range(2)
            for g in range(width // head_dim)
        ],
        axis=0,
    )
    out_ref[...] = jnp.dot(left.astype(jnp.bfloat16), w_ref[...], preferred_element_type=jnp.float32)


def spread(array, axis_name, masks, size):
    halves = (array[None],)
    for mask in masks:
        held = jnp.concatenate(halves, axis=0) if len(halves) == 2 else halves[0]
        halves = (held, lax.ppermute(held, axis_name, [(i, i ^ mask) for i in range(size)]))
    return halves


def double(array, axis_name, mask, size):
    pairs = [(i, i ^ mask) for i in range(size)]
    return array + lax.ppermute(array, axis_name, pairs)


def body(token_ids, lengths, embedding, norm_gain, w_qkv, k_cache, v_cache, w_out):
    n_seq, n_head = lax.axis_size("seq"), lax.axis_size("head")
    feat = embedding.shape[1]
    row_count, _, cache_dev, head_dim = k_cache.shape
    tokens = 2 * row_count
    own = tokens // n_seq
    width = w_qkv.shape[2]
    block = (own + 1) * SUB

    picked, rope, limits, w_near = pl.pallas_call(
        functools.partial(pick_kernel, cache_dev),
        out_shape=[
            jax.ShapeDtypeStruct((tokens, feat), jnp.bfloat16),
            jax.ShapeDtypeStruct((2 * SUB, LANES), jnp.float32),
            jax.ShapeDtypeStruct((SUB, LANES), jnp.int32),
            pltpu.VMEM((feat, width), jnp.bfloat16),
        ],
        in_specs=[SMEM, SMEM, VMEM, ANY, ANY],
        out_specs=[VMEM] * 4,
        scratch_shapes=[
            pltpu.VMEM((tokens * TILE, feat), jnp.bfloat16),
            pltpu.SemaphoreType.DMA,
            pltpu.SemaphoreType.DMA,
        ],
        compiler_params=pltpu.CompilerParams(vmem_limit_bytes=8 << 20),
        name="pick",
    )(
        in_hbm(token_ids),
        in_hbm(lengths),
        rope_frequency(head_dim),
        in_hbm(embedding),
        in_hbm(w_qkv.reshape(feat, width)),
    )
    for mask in (1, 2, 6):
        picked = double(picked, "head", mask, n_head)
    gain = norm_gain.astype(jnp.float32).reshape(1, feat)

    partial = call(
        project_kernel, "project", ((n_seq, own, width + LANES), jnp.float32), [VMEM] * 3
    )(picked, gain, in_vmem(w_near))
    partial = swap(partial, "seq")
    rows = call(finish_kernel, "finish", ((block, head_dim), jnp.bfloat16), [VMEM] * 2)(
        partial, rope
    )
    rows = spread(rows, "seq", SEQ_MASKS, n_seq)

    partial = call(
        attend_kernel,
        "attend",
        ((n_seq, block, head_dim), jnp.float32),
        [VMEM] * 5,
        [
            pltpu.VMEM((n_seq, block, head_dim), jnp.bfloat16),
            pltpu.VMEM((own, cache_dev, LANES), jnp.float32),
        ],
        8,
    )(limits, *rows, in_vmem(k_cache[:, 0]), in_vmem(v_cache[:, 0]))
    partial = swap(partial, "seq")
    attention = call(merge_kernel, "merge", ((SUB, own * head_dim), jnp.bfloat16), [VMEM])(
        partial
    )
    attention = spread(attention, "seq", SEQ_MASKS, n_seq)

    terms = call(
        output_kernel,
        "output",
        ((tokens, w_out.shape[2]), jnp.float32),
        [VMEM] * 3,
        [
            pltpu.VMEM((n_seq, SUB, own * head_dim), jnp.bfloat16),
            pltpu.VMEM((own, n_seq * SUB, head_dim), jnp.float32),
        ],
    )(*attention, in_vmem(w_out[0]))
    for mask in (1, 2, 6):
        terms = double(terms, "head", mask, n_head)
    return terms.astype(jnp.bfloat16).reshape(2, row_count, -1)


def solution(mesh):
    return jax.shard_map(
        body,
        mesh=mesh,
        in_specs=(
            P(),
            P(),
            P("head", "seq"),
            P("seq"),
            P("seq", "head", None),
            P(None, "head", "seq", None),
            P(None, "head", "seq", None),
            P("head", None, "seq"),
        ),
        out_specs=P(None, None, "seq"),
        check_vma=False,
    )
```

time: 393 us -> 97 us (0.25)
  blocking collectives: 197 us -> 24.8 us
  waiting for transfers between devices: 158 us -> 35.1 us
  starting transfers between devices: 0.04 us -> 26.8 us
  between operations: 13.6 us -> 0.12 us
  matrix products: 12 us -> 0 us
  Pallas kernels: 0 us -> 8.62 us
  local copies, waits for them, and re-layouts: 5.51 us -> 0.02 us
    psum x2 -> x0, waiting for transfers between devices: 158 us -> none  [the longest x1 108 us: body(): lax.psum((partial_out * factor, local_sum * factor), 'seq')]
    psum x4 -> x0, blocking collectives: 139 us -> none  [the longest x1 55.6 us: body(): lax.psum((partial_out * factor, local_sum * factor), 'seq')]
    pmax x1 -> x0, blocking collectives: 58.2 us -> none  [body(): merged_top = lax.pmax(local_top, 'seq')]
    ppermute x0 -> x14, waiting for transfers between devices: none -> 35.1 us  [the longest x8 24.3 us: spread(): lax.ppermute(held, axis_name, [(i, i ^ mask) for i in range(size)])]
    ppermute x0 -> x14, starting transfers between devices: none -> 26.8 us  [the longest x6 23.7 us: double(): return array + lax.ppermute(array, axis_name, pairs)]
    all_to_all x0 -> x2, blocking collectives: none -> 24.8 us  [swap(): return lax.all_to_all(array, axis_name, 0, 0, tiled=True)]
    dot_general x6 -> x0, matrix products: 12 us -> none  [the longest x1 4.65 us: body(): jnp.einsum('rgqd,rgpd->rgqp', query_rows, k_cache, preferred_element_type...]
    pallas_call x0 -> x6, Pallas kernels: none -> 8.62 us  [the longest x1 3.76 us: body(): call(attend_kernel, 'attend', ((n_seq, block, head_dim), jnp.float32), [V...]
  transfers between devices with their start and end apart: 2 -> 14, of which waited for: 2 -> 14; matrix products, arithmetic and copies ran while one was open for 0% -> 0% of each run, Pallas kernels for 0% -> 0%
where the time goes in v1:
time: 97 us; the launch traced here: 96.3 us
  waiting for transfers between devices  35.1 us (36%)
  starting transfers between devices  26.8 us (28%)
  blocking collectives  24.8 us (26%)
  Pallas kernels  8.62 us (9%)
    all_to_all x2, blocking collectives, swap(): return lax.all_to_all(array, axis_name, 0, 0, tiled=True)  24.8 us
    ppermute x8, waiting for transfers between devices, spread(): lax.ppermute(held, axis_name, [(i, i ^ mask) for i in range(size)])  24.3 us
    ppermute x6, starting transfers between devices, double(): return array + lax.ppermute(array, axis_name, pairs)  23.7 us
    ppermute x6, waiting for transfers between devices, double(): return array + lax.ppermute(array, axis_name, pairs)  10.8 us
    pallas_call x1, Pallas kernels, body(): call(attend_kernel, 'attend', ((n_seq, block, head_dim), jnp.float32), [V...  3.76 us
    pallas_call x1, Pallas kernels, body(): pl.pallas_call(functools.partial(pick_kernel, cache_dev), out_shape=[jax....  3.73 us
    ppermute x8, starting transfers between devices, spread(): lax.ppermute(held, axis_name, [(i, i ^ mask) for i in range(size)])  3.15 us
  transfers between devices with their start and end apart: 14, of which 14 were waited for; matrix products, arithmetic and copies ran while one was open for 0% of the time, Pallas kernels for 0%

profile of v1, /device:TPU:1, one launch (start us, length us, event | category | flops | bytes accessed | tf_op | source)
XLA Modules:
  0.0 96.3 jit_solution(13647398082699076913)
XLA Ops:
  0.0 0.0 copy-start.2
  0.0 0.1 maximum_bitcast_fusion.frequency_ref
  0.1 0.0 slice-start
  0.1 0.0 slice-start.1
  0.1 0.0 copy-start
  0.1 3.7 %pick.1 = (bf16[48,512]{1,0:T(8,128)(2,1)S(1)}, f32[16,128]{1,0:T(8,128)S(1)}, s32[8,128]{1,0:T(8,128)S(1)}, bf16[512,1280]{1,0:T(8,128)(2,1)S(1)}) custom-call(s32[2,24]{1,0:T(2,128)} %ids_ref.1, s32[24]{0:T(128)} %lengths_ref.1, f32[1,128]{1,0:T(1,128)S(1)} %maximum_bitcast_fusion.frequency_ref, bf16[8016,512]{1,0:T(8,128)(2,1)} %table_ref.1, ...), custom_call_target="tpu_custom_call" | custom-call | tf_op jit(solution)/shard_map/pick/pallas_call | solution.py:319
  3.8 1.4 %collective-permute-start = (bf16[48,512]{1,0:T(8,128)(2,1)S(1)}, bf16[48,512]{1,0:T(8,128)(2,1)S(1)}, u32[]{:S(2)}, u32[]{:S(2)}) collective-permute-start(bf16[48,512]{1,0:T(8,128)(2,1)S(1)} %get-tuple-element.10), channel_id=1, source_target_pairs={{0,1},{1,0},{2,3},{3,2},{4,5},{5,4},{6,7},{7,6},{8,9},{9,8},{10,11... | collective-permute-start | bytes 147464 | tf_op jit(solution)/shard_map/ppermute | solution.py:307
  5.2 0.9 collective-permute-done
  6.1 2.0 %collective-permute-start.1 = (bf16[48,512]{1,0:T(8,128)(2,1)S(1)}, bf16[48,512]{1,0:T(8,128)(2,1)S(1)}, u32[]{:S(2)}, u32[]{:S(2)}) collective-permute-start(bf16[48,512]{1,0:T(8,128)(2,1)S(1)} %add.18), channel_id=1, source_target_pairs={{0,2},{1,3},{2,0},{3,1},{4,6},{5,7},{6,4},{7,5},{8,10},{9,11},{10,... | collective-permute-start | bytes 147464 | tf_op jit(solution)/shard_map/ppermute | solution.py:307
  8.1 1.5 %collective-permute-done.1 = bf16[48,512]{1,0:T(8,128)(2,1)S(1)} collective-permute-done((bf16[48,512]{1,0:T(8,128)(2,1)S(1)}, bf16[48,512]{1,0:T(8,128)(2,1)S(1)}, u32[]{:S(2)}, u32[]{:S(2)}) %collective-permute-start.1) | collective-permute-done | bytes 49184 | tf_op jit(solution)/shard_map/ppermute | solution.py:307
  9.6 3.6 %collective-permute-start.2 = (bf16[48,512]{1,0:T(8,128)(2,1)S(1)}, bf16[48,512]{1,0:T(8,128)(2,1)S(1)}, u32[]{:S(2)}, u32[]{:S(2)}) collective-permute-start(bf16[48,512]{1,0:T(8,128)(2,1)S(1)} %add.19), channel_id=1, source_target_pairs={{0,6},{1,7},{2,4},{3,5},{4,2},{5,3},{6,0},{7,1},{8,14},{9,15},{10,... | collective-permute-start | bytes 147464 | tf_op jit(solution)/shard_map/ppermute | solution.py:307
  13.1 0.0 copy-done.2
  13.1 1.5 %collective-permute-done.2 = bf16[48,512]{1,0:T(8,128)(2,1)S(1)} collective-permute-done((bf16[48,512]{1,0:T(8,128)(2,1)S(1)}, bf16[48,512]{1,0:T(8,128)(2,1)S(1)}, u32[]{:S(2)}, u32[]{:S(2)}) %collective-permute-start.2) | collective-permute-done | bytes 49184 | tf_op jit(solution)/shard_map/ppermute | solution.py:307
  14.6 0.5 project.1
  15.1 14.6 %all_to_all.10.parts_ref = f32[16,3,1408]{2,1,0:T(4,128)S(1)} all-to-all(f32[16,3,1408]{2,1,0:T(4,128)S(1)} %project.1), channel_id=1, replica_groups=mesh['seq'=16,'head'=8] {'seq'}, dimensions={0} | all-to-all | bytes 540672 | tf_op jit(solution)/shard_map/all_to_all | solution.py:45
  29.7 0.1 finish.1
  29.8 0.5 collective-permute-start.3
  30.3 2.4 %collective-permute-done.3 = bf16[1,32,128]{2,1,0:T(8,128)(2,1)S(1)} collective-permute-done((bf16[1,32,128]{2,1,0:T(8,128)(2,1)S(1)}, bf16[1,32,128]{2,1,0:T(8,128)(2,1)S(1)}, u32[]{:S(2)}, u32[]{:S(2)}) %collective-permute-start.3) | collective-permute-done | bytes 8224 | tf_op jit(solution)/shard_map/ppermute | solution.py:301
  32.7 0.3 collective-permute-start.4
  33.0 3.5 %collective-permute-done.4 = bf16[2,32,128]{2,1,0:T(8,128)(2,1)S(1)} collective-permute-done((bf16[2,32,128]{2,1,0:T(8,128)(2,1)S(1)}, bf16[2,32,128]{2,1,0:T(8,128)(2,1)S(1)}, u32[]{:S(2)}, u32[]{:S(2)}) %collective-permute-start.4) | collective-permute-done | bytes 16416 | tf_op jit(solution)/shard_map/ppermute | solution.py:301
  36.5 0.0 collective-permute-start.5
  36.5 2.8 %collective-permute-done.5 = bf16[4,32,128]{2,1,0:T(8,128)(2,1)S(1)} collective-permute-done((bf16[4,32,128]{2,1,0:T(8,128)(2,1)S(1)}, bf16[4,32,128]{2,1,0:T(8,128)(2,1)S(1)}, u32[]{:S(2)}, u32[]{:S(2)}) %collective-permute-start.5) | collective-permute-done | bytes 32800 | tf_op jit(solution)/shard_map/ppermute | solution.py:301
  39.3 0.7 collective-permute-start.6
  39.9 3.8 %collective-permute-done.6.second_ref = bf16[8,32,128]{2,1,0:T(8,128)(2,1)S(1)} collective-permute-done((bf16[8,32,128]{2,1,0:T(8,128)(2,1)S(1)}, bf16[8,32,128]{2,1,0:T(8,128)(2,1)S(1)}, u32[]{:S(2)}, u32[]{:S(2)}) %collective-permute-start.6) | collective-permute-done | bytes 65568 | tf_op jit(solution)/shard_map/ppermute | solution.py:301
  43.7 0.0 slice-done
  43.7 0.0 slice-done.1
  43.7 0.0 copy-done
  43.7 0.0 copy-start.1
  43.7 3.8 %attend.1 = f32[16,32,128]{2,1,0:T(8,128)S(1)} custom-call(s32[8,128]{1,0:T(8,128)S(1)} %get-tuple-element.9.limits_ref, bf16[8,32,128]{2,1,0:T(8,128)(2,1)S(1)} %pad_maximum_fusion.first_ref, bf16[8,32,128]{2,1,0:T(8,128)(2,1)S(1)} %collective-permute-done.6.second_ref, bf16[24,1024,128]{2,1,0:T(8,128)(2,1)S(1)} %bitcast.12, bf16[24,1024,128]{2,1,0:T(8,128)(2,1)S(1)} %bitcast.13), custom_call_target="tpu_custom_call" | custom-call | tf_op jit(solution)/shard_map/attend/pallas_call | solution.py:356
  47.5 10.1 %all_to_all.11.parts_ref = f32[16,32,128]{2,1,0:T(8,128)S(1)} all-to-all(f32[16,32,128]{2,1,0:T(8,128)S(1)} %attend.1), channel_id=1, replica_groups=mesh['seq'=16,'head'=8] {'seq'}, dimensions={0} | all-to-all | bytes 524288 | tf_op jit(solution)/shard_map/all_to_all | solution.py:45
  57.6 0.3 merge.1
  57.9 0.4 collective-permute-start.7
  58.3 2.2 %collective-permute-done.7 = bf16[1,8,384]{2,1,0:T(8,128)(2,1)S(1)} collective-permute-done((bf16[1,8,384]{2,1,0:T(8,128)(2,1)S(1)}, bf16[1,8,384]{2,1,0:T(8,128)(2,1)S(1)}, u32[]{:S(2)}, u32[]{:S(2)}) %collective-permute-start.7) | collective-permute-done | bytes 6176 | tf_op jit(solution)/shard_map/ppermute | solution.py:301
  60.5 0.4 collective-permute-start.8
  60.9 3.6 %collective-permute-done.8 = bf16[2,8,384]{2,1,0:T(8,128)(2,1)S(1)} collective-permute-done((bf16[2,8,384]{2,1,0:T(8,128)(2,1)S(1)}, bf16[2,8,384]{2,1,0:T(8,128)(2,1)S(1)}, u32[]{:S(2)}, u32[]{:S(2)}) %collective-permute-start.8) | collective-permute-done | bytes 12320 | tf_op jit(solution)/shard_map/ppermute | solution.py:301
  64.6 0.3 collective-permute-start.9
  64.9 2.5 %collective-permute-done.9 = bf16[4,8,384]{2,1,0:T(8,128)(2,1)S(1)} collective-permute-done((bf16[4,8,384]{2,1,0:T(8,128)(2,1)S(1)}, bf16[4,8,384]{2,1,0:T(8,128)(2,1)S(1)}, u32[]{:S(2)}, u32[]{:S(2)}) %collective-permute-start.9) | collective-permute-done | bytes 24608 | tf_op jit(solution)/shard_map/ppermute | solution.py:301
  67.3 0.6 collective-permute-start.10
  68.0 3.6 %collective-permute-done.10.second_ref = bf16[8,8,384]{2,1,0:T(8,128)(2,1)S(1)} collective-permute-done((bf16[8,8,384]{2,1,0:T(8,128)(2,1)S(1)}, bf16[8,8,384]{2,1,0:T(8,128)(2,1)S(1)}, u32[]{:S(2)}, u32[]{:S(2)}) %collective-permute-start.10) | collective-permute-done | bytes 49184 | tf_op jit(solution)/shard_map/ppermute | solution.py:301
  71.6 0.0 copy-done.1
  71.6 0.3 output.1
  71.8 13.6 %collective-permute-start.11 = (f32[48,512]{1,0:T(8,128)S(1)}, f32[48,512]{1,0:T(8,128)S(1)}, u32[]{:S(2)}, u32[]{:S(2)}) collective-permute-start(f32[48,512]{1,0:T(8,128)S(1)} %output.1), channel_id=1, source_target_pairs={{0,1},{1,0},{2,3},{3,2},{4,5},{5,4},{6,7},{7,6},{8,9},{9,8},{10,11... | collective-permute-start | bytes 294920 | tf_op jit(solution)/shard_map/ppermute | solution.py:307
  85.4 0.9 collective-permute-done.11
  86.4 0.1 collective-permute-start.12
  86.5 4.0 %collective-permute-done.12 = f32[48,512]{1,0:T(8,128)S(1)} collective-permute-done((f32[48,512]{1,0:T(8,128)S(1)}, f32[48,512]{1,0:T(8,128)S(1)}, u32[]{:S(2)}, u32[]{:S(2)}) %collective-permute-start.12) | collective-permute-done | bytes 98336 | tf_op jit(solution)/shard_map/ppermute | solution.py:307
  90.5 3.1 %collective-permute-start.13 = (f32[48,512]{1,0:T(8,128)S(1)}, f32[48,512]{1,0:T(8,128)S(1)}, u32[]{:S(2)}, u32[]{:S(2)}) collective-permute-start(f32[48,512]{1,0:T(8,128)S(1)} %add.22), channel_id=1, source_target_pairs={{0,6},{1,7},{2,4},{3,5},{4,2},{5,3},{6,0},{7,1},{8,14},{9,15},{10,... | collective-permute-start | bytes 294920 | tf_op jit(solution)/shard_map/ppermute | solution.py:307
  93.6 2.0 %collective-permute-done.13 = f32[48,512]{1,0:T(8,128)S(1)} collective-permute-done((f32[48,512]{1,0:T(8,128)S(1)}, f32[48,512]{1,0:T(8,128)S(1)}, u32[]{:S(2)}, u32[]{:S(2)}) %collective-permute-start.13) | collective-permute-done | bytes 98336 | tf_op jit(solution)/shard_map/ppermute | solution.py:307
  95.6 0.6 add_convert_fusion
  (14 shorter events, 0.1 us)
Async XLA Ops:
  0.0 13.1 %copy-start.2 = (bf16[512]{0:T(512)(128)(2,1)S(1)}, bf16[512]{0:T(512)(128)(2,1)}, u32[]{:S(2)}) copy-start(bf16[512]{0:T(512)(128)(2,1)} %param.11) | copy-start | bytes 3076
  0.1 43.6 %slice-start = ((s8[6291456]{0:T(1024)(128)(4,1)}), s8[4194304]{0:T(1024)(128)(4,1)S(1)}, s32[]{:S(2)}) async-start(s8[6291456]{0:T(1024)(128)(4,1)} %bitcast.10), calls=%async_computation.2 | async-start | bytes 8388608
  0.1 43.6 %slice-start.1 = ((s8[6291456]{0:T(1024)(128)(4,1)}), s8[2097152]{0:T(1024)(128)(4,1)S(1)}, s32[]{:S(2)}) async-start(s8[6291456]{0:T(1024)(128)(4,1)} %bitcast.10), calls=%async_computation.3 | async-start | bytes 4194304
  0.1 43.6 %copy-start = (bf16[24,1,1024,128]{3,2,1,0:T(8,128)(2,1)S(1)}, bf16[24,1,1024,128]{3,2,1,0:T(8,128)(2,1)}, u32[]{:S(2)}) copy-start(bf16[24,1,1024,128]{3,2,1,0:T(8,128)(2,1)} %param.14) | copy-start | bytes 18874372
  3.8 2.2 %collective-permute-start = (bf16[48,512]{1,0:T(8,128)(2,1)S(1)}, bf16[48,512]{1,0:T(8,128)(2,1)S(1)}, u32[]{:S(2)}, u32[]{:S(2)}) collective-permute-start(bf16[48,512]{1,0:T(8,128)(2,1)S(1)} %get-tuple-element.10), channel_id=1, source_target_pairs={{0,1},{1,0},{2,3},{3,2},{4,5},{5,4},{6,7},{7,6},{8,9},{9,8},{10,11... | collective-permute-start | bytes 147464 | tf_op jit(solution)/shard_map/ppermute | solution.py:307
  6.1 3.4 %collective-permute-start.1 = (bf16[48,512]{1,0:T(8,128)(2,1)S(1)}, bf16[48,512]{1,0:T(8,128)(2,1)S(1)}, u32[]{:S(2)}, u32[]{:S(2)}) collective-permute-start(bf16[48,512]{1,0:T(8,128)(2,1)S(1)} %add.18), channel_id=1, source_target_pairs={{0,2},{1,3},{2,0},{3,1},{4,6},{5,7},{6,4},{7,5},{8,10},{9,11},{10,... | collective-permute-start | bytes 147464 | tf_op jit(solution)/shard_map/ppermute | solution.py:307
  9.6 5.0 %collective-permute-start.2 = (bf16[48,512]{1,0:T(8,128)(2,1)S(1)}, bf16[48,512]{1,0:T(8,128)(2,1)S(1)}, u32[]{:S(2)}, u32[]{:S(2)}) collective-permute-start(bf16[48,512]{1,0:T(8,128)(2,1)S(1)} %add.19), channel_id=1, source_target_pairs={{0,6},{1,7},{2,4},{3,5},{4,2},{5,3},{6,0},{7,1},{8,14},{9,15},{10,... | collective-permute-start | bytes 147464 | tf_op jit(solution)/shard_map/ppermute | solution.py:307
  29.8 2.9 %collective-permute-start.3 = (bf16[1,32,128]{2,1,0:T(8,128)(2,1)S(1)}, bf16[1,32,128]{2,1,0:T(8,128)(2,1)S(1)}, u32[]{:S(2)}, u32[]{:S(2)}) collective-permute-start(bf16[1,32,128]{2,1,0:T(8,128)(2,1)S(1)} %bitcast.15), channel_id=1, source_target_pairs={{0,8},{8,0},{16,24},{24,16},{32,40},{40,32},{48,56},{56,48},{64,72... | collective-permute-start | bytes 24584 | tf_op jit(solution)/shard_map/ppermute | solution.py:301
  32.7 3.8 %collective-permute-start.4 = (bf16[2,32,128]{2,1,0:T(8,128)(2,1)S(1)}, bf16[2,32,128]{2,1,0:T(8,128)(2,1)S(1)}, u32[]{:S(2)}, u32[]{:S(2)}) collective-permute-start(bf16[2,32,128]{2,1,0:T(8,128)(2,1)S(1)} %pad_maximum_fusion.4), channel_id=1, source_target_pairs={{0,24},{8,16},{16,8},{24,0},{32,56},{40,48},{48,40},{56,32},{64,88... | collective-permute-start | bytes 49160 | tf_op jit(solution)/shard_map/ppermute | solution.py:301
  36.5 2.8 %collective-permute-start.5 = (bf16[4,32,128]{2,1,0:T(8,128)(2,1)S(1)}, bf16[4,32,128]{2,1,0:T(8,128)(2,1)S(1)}, u32[]{:S(2)}, u32[]{:S(2)}) collective-permute-start(bf16[4,32,128]{2,1,0:T(8,128)(2,1)S(1)} %pad_maximum_fusion.2), channel_id=1, source_target_pairs={{0,32},{8,40},{16,48},{24,56},{32,0},{40,8},{48,16},{56,24},{64,96... | collective-permute-start | bytes 98312 | tf_op jit(solution)/shard_map/ppermute | solution.py:301
  39.3 4.4 %collective-permute-start.6 = (bf16[8,32,128]{2,1,0:T(8,128)(2,1)S(1)}, bf16[8,32,128]{2,1,0:T(8,128)(2,1)S(1)}, u32[]{:S(2)}, u32[]{:S(2)}) collective-permute-start(bf16[8,32,128]{2,1,0:T(8,128)(2,1)S(1)} %pad_maximum_fusion.first_ref), channel_id=1, source_target_pairs={{0,96},{8,104},{16,112},{24,120},{32,64},{40,72},{48,80},{56,88},{... | collective-permute-start | bytes 196616 | tf_op jit(solution)/shard_map/ppermute | solution.py:301
  43.7 27.8 %copy-start.1 = (bf16[1,1024,512]{2,1,0:T(8,128)(2,1)S(1)}, bf16[1,1024,512]{2,1,0:T(8,128)(2,1)}, u32[]{:S(2)}) copy-start(bf16[1,1024,512]{2,1,0:T(8,128)(2,1)} %param.15) | copy-start | bytes 3145732
  57.9 2.6 %collective-permute-start.7 = (bf16[1,8,384]{2,1,0:T(8,128)(2,1)S(1)}, bf16[1,8,384]{2,1,0:T(8,128)(2,1)S(1)}, u32[]{:S(2)}, u32[]{:S(2)}) collective-permute-start(bf16[1,8,384]{2,1,0:T(8,128)(2,1)S(1)} %bitcast.19), channel_id=1, source_target_pairs={{0,8},{8,0},{16,24},{24,16},{32,40},{40,32},{48,56},{56,48},{64,72... | collective-permute-start | bytes 18440 | tf_op jit(solution)/shard_map/ppermute | solution.py:301
  60.5 4.1 %collective-permute-start.8 = (bf16[2,8,384]{2,1,0:T(8,128)(2,1)S(1)}, bf16[2,8,384]{2,1,0:T(8,128)(2,1)S(1)}, u32[]{:S(2)}, u32[]{:S(2)}) collective-permute-start(bf16[2,8,384]{2,1,0:T(8,128)(2,1)S(1)} %pad_maximum_fusion.5), channel_id=1, source_target_pairs={{0,24},{8,16},{16,8},{24,0},{32,56},{40,48},{48,40},{56,32},{64,88... | collective-permute-start | bytes 36872 | tf_op jit(solution)/shard_map/ppermute | solution.py:301
  64.6 2.8 %collective-permute-start.9 = (bf16[4,8,384]{2,1,0:T(8,128)(2,1)S(1)}, bf16[4,8,384]{2,1,0:T(8,128)(2,1)S(1)}, u32[]{:S(2)}, u32[]{:S(2)}) collective-permute-start(bf16[4,8,384]{2,1,0:T(8,128)(2,1)S(1)} %pad_maximum_fusion.3), channel_id=1, source_target_pairs={{0,32},{8,40},{16,48},{24,56},{32,0},{40,8},{48,16},{56,24},{64,96... | collective-permute-start | bytes 73736 | tf_op jit(solution)/shard_map/ppermute | solution.py:301
  67.3 4.2 %collective-permute-start.10 = (bf16[8,8,384]{2,1,0:T(8,128)(2,1)S(1)}, bf16[8,8,384]{2,1,0:T(8,128)(2,1)S(1)}, u32[]{:S(2)}, u32[]{:S(2)}) collective-permute-start(bf16[8,8,384]{2,1,0:T(8,128)(2,1)S(1)} %pad_maximum_fusion.1.first_ref), channel_id=1, source_target_pairs={{0,96},{8,104},{16,112},{24,120},{32,64},{40,72},{48,80},{56,88},{... | collective-permute-start | bytes 147464 | tf_op jit(solution)/shard_map/ppermute | solution.py:301
  71.8 14.5 %collective-permute-start.11 = (f32[48,512]{1,0:T(8,128)S(1)}, f32[48,512]{1,0:T(8,128)S(1)}, u32[]{:S(2)}, u32[]{:S(2)}) collective-permute-start(f32[48,512]{1,0:T(8,128)S(1)} %output.1), channel_id=1, source_target_pairs={{0,1},{1,0},{2,3},{3,2},{4,5},{5,4},{6,7},{7,6},{8,9},{9,8},{10,11... | collective-permute-start | bytes 294920 | tf_op jit(solution)/shard_map/ppermute | solution.py:307
  86.4 4.1 %collective-permute-start.12 = (f32[48,512]{1,0:T(8,128)S(1)}, f32[48,512]{1,0:T(8,128)S(1)}, u32[]{:S(2)}, u32[]{:S(2)}) collective-permute-start(f32[48,512]{1,0:T(8,128)S(1)} %add.21), channel_id=1, source_target_pairs={{0,2},{1,3},{2,0},{3,1},{4,6},{5,7},{6,4},{7,5},{8,10},{9,11},{10,... | collective-permute-start | bytes 294920 | tf_op jit(solution)/shard_map/ppermute | solution.py:307
  90.5 5.1 %collective-permute-start.13 = (f32[48,512]{1,0:T(8,128)S(1)}, f32[48,512]{1,0:T(8,128)S(1)}, u32[]{:S(2)}, u32[]{:S(2)}) collective-permute-start(f32[48,512]{1,0:T(8,128)S(1)} %add.22), channel_id=1, source_target_pairs={{0,6},{1,7},{2,4},{3,5},{4,2},{5,3},{6,0},{7,1},{8,14},{9,15},{10,... | collective-permute-start | bytes 294920 | tf_op jit(solution)/shard_map/ppermute | solution.py:307

commit v2 on v1

--- a/solution.py
+++ b/solution.py
@@ -11,6 +11,8 @@
 TILE = 16
 LANES = 128
 SUB = 8
+BLOCK = 32
+SPAN = 32
 
 rope_base = 500000.0
 epsilon = 1e-05
@@ -43,14 +45,6 @@
 
 def swap(array, axis_name):
     return lax.all_to_all(array, axis_name, 0, 0, tiled=True)
-
-
-SEQ_MASKS = (1, 3, 4, 12)
-
-
-def place_of(me, source):
-    differ = me ^ source
-    return differ ^ ((differ >> 1) & 5)
 
 
 def rope_frequency(head_dim):
@@ -103,17 +97,23 @@
     near = LANES // (2 * SUB)
     sub = lax.broadcasted_iota(jnp.int32, (SUB, LANES), 0)
     lane = lax.broadcasted_iota(jnp.int32, (SUB, LANES), 1)
-    position = jnp.zeros((SUB, LANES), jnp.int32)
+    own = rows // near
+    block = rope_ref.shape[0] // 2
+    line = lax.broadcasted_iota(jnp.int32, (block, LANES), 0)
+    position = jnp.zeros((block, LANES), jnp.int32)
     limits = jnp.zeros((SUB, LANES), jnp.int32)
-    for g in range(rows // near):
-        position = jnp.where(sub == g, lengths_ref[g * near + me // 2] + me % 2, position)
+    for g in range(own):
+        here = (line // SUB == g) | (line == own * SUB + g)
+        position = jnp.where(here, lengths_ref[g * near + me // 2] + me % 2, position)
         for r in range(near):
             here = (sub == g) & (lane // (2 * SUB) == r)
             limits = jnp.where(here, lengths_ref[g * near + r], limits)
     limits_ref[...] = limits - me * cache_dev
     cosine, sine = cos_sin(position.astype(jnp.float32) * frequency_ref[...])
-    rope_ref[:SUB] = cosine
-    rope_ref[SUB:] = jnp.where(lane < LANES // 2, -sine, sine)
+    turned = line < own * SUB + own
+    first_half = lax.broadcasted_iota(jnp.int32, (block, LANES), 1) < LANES // 2
+    rope_ref[:block] = jnp.where(turned, cosine, 1.0)
+    rope_ref[block:] = jnp.where(turned, jnp.where(first_half, -sine, sine), 0.0)
 
     row = lax.broadcasted_iota(jnp.int32, (tokens, 1), 0)
     choice = jnp.full((tokens, 1), -1, jnp.int32)
@@ -129,53 +129,52 @@
 
 def project_kernel(x_ref, gain_ref, w_ref, out_ref):
     tokens = x_ref.shape[0]
-    count, own, width = out_ref.shape
-    width -= LANES
-    row = lax.broadcasted_iota(jnp.int32, (count * SUB, tokens), 0)
-    column = lax.broadcasted_iota(jnp.int32, (count * SUB, tokens), 1)
-    owner, k = row // SUB, row % SUB
+    count = out_ref.shape[0] // BLOCK
+    own = tokens // count
+    row = lax.broadcasted_iota(jnp.int32, (tokens, tokens), 0)
+    column = lax.broadcasted_iota(jnp.int32, (tokens, tokens), 1)
+    owner, k = row % count, row // count
     token = (owner % 2) * (tokens // 2) + owner // 2 + (count // 2) * k
-    spread = jnp.where((column == token) & (k < own), 1.0, 0.0).astype(jnp.bfloat16)
-    x = jnp.dot(spread, x_ref[...], preferred_element_type=jnp.float32)
+    order = jnp.where(column == token, 1.0, 0.0).astype(jnp.bfloat16)
+    x = jnp.dot(order, x_ref[...], preferred_element_type=jnp.float32)
     squares = jnp.sum(x * x, axis=1, keepdims=True)
     scaled = (x * gain_ref[...]).astype(jnp.bfloat16)
     partial = jnp.dot(scaled, w_ref[...], preferred_element_type=jnp.float32)
-    squares = jnp.broadcast_to(squares, (count * SUB, LANES))
-    for j in range(count):
-        out_ref[j, :, :width] = partial[j * SUB : j * SUB + own]
-        out_ref[j, :, width:] = squares[j * SUB : j * SUB + own]
+    lane = lax.broadcasted_iota(jnp.int32, (count, LANES), 1)
+    last = jnp.zeros((count, LANES), jnp.float32)
+    for k in range(own):
+        part = slice(k * count, (k + 1) * count)
+        for b in range(SUB + 2):
+            line = k * SUB + b if b < SUB else (own * (b - SUB) + own * SUB + k)
+            out_ref[pl.ds(line, count, stride=BLOCK)] = partial[part, b * LANES : (b + 1) * LANES]
+        last = jnp.where(lane // SPAN == k, squares[part], last)
+    out_ref[pl.ds(BLOCK - 2, count, stride=BLOCK)] = last
+    out_ref[pl.ds(BLOCK - 1, count, stride=BLOCK)] = jnp.zeros((count, LANES), jnp.float32)
 
 
 def finish_kernel(parts_ref, rope_ref, out_ref):
-    _, own, width = parts_ref.shape
-    head_dim = out_ref.shape[1]
+    count, block, head_dim = parts_ref.shape
+    own = block // SUB - 1
     summed = parts_ref[0]
-    for j in range(1, parts_ref.shape[0]):
+    for j in range(1, count):
         summed = summed + parts_ref[j]
-    scale = lax.rsqrt(summed[:, width - LANES :] / D + epsilon)
-    cosine, sine_part = rope_ref[:own], rope_ref[SUB : SUB + own]
-    group = (width - LANES) // head_dim - 2
-    blocks = []
-    for b in range(group + 2):
-        block = summed[:, b * head_dim : (b + 1) * head_dim] * scale
-        if b <= group:
-            block = block * cosine + pltpu.roll(block, head_dim // 2, 1) * sine_part
-        if b < group:
-            block = block * head_dim ** (-0.5)
-        blocks.append(block)
-    rows = [blocks[b][k : k + 1] for k in range(own) for b in range(group)]
-    rows += [blocks[group], blocks[group + 1]]
-    rows.append(jnp.zeros((out_ref.shape[0] - own * (group + 2), head_dim), jnp.float32))
-    out_ref[...] = jnp.concatenate(rows, axis=0).astype(jnp.bfloat16)
-
-
-def attend_kernel(
-    limits_ref, first_ref, second_ref, k_ref, v_ref, out_ref, rows_ref, scores_ref
-):
+    inverse = lax.rsqrt(summed[block - 2 : block - 1] / D + epsilon)
+    line = lax.broadcasted_iota(jnp.int32, (block, head_dim), 0)
+    scale = jnp.zeros((block, head_dim), jnp.float32)
+    for k in range(own):
+        here = (line // SUB == k) | (line == own * SUB + k) | (line == own * SUB + own + k)
+        here = here & ((line < own * SUB) | (line % SUB < 2 * own))
+        scale = jnp.where(here, inverse[:, k * SPAN : k * SPAN + 1], scale)
+    normed = summed * scale
+    turned = normed * rope_ref[:block] + pltpu.roll(normed, head_dim // 2, 1) * rope_ref[block:]
+    turned = jnp.where(line < own * SUB, turned * head_dim ** (-0.5), turned).astype(jnp.bfloat16)
+    for j in range(out_ref.shape[0]):
+        out_ref[j] = turned
+
+
+def attend_kernel(limits_ref, rows_ref, k_ref, v_ref, out_ref, scores_ref):
     row_count, cache_dev, head_dim = k_ref.shape
     count = rows_ref.shape[0]
-    rows_ref[: count // 2] = first_ref[...]
-    rows_ref[count // 2 :] = second_ref[...]
     per_row = 2 * SUB
     near = LANES // per_row
     groups = row_count // near
@@ -184,19 +183,18 @@
     lane = lax.broadcasted_iota(jnp.int32, (1, LANES), 1)
     position = lax.broadcasted_iota(jnp.int32, (chunk, LANES), 0)
     slot = lax.broadcasted_iota(jnp.int32, (LANES, LANES), 0)
-    rows = [rows_ref[place_of(me, j)].astype(jnp.float32) for j in range(count)]
-    new_keys = jnp.concatenate([part[groups * SUB :] for part in rows], axis=0)
+    rows = rows_ref[...].astype(jnp.float32)
+    new_keys = rows[:, groups * SUB :].reshape(count * SUB, head_dim)
     new_values = pltpu.roll(new_keys, LANES - groups, 0).astype(jnp.bfloat16)
     new_keys = new_keys.astype(jnp.bfloat16)
-    tops, totals = [], []
-    for g in range(groups):
-        turned = jnp.concatenate([part[g * SUB : (g + 1) * SUB] for part in rows], axis=0).T
+
+    def score(g):
+        turned = rows[:, g * SUB : (g + 1) * SUB].reshape(count * SUB, head_dim).T
         blocks = [
             jnp.where(lane // per_row == r, turned, 0.0).astype(jnp.bfloat16) for r in range(near)
         ]
         weights = jnp.concatenate(blocks, axis=0)
         limit = limits_ref[g : g + 1]
-
         fresh = jnp.dot(new_keys, turned.astype(jnp.bfloat16), preferred_element_type=jnp.float32)
         seen = (
             (slot % SUB == g)
@@ -214,7 +212,9 @@
             scores = jnp.where(position < limit - c * chunk, scores, negative)
             scores_ref[g, pl.ds(c * chunk, chunk)] = scores
             top = jnp.maximum(top, jnp.max(scores, axis=0, keepdims=True))
-
+        return top, fresh
+
+    def weigh(g, top, fresh):
         fresh = jnp.exp(fresh - top)
         total = jnp.sum(fresh, axis=0, keepdims=True)
         parts = []
@@ -223,21 +223,28 @@
             total = total + jnp.sum(weight, axis=0, keepdims=True)
             parts.append(weight.astype(jnp.bfloat16).T)
         parts = jnp.concatenate(parts, axis=1)
-        value = []
-        for r in range(0, near, 2):
-            both = jnp.dot(
-                parts[r * per_row : (r + 2) * per_row],
-                jnp.concatenate([v_ref[g * near + r], v_ref[g * near + r + 1]], axis=1),
-                preferred_element_type=jnp.float32,
-            )
-            value += [both[:per_row, :head_dim], both[per_row:, head_dim:]]
-        value = jnp.concatenate(value, axis=0) + jnp.dot(
-            fresh.T.astype(jnp.bfloat16), new_values, preferred_element_type=jnp.float32
-        )
+        value = jnp.concatenate(
+            [
+                jnp.dot(
+                    parts[r * per_row : (r + 1) * per_row],
+                    v_ref[g * near + r],
+                    preferred_element_type=jnp.float32,
+                )
+                for r in range(near)
+            ],
+            axis=0,
+        ) + jnp.dot(fresh.T.astype(jnp.bfloat16), new_values, preferred_element_type=jnp.float32)
         for j in range(count):
             out_ref[j, pl.ds(g * SUB, SUB)] = value[j * SUB : (j + 1) * SUB]
-        tops.append(top)
-        totals.append(total)
+        return total
+
+    tops, totals = [], []
+    ready = score(0)
+    for g in range(groups):
+        later = score(g + 1) if g + 1 < groups else None
+        tops.append(ready[0])
+        totals.append(weigh(g, *ready))
+        ready = later
     spare = jnp.zeros((SUB - 2 * groups, LANES), jnp.float32)
     stats = jnp.concatenate(tops + totals + [spare], axis=0)
     for j in range(count):
@@ -264,19 +271,17 @@
             column = j * SUB + g
             total = total + parts_ref[j, pl.ds(g * SUB, SUB)] * shares[:, column : column + 1]
         merged.append(total)
-    out_ref[...] = jnp.concatenate(merged, axis=1).astype(jnp.bfloat16)
-
-
-def output_kernel(first_ref, second_ref, w_ref, out_ref, attention_ref, held):
+    merged = jnp.concatenate(merged, axis=1).astype(jnp.bfloat16)
+    for j in range(out_ref.shape[0]):
+        out_ref[j] = merged
+
+
+def output_kernel(attention_ref, w_ref, out_ref, held):
     count, heads, width = attention_ref.shape
-    attention_ref[: count // 2] = first_ref[...]
-    attention_ref[count // 2 :] = second_ref[...]
-    head_dim = width // (out_ref.shape[0] // count)
-    me = lax.axis_index("seq")
-    for j in range(count):
-        part = attention_ref[place_of(me, j)].astype(jnp.float32)
-        for g in range(width // head_dim):
-            held[g, pl.ds(j * heads, heads)] = part[:, g * head_dim : (g + 1) * head_dim]
+    groups, _, head_dim = held.shape
+    for g in range(groups):
+        part = attention_ref[:, :, g * head_dim : (g + 1) * head_dim]
+        held[g] = part.astype(jnp.float32).reshape(count * heads, head_dim)
     left = jnp.concatenate(
         [
             jnp.concatenate(
@@ -287,19 +292,11 @@
                 axis=1,
             )
             for step in range(2)
-            for g in range(width // head_dim)
+            for g in range(groups)
         ],
         axis=0,
     )
     out_ref[...] = jnp.dot(left.astype(jnp.bfloat16), w_ref[...], preferred_element_type=jnp.float32)
-
-
-def spread(array, axis_name, masks, size):
-    halves = (array[None],)
-    for mask in masks:
-        held = jnp.concatenate(halves, axis=0) if len(halves) == 2 else halves[0]
-        halves = (held, lax.ppermute(held, axis_name, [(i, i ^ mask) for i in range(size)]))
-    return halves
 
 
 def double(array, axis_name, mask, size):
@@ -314,13 +311,12 @@
     tokens = 2 * row_count
     own = tokens // n_seq
     width = w_qkv.shape[2]
-    block = (own + 1) * SUB
 
     picked, rope, limits, w_near = pl.pallas_call(
         functools.partial(pick_kernel, cache_dev),
         out_shape=[
             jax.ShapeDtypeStruct((tokens, feat), jnp.bfloat16),
-            jax.ShapeDtypeStruct((2 * SUB, LANES), jnp.float32),
+            jax.ShapeDtypeStruct((2 * BLOCK, LANES), jnp.float32),
             jax.ShapeDtypeStruct((SUB, LANES), jnp.int32),
             pltpu.VMEM((feat, width), jnp.bfloat16),
         ],
@@ -345,42 +341,36 @@
     gain = norm_gain.astype(jnp.float32).reshape(1, feat)
 
     partial = call(
-        project_kernel, "project", ((n_seq, own, width + LANES), jnp.float32), [VMEM] * 3
+        project_kernel, "project", ((n_seq * BLOCK, head_dim), jnp.float32), [VMEM] * 3
     )(picked, gain, in_vmem(w_near))
-    partial = swap(partial, "seq")
-    rows = call(finish_kernel, "finish", ((block, head_dim), jnp.bfloat16), [VMEM] * 2)(
+    partial = swap(partial.reshape(n_seq, BLOCK, head_dim), "seq")
+    rows = call(finish_kernel, "finish", ((n_seq, BLOCK, head_dim), jnp.bfloat16), [VMEM] * 2)(
         partial, rope
     )
-    rows = spread(rows, "seq", SEQ_MASKS, n_seq)
+    rows = swap(rows, "seq")
 
     partial = call(
         attend_kernel,
         "attend",
-        ((n_seq, block, head_dim), jnp.float32),
-        [VMEM] * 5,
-        [
-            pltpu.VMEM((n_seq, block, head_dim), jnp.bfloat16),
-            pltpu.VMEM((own, cache_dev, LANES), jnp.float32),
-        ],
+        ((n_seq, BLOCK, head_dim), jnp.float32),
+        [VMEM] * 4,
+        [pltpu.VMEM((own, cache_dev, LANES), jnp.float32)],
         8,
-    )(limits, *rows, in_vmem(k_cache[:, 0]), in_vmem(v_cache[:, 0]))
+    )(limits, rows, in_vmem(k_cache[:, 0]), in_vmem(v_cache[:, 0]))
     partial = swap(partial, "seq")
-    attention = call(merge_kernel, "merge", ((SUB, own * head_dim), jnp.bfloat16), [VMEM])(
+    attention = call(merge_kernel, "merge", ((n_seq, SUB, own * head_dim), jnp.bfloat16), [VMEM])(
         partial
     )
-    attention = spread(attention, "seq", SEQ_MASKS, n_seq)
+    attention = swap(attention, "seq")
 
     terms = call(
         output_kernel,
         "output",
         ((tokens, w_out.shape[2]), jnp.float32),
-        [VMEM] * 3,
-        [
-            pltpu.VMEM((n_seq, SUB, own * head_dim), jnp.bfloat16),
-            pltpu.VMEM((own, n_seq * SUB, head_dim), jnp.float32),
-        ],
-    )(*attention, in_vmem(w_out[0]))
-    for mask in (1, 2, 6):
+        [VMEM] * 2,
+        [pltpu.VMEM((own, n_seq * SUB, head_dim), jnp.float32)],
+    )(attention, in_vmem(w_out[0]))
+    for mask in (2, 6, 1):
         terms = double(terms, "head", mask, n_head)
     return terms.astype(jnp.bfloat16).reshape(2, row_count, -1)
 

time: 97 us -> 82.7 us (0.85)
  waiting for transfers between devices: 35.1 us -> 10.9 us
  blocking collectives: 24.8 us -> 43.5 us
  starting transfers between devices: 26.8 us -> 19.1 us
    ppermute x8 -> x0, waiting for transfers between devices: 24.3 us -> none  [spread(): lax.ppermute(held, axis_name, [(i, i ^ mask) for i in range(size)])]
    all_to_all x2 -> x4, blocking collectives: 24.8 us -> 43.5 us  [swap(): return lax.all_to_all(array, axis_name, 0, 0, tiled=True)]
    ppermute x6, starting transfers between devices: 23.7 us -> 19.1 us  [double(): return array + lax.ppermute(array, axis_name, pairs)]
    ppermute x8 -> x0, starting transfers between devices: 3.15 us -> none  [spread(): lax.ppermute(held, axis_name, [(i, i ^ mask) for i in range(size)])]
  transfers between devices with their start and end apart: 14 -> 6, of which waited for: 14 -> 6; matrix products, arithmetic and copies ran while one was open for 0% -> 0% of each run, Pallas kernels for 0% -> 0%
where the time goes in v2:
time: 82.7 us; the launch traced here: 82.4 us
  blocking collectives  43.5 us (53%)
  starting transfers between devices  19.1 us (23%)
  waiting for transfers between devices  10.9 us (13%)
  Pallas kernels  8.01 us (10%)
    all_to_all x4, blocking collectives, swap(): return lax.all_to_all(array, axis_name, 0, 0, tiled=True)  43.5 us
    ppermute x6, starting transfers between devices, double(): return array + lax.ppermute(array, axis_name, pairs)  19.1 us
    ppermute x6, waiting for transfers between devices, double(): return array + lax.ppermute(array, axis_name, pairs)  10.9 us
    pallas_call x1, Pallas kernels, body(): pl.pallas_call(functools.partial(pick_kernel, cache_dev), out_shape=[jax....  3.73 us
    pallas_call x1, Pallas kernels, body(): call(attend_kernel, 'attend', ((n_seq, BLOCK, head_dim), jnp.float32), [V...  3 us
  transfers between devices with their start and end apart: 6, of which 6 were waited for; matrix products, arithmetic and copies ran while one was open for 0% of the time, Pallas kernels for 0%

profile of v2, /device:TPU:1, one launch (start us, length us, event | category | flops | bytes accessed | tf_op | source)
XLA Modules:
  0.0 82.4 jit_solution(11289937938961256424)
XLA Ops:
  0.0 0.0 copy-start.2
  0.0 0.1 maximum_bitcast_fusion.frequency_ref
  0.1 0.0 slice-start
  0.1 0.0 slice-start.1
  0.1 0.0 copy-start
  0.1 3.7 %pick.1 = (bf16[48,512]{1,0:T(8,128)(2,1)S(1)}, f32[64,128]{1,0:T(8,128)S(1)}, s32[8,128]{1,0:T(8,128)S(1)}, bf16[512,1280]{1,0:T(8,128)(2,1)S(1)}) custom-call(s32[2,24]{1,0:T(2,128)} %ids_ref.1, s32[24]{0:T(128)} %lengths_ref.1, f32[1,128]{1,0:T(1,128)S(1)} %maximum_bitcast_fusion.frequency_ref, bf16[8016,512]{1,0:T(8,128)(2,1)} %table_ref.1, ...), custom_call_target="tpu_custom_call" | custom-call | tf_op jit(solution)/shard_map/pick/pallas_call | solution.py:315
  3.8 1.5 %collective-permute-start = (bf16[48,512]{1,0:T(8,128)(2,1)S(1)}, bf16[48,512]{1,0:T(8,128)(2,1)S(1)}, u32[]{:S(2)}, u32[]{:S(2)}) collective-permute-start(bf16[48,512]{1,0:T(8,128)(2,1)S(1)} %get-tuple-element.10), channel_id=1, source_target_pairs={{0,1},{1,0},{2,3},{3,2},{4,5},{5,4},{6,7},{7,6},{8,9},{9,8},{10,11... | collective-permute-start | bytes 147464 | tf_op jit(solution)/shard_map/ppermute | solution.py:304
  5.3 0.9 %collective-permute-done = bf16[48,512]{1,0:T(8,128)(2,1)S(1)} collective-permute-done((bf16[48,512]{1,0:T(8,128)(2,1)S(1)}, bf16[48,512]{1,0:T(8,128)(2,1)S(1)}, u32[]{:S(2)}, u32[]{:S(2)}) %collective-permute-start) | collective-permute-done | bytes 49184 | tf_op jit(solution)/shard_map/ppermute | solution.py:304
  6.2 1.8 %collective-permute-start.1 = (bf16[48,512]{1,0:T(8,128)(2,1)S(1)}, bf16[48,512]{1,0:T(8,128)(2,1)S(1)}, u32[]{:S(2)}, u32[]{:S(2)}) collective-permute-start(bf16[48,512]{1,0:T(8,128)(2,1)S(1)} %add.18), channel_id=1, source_target_pairs={{0,2},{1,3},{2,0},{3,1},{4,6},{5,7},{6,4},{7,5},{8,10},{9,11},{10,... | collective-permute-start | bytes 147464 | tf_op jit(solution)/shard_map/ppermute | solution.py:304
  8.0 1.5 %collective-permute-done.1 = bf16[48,512]{1,0:T(8,128)(2,1)S(1)} collective-permute-done((bf16[48,512]{1,0:T(8,128)(2,1)S(1)}, bf16[48,512]{1,0:T(8,128)(2,1)S(1)}, u32[]{:S(2)}, u32[]{:S(2)}) %collective-permute-start.1) | collective-permute-done | bytes 49184 | tf_op jit(solution)/shard_map/ppermute | solution.py:304
  9.5 3.6 %collective-permute-start.2 = (bf16[48,512]{1,0:T(8,128)(2,1)S(1)}, bf16[48,512]{1,0:T(8,128)(2,1)S(1)}, u32[]{:S(2)}, u32[]{:S(2)}) collective-permute-start(bf16[48,512]{1,0:T(8,128)(2,1)S(1)} %add.19), channel_id=1, source_target_pairs={{0,6},{1,7},{2,4},{3,5},{4,2},{5,3},{6,0},{7,1},{8,14},{9,15},{10,... | collective-permute-start | bytes 147464 | tf_op jit(solution)/shard_map/ppermute | solution.py:304
  13.1 0.0 copy-done.2
  13.1 1.5 %collective-permute-done.2 = bf16[48,512]{1,0:T(8,128)(2,1)S(1)} collective-permute-done((bf16[48,512]{1,0:T(8,128)(2,1)S(1)}, bf16[48,512]{1,0:T(8,128)(2,1)S(1)}, u32[]{:S(2)}, u32[]{:S(2)}) %collective-permute-start.2) | collective-permute-done | bytes 49184 | tf_op jit(solution)/shard_map/ppermute | solution.py:304
  14.6 0.5 project.1
  15.1 14.2 %all_to_all.20.parts_ref = f32[16,32,128]{2,1,0:T(8,128)S(1)} all-to-all(f32[16,32,128]{2,1,0:T(8,128)S(1)} %bitcast.13), channel_id=1, replica_groups=mesh['seq'=16,'head'=8] {'seq'}, dimensions={0} | all-to-all | bytes 524288 | tf_op jit(solution)/shard_map/all_to_all | solution.py:47
  29.3 0.2 finish.1
  29.5 9.6 %all_to_all.21.rows_ref = bf16[16,32,128]{2,1,0:T(8,128)(2,1)S(1)} all-to-all(bf16[16,32,128]{2,1,0:T(8,128)(2,1)S(1)} %finish.1), channel_id=1, replica_groups=mesh['seq'=16,'head'=8] {'seq'}, dimensions={0} | all-to-all | bytes 262144 | tf_op jit(solution)/shard_map/all_to_all | solution.py:47
  39.2 0.0 slice-done
  39.2 0.0 slice-done.1
  39.2 0.0 copy-done
  39.2 0.0 copy-start.1
  39.2 3.0 %attend.1 = f32[16,32,128]{2,1,0:T(8,128)S(1)} custom-call(s32[8,128]{1,0:T(8,128)S(1)} %get-tuple-element.9.limits_ref, bf16[16,32,128]{2,1,0:T(8,128)(2,1)S(1)} %all_to_all.21.rows_ref, bf16[24,1024,128]{2,1,0:T(8,128)(2,1)S(1)} %bitcast.11, bf16[24,1024,128]{2,1,0:T(8,128)(2,1)S(1)} %bitcast.12), custom_call_target="tpu_custom_call" | custom-call | tf_op jit(solution)/shard_map/attend/pallas_call | solution.py:352
  42.2 10.3 %all_to_all.22.parts_ref = f32[16,32,128]{2,1,0:T(8,128)S(1)} all-to-all(f32[16,32,128]{2,1,0:T(8,128)S(1)} %attend.1), channel_id=1, replica_groups=mesh['seq'=16,'head'=8] {'seq'}, dimensions={0} | all-to-all | bytes 524288 | tf_op jit(solution)/shard_map/all_to_all | solution.py:47
  52.5 0.3 merge.1
  52.8 9.3 %all_to_all.23.attention_ref = bf16[16,8,384]{2,1,0:T(8,128)(2,1)S(1)} all-to-all(bf16[16,8,384]{2,1,0:T(8,128)(2,1)S(1)} %merge.1), channel_id=1, replica_groups=mesh['seq'=16,'head'=8] {'seq'}, dimensions={0} | all-to-all | bytes 196608 | tf_op jit(solution)/shard_map/all_to_all | solution.py:47
  62.1 0.0 copy-done.1
  62.1 0.3 output.1
  62.4 0.0 collective-permute-start.3
  62.4 3.8 %collective-permute-done.3 = f32[48,512]{1,0:T(8,128)S(1)} collective-permute-done((f32[48,512]{1,0:T(8,128)S(1)}, f32[48,512]{1,0:T(8,128)S(1)}, u32[]{:S(2)}, u32[]{:S(2)}) %collective-permute-start.3) | collective-permute-done | bytes 98336 | tf_op jit(solution)/shard_map/ppermute | solution.py:304
  66.2 2.4 %collective-permute-start.4 = (f32[48,512]{1,0:T(8,128)S(1)}, f32[48,512]{1,0:T(8,128)S(1)}, u32[]{:S(2)}, u32[]{:S(2)}) collective-permute-start(f32[48,512]{1,0:T(8,128)S(1)} %add.21), channel_id=1, source_target_pairs={{0,6},{1,7},{2,4},{3,5},{4,2},{5,3},{6,0},{7,1},{8,14},{9,15},{10,... | collective-permute-start | bytes 294920 | tf_op jit(solution)/shard_map/ppermute | solution.py:304
  68.6 2.4 %collective-permute-done.4 = f32[48,512]{1,0:T(8,128)S(1)} collective-permute-done((f32[48,512]{1,0:T(8,128)S(1)}, f32[48,512]{1,0:T(8,128)S(1)}, u32[]{:S(2)}, u32[]{:S(2)}) %collective-permute-start.4) | collective-permute-done | bytes 98336 | tf_op jit(solution)/shard_map/ppermute | solution.py:304
  71.0 9.9 %collective-permute-start.5 = (f32[48,512]{1,0:T(8,128)S(1)}, f32[48,512]{1,0:T(8,128)S(1)}, u32[]{:S(2)}, u32[]{:S(2)}) collective-permute-start(f32[48,512]{1,0:T(8,128)S(1)} %add.22), channel_id=1, source_target_pairs={{0,1},{1,0},{2,3},{3,2},{4,5},{5,4},{6,7},{7,6},{8,9},{9,8},{10,11... | collective-permute-start | bytes 294920 | tf_op jit(solution)/shard_map/ppermute | solution.py:304
  80.8 0.9 %collective-permute-done.5 = f32[48,512]{1,0:T(8,128)S(1)} collective-permute-done((f32[48,512]{1,0:T(8,128)S(1)}, f32[48,512]{1,0:T(8,128)S(1)}, u32[]{:S(2)}, u32[]{:S(2)}) %collective-permute-start.5) | collective-permute-done | bytes 98336 | tf_op jit(solution)/shard_map/ppermute | solution.py:304
  81.8 0.6 add_convert_fusion
  (8 shorter events, 0.1 us)
Async XLA Ops:
  0.0 13.1 %copy-start.2 = (bf16[512]{0:T(512)(128)(2,1)S(1)}, bf16[512]{0:T(512)(128)(2,1)}, u32[]{:S(2)}) copy-start(bf16[512]{0:T(512)(128)(2,1)} %param.11) | copy-start | bytes 3076
  0.1 39.1 %slice-start = ((s8[6291456]{0:T(1024)(128)(4,1)}), s8[4194304]{0:T(1024)(128)(4,1)S(1)}, s32[]{:S(2)}) async-start(s8[6291456]{0:T(1024)(128)(4,1)} %bitcast.9), calls=%async_computation.4 | async-start | bytes 8388608
  0.1 39.1 %slice-start.1 = ((s8[6291456]{0:T(1024)(128)(4,1)}), s8[2097152]{0:T(1024)(128)(4,1)S(1)}, s32[]{:S(2)}) async-start(s8[6291456]{0:T(1024)(128)(4,1)} %bitcast.9), calls=%async_computation.5 | async-start | bytes 4194304
  0.1 39.1 %copy-start = (bf16[24,1,1024,128]{3,2,1,0:T(8,128)(2,1)S(1)}, bf16[24,1,1024,128]{3,2,1,0:T(8,128)(2,1)}, u32[]{:S(2)}) copy-start(bf16[24,1,1024,128]{3,2,1,0:T(8,128)(2,1)} %param.14) | copy-start | bytes 18874372
  3.8 2.4 %collective-permute-start = (bf16[48,512]{1,0:T(8,128)(2,1)S(1)}, bf16[48,512]{1,0:T(8,128)(2,1)S(1)}, u32[]{:S(2)}, u32[]{:S(2)}) collective-permute-start(bf16[48,512]{1,0:T(8,128)(2,1)S(1)} %get-tuple-element.10), channel_id=1, source_target_pairs={{0,1},{1,0},{2,3},{3,2},{4,5},{5,4},{6,7},{7,6},{8,9},{9,8},{10,11... | collective-permute-start | bytes 147464 | tf_op jit(solution)/shard_map/ppermute | solution.py:304
  6.2 3.3 %collective-permute-start.1 = (bf16[48,512]{1,0:T(8,128)(2,1)S(1)}, bf16[48,512]{1,0:T(8,128)(2,1)S(1)}, u32[]{:S(2)}, u32[]{:S(2)}) collective-permute-start(bf16[48,512]{1,0:T(8,128)(2,1)S(1)} %add.18), channel_id=1, source_target_pairs={{0,2},{1,3},{2,0},{3,1},{4,6},{5,7},{6,4},{7,5},{8,10},{9,11},{10,... | collective-permute-start | bytes 147464 | tf_op jit(solution)/shard_map/ppermute | solution.py:304
  9.5 5.1 %collective-permute-start.2 = (bf16[48,512]{1,0:T(8,128)(2,1)S(1)}, bf16[48,512]{1,0:T(8,128)(2,1)S(1)}, u32[]{:S(2)}, u32[]{:S(2)}) collective-permute-start(bf16[48,512]{1,0:T(8,128)(2,1)S(1)} %add.19), channel_id=1, source_target_pairs={{0,6},{1,7},{2,4},{3,5},{4,2},{5,3},{6,0},{7,1},{8,14},{9,15},{10,... | collective-permute-start | bytes 147464 | tf_op jit(solution)/shard_map/ppermute | solution.py:304
  39.2 22.9 %copy-start.1 = (bf16[1,1024,512]{2,1,0:T(8,128)(2,1)S(1)}, bf16[1,1024,512]{2,1,0:T(8,128)(2,1)}, u32[]{:S(2)}) copy-start(bf16[1,1024,512]{2,1,0:T(8,128)(2,1)} %param.15) | copy-start | bytes 3145732
  62.4 3.8 %collective-permute-start.3 = (f32[48,512]{1,0:T(8,128)S(1)}, f32[48,512]{1,0:T(8,128)S(1)}, u32[]{:S(2)}, u32[]{:S(2)}) collective-permute-start(f32[48,512]{1,0:T(8,128)S(1)} %output.1), channel_id=1, source_target_pairs={{0,2},{1,3},{2,0},{3,1},{4,6},{5,7},{6,4},{7,5},{8,10},{9,11},{10,... | collective-permute-start | bytes 294920 | tf_op jit(solution)/shard_map/ppermute | solution.py:304
  66.2 4.8 %collective-permute-start.4 = (f32[48,512]{1,0:T(8,128)S(1)}, f32[48,512]{1,0:T(8,128)S(1)}, u32[]{:S(2)}, u32[]{:S(2)}) collective-permute-start(f32[48,512]{1,0:T(8,128)S(1)} %add.21), channel_id=1, source_target_pairs={{0,6},{1,7},{2,4},{3,5},{4,2},{5,3},{6,0},{7,1},{8,14},{9,15},{10,... | collective-permute-start | bytes 294920 | tf_op jit(solution)/shard_map/ppermute | solution.py:304
  71.0 10.8 %collective-permute-start.5 = (f32[48,512]{1,0:T(8,128)S(1)}, f32[48,512]{1,0:T(8,128)S(1)}, u32[]{:S(2)}, u32[]{:S(2)}) collective-permute-start(f32[48,512]{1,0:T(8,128)S(1)} %add.22), channel_id=1, source_target_pairs={{0,1},{1,0},{2,3},{3,2},{4,5},{5,4},{6,7},{7,6},{8,9},{9,8},{10,11... | collective-permute-start | bytes 294920 | tf_op jit(solution)/shard_map/ppermute | solution.py:304

commit v3 on v2

--- a/solution.py
+++ b/solution.py
@@ -78,17 +78,24 @@
     steps, rows = ids_ref.shape
     tokens = steps * rows
     first = lax.axis_index("head") * vocab_dev
+    held[...] = jnp.zeros_like(held)
     places = []
+    found = 0
     for i in range(tokens):
         local = ids_ref[i // rows, i % rows] - first
         inside = (local >= 0) & (local < vocab_dev)
         local = jnp.clip(local, 0, vocab_dev - 1)
         within = local & (TILE - 1)
-        pltpu.make_async_copy(
-            table_ref.at[pl.ds(pl.multiple_of(local - within, TILE), TILE)],
-            held.at[pl.ds(i * TILE, TILE)],
-            sem,
-        ).start()
+
+        @pl.when(inside)
+        def _(start=local - within, i=i):
+            pltpu.make_async_copy(
+                table_ref.at[pl.ds(pl.multiple_of(start, TILE), TILE)],
+                held.at[pl.ds(i * TILE, TILE)],
+                sem,
+            ).start()
+
+        found = found + inside.astype(jnp.int32)
         places.append(jnp.where(inside, i * TILE + within, -1))
     w_copy = pltpu.make_async_copy(far_w_ref, w_ref, w_sem)
     w_copy.start()
@@ -118,10 +125,15 @@
     row = lax.broadcasted_iota(jnp.int32, (tokens, 1), 0)
     choice = jnp.full((tokens, 1), -1, jnp.int32)
     for i in range(tokens):
-        choice = jnp.where(row == i, places[i], choice)
+        step, r = i // rows, i % rows
+        choice = jnp.where(row == r // near * 2 * near + r % near * 2 + step, places[i], choice)
     column = lax.broadcasted_iota(jnp.int32, (tokens, tokens * TILE), 1)
     select = jnp.where(column == choice, 1.0, 0.0).astype(jnp.bfloat16)
-    pltpu.make_async_copy(table_ref.at[pl.ds(0, tokens * TILE)], held, sem).wait()
+    def wait(i, carry):
+        pltpu.make_async_copy(table_ref.at[pl.ds(0, TILE)], held.at[pl.ds(0, TILE)], sem).wait()
+        return carry
+
+    lax.fori_loop(0, found, wait, 0)
     picked = jnp.dot(select, held[...], preferred_element_type=jnp.float32)
     x_ref[...] = picked.astype(jnp.bfloat16)
     w_copy.wait()
@@ -131,12 +143,7 @@
     tokens = x_ref.shape[0]
     count = out_ref.shape[0] // BLOCK
     own = tokens // count
-    row = lax.broadcasted_iota(jnp.int32, (tokens, tokens), 0)
-    column = lax.broadcasted_iota(jnp.int32, (tokens, tokens), 1)
-    owner, k = row % count, row // count
-    token = (owner % 2) * (tokens // 2) + owner // 2 + (count // 2) * k
-    order = jnp.where(column == token, 1.0, 0.0).astype(jnp.bfloat16)
-    x = jnp.dot(order, x_ref[...], preferred_element_type=jnp.float32)
+    x = x_ref[...].astype(jnp.float32)
     squares = jnp.sum(x * x, axis=1, keepdims=True)
     scaled = (x * gain_ref[...]).astype(jnp.bfloat16)
     partial = jnp.dot(scaled, w_ref[...], preferred_element_type=jnp.float32)

time: 82.7 us -> 82.1 us (level)
  no operation moved by 1% of the time
where the time goes in v3:
time: 82.1 us; the launch traced here: 81.8 us
  blocking collectives  43.5 us (53%)
  starting transfers between devices  19.2 us (23%)
  waiting for transfers between devices  10.9 us (13%)
  Pallas kernels  7.26 us (9%)
    all_to_all x4, blocking collectives, swap(): return lax.all_to_all(array, axis_name, 0, 0, tiled=True)  43.5 us
    ppermute x6, starting transfers between devices, double(): return array + lax.ppermute(array, axis_name, pairs)  19.2 us
    ppermute x6, waiting for transfers between devices, double(): return array + lax.ppermute(array, axis_name, pairs)  10.9 us
    pallas_call x1, Pallas kernels, body(): pl.pallas_call(functools.partial(pick_kernel, cache_dev), out_shape=[jax....  3.09 us
    pallas_call x1, Pallas kernels, body(): call(attend_kernel, 'attend', ((n_seq, BLOCK, head_dim), jnp.float32), [V...  3 us
  transfers between devices with their start and end apart: 6, of which 6 were waited for; matrix products, arithmetic and copies ran while one was open for 0% of the time, Pallas kernels for 0%

profile of v3, /device:TPU:1, one launch (start us, length us, event | category | flops | bytes accessed | tf_op | source)
XLA Modules:
  0.0 81.8 jit_solution(16490843654256650332)
XLA Ops:
  0.0 0.0 copy-start.2
  0.0 0.1 maximum_bitcast_fusion.frequency_ref
  0.1 0.0 slice-start
  0.1 0.0 slice-start.1
  0.1 0.0 copy-start
  0.1 3.1 %pick.1 = (bf16[48,512]{1,0:T(8,128)(2,1)S(1)}, f32[64,128]{1,0:T(8,128)S(1)}, s32[8,128]{1,0:T(8,128)S(1)}, bf16[512,1280]{1,0:T(8,128)(2,1)S(1)}) custom-call(s32[2,24]{1,0:T(2,128)} %ids_ref.1, s32[24]{0:T(128)} %lengths_ref.1, f32[1,128]{1,0:T(1,128)S(1)} %maximum_bitcast_fusion.frequency_ref, bf16[8016,512]{1,0:T(8,128)(2,1)} %table_ref.1, ...), custom_call_target="tpu_custom_call" | custom-call | tf_op jit(solution)/shard_map/pick/pallas_call | solution.py:322
  3.2 1.5 %collective-permute-start = (bf16[48,512]{1,0:T(8,128)(2,1)S(1)}, bf16[48,512]{1,0:T(8,128)(2,1)S(1)}, u32[]{:S(2)}, u32[]{:S(2)}) collective-permute-start(bf16[48,512]{1,0:T(8,128)(2,1)S(1)} %get-tuple-element.10), channel_id=1, source_target_pairs={{0,1},{1,0},{2,3},{3,2},{4,5},{5,4},{6,7},{7,6},{8,9},{9,8},{10,11... | collective-permute-start | bytes 147464 | tf_op jit(solution)/shard_map/ppermute | solution.py:311
  4.7 0.9 %collective-permute-done = bf16[48,512]{1,0:T(8,128)(2,1)S(1)} collective-permute-done((bf16[48,512]{1,0:T(8,128)(2,1)S(1)}, bf16[48,512]{1,0:T(8,128)(2,1)S(1)}, u32[]{:S(2)}, u32[]{:S(2)}) %collective-permute-start) | collective-permute-done | bytes 49184 | tf_op jit(solution)/shard_map/ppermute | solution.py:311
  5.6 1.8 %collective-permute-start.1 = (bf16[48,512]{1,0:T(8,128)(2,1)S(1)}, bf16[48,512]{1,0:T(8,128)(2,1)S(1)}, u32[]{:S(2)}, u32[]{:S(2)}) collective-permute-start(bf16[48,512]{1,0:T(8,128)(2,1)S(1)} %add.18), channel_id=1, source_target_pairs={{0,2},{1,3},{2,0},{3,1},{4,6},{5,7},{6,4},{7,5},{8,10},{9,11},{10,... | collective-permute-start | bytes 147464 | tf_op jit(solution)/shard_map/ppermute | solution.py:311
  7.4 1.5 %collective-permute-done.1 = bf16[48,512]{1,0:T(8,128)(2,1)S(1)} collective-permute-done((bf16[48,512]{1,0:T(8,128)(2,1)S(1)}, bf16[48,512]{1,0:T(8,128)(2,1)S(1)}, u32[]{:S(2)}, u32[]{:S(2)}) %collective-permute-start.1) | collective-permute-done | bytes 49184 | tf_op jit(solution)/shard_map/ppermute | solution.py:311
  8.9 3.7 %collective-permute-start.2 = (bf16[48,512]{1,0:T(8,128)(2,1)S(1)}, bf16[48,512]{1,0:T(8,128)(2,1)S(1)}, u32[]{:S(2)}, u32[]{:S(2)}) collective-permute-start(bf16[48,512]{1,0:T(8,128)(2,1)S(1)} %add.19), channel_id=1, source_target_pairs={{0,6},{1,7},{2,4},{3,5},{4,2},{5,3},{6,0},{7,1},{8,14},{9,15},{10,... | collective-permute-start | bytes 147464 | tf_op jit(solution)/shard_map/ppermute | solution.py:311
  12.6 0.0 copy-done.2
  12.6 1.5 %collective-permute-done.2 = bf16[48,512]{1,0:T(8,128)(2,1)S(1)} collective-permute-done((bf16[48,512]{1,0:T(8,128)(2,1)S(1)}, bf16[48,512]{1,0:T(8,128)(2,1)S(1)}, u32[]{:S(2)}, u32[]{:S(2)}) %collective-permute-start.2) | collective-permute-done | bytes 49184 | tf_op jit(solution)/shard_map/ppermute | solution.py:311
  14.1 0.4 project.1
  14.5 14.2 %all_to_all.20.parts_ref = f32[16,32,128]{2,1,0:T(8,128)S(1)} all-to-all(f32[16,32,128]{2,1,0:T(8,128)S(1)} %bitcast.13), channel_id=1, replica_groups=mesh['seq'=16,'head'=8] {'seq'}, dimensions={0} | all-to-all | bytes 524288 | tf_op jit(solution)/shard_map/all_to_all | solution.py:47
  28.7 0.2 finish.1
  28.9 9.6 %all_to_all.21.rows_ref = bf16[16,32,128]{2,1,0:T(8,128)(2,1)S(1)} all-to-all(bf16[16,32,128]{2,1,0:T(8,128)(2,1)S(1)} %finish.1), channel_id=1, replica_groups=mesh['seq'=16,'head'=8] {'seq'}, dimensions={0} | all-to-all | bytes 262144 | tf_op jit(solution)/shard_map/all_to_all | solution.py:47
  38.5 0.0 slice-done
  38.5 0.0 slice-done.1
  38.5 0.0 copy-done
  38.5 0.0 copy-start.1
  38.6 3.0 %attend.1 = f32[16,32,128]{2,1,0:T(8,128)S(1)} custom-call(s32[8,128]{1,0:T(8,128)S(1)} %get-tuple-element.9.limits_ref, bf16[16,32,128]{2,1,0:T(8,128)(2,1)S(1)} %all_to_all.21.rows_ref, bf16[24,1024,128]{2,1,0:T(8,128)(2,1)S(1)} %bitcast.11, bf16[24,1024,128]{2,1,0:T(8,128)(2,1)S(1)} %bitcast.12), custom_call_target="tpu_custom_call" | custom-call | tf_op jit(solution)/shard_map/attend/pallas_call | solution.py:359
  41.6 10.3 %all_to_all.22.parts_ref = f32[16,32,128]{2,1,0:T(8,128)S(1)} all-to-all(f32[16,32,128]{2,1,0:T(8,128)S(1)} %attend.1), channel_id=1, replica_groups=mesh['seq'=16,'head'=8] {'seq'}, dimensions={0} | all-to-all | bytes 524288 | tf_op jit(solution)/shard_map/all_to_all | solution.py:47
  51.9 0.3 merge.1
  52.2 9.3 %all_to_all.23.attention_ref = bf16[16,8,384]{2,1,0:T(8,128)(2,1)S(1)} all-to-all(bf16[16,8,384]{2,1,0:T(8,128)(2,1)S(1)} %merge.1), channel_id=1, replica_groups=mesh['seq'=16,'head'=8] {'seq'}, dimensions={0} | all-to-all | bytes 196608 | tf_op jit(solution)/shard_map/all_to_all | solution.py:47
  61.5 0.0 copy-done.1
  61.5 0.3 output.1
  61.8 0.0 collective-permute-start.3
  61.8 3.8 %collective-permute-done.3 = f32[48,512]{1,0:T(8,128)S(1)} collective-permute-done((f32[48,512]{1,0:T(8,128)S(1)}, f32[48,512]{1,0:T(8,128)S(1)}, u32[]{:S(2)}, u32[]{:S(2)}) %collective-permute-start.3) | collective-permute-done | bytes 98336 | tf_op jit(solution)/shard_map/ppermute | solution.py:311
  65.6 2.4 %collective-permute-start.4 = (f32[48,512]{1,0:T(8,128)S(1)}, f32[48,512]{1,0:T(8,128)S(1)}, u32[]{:S(2)}, u32[]{:S(2)}) collective-permute-start(f32[48,512]{1,0:T(8,128)S(1)} %add.21), channel_id=1, source_target_pairs={{0,6},{1,7},{2,4},{3,5},{4,2},{5,3},{6,0},{7,1},{8,14},{9,15},{10,... | collective-permute-start | bytes 294920 | tf_op jit(solution)/shard_map/ppermute | solution.py:311
  67.9 2.4 %collective-permute-done.4 = f32[48,512]{1,0:T(8,128)S(1)} collective-permute-done((f32[48,512]{1,0:T(8,128)S(1)}, f32[48,512]{1,0:T(8,128)S(1)}, u32[]{:S(2)}, u32[]{:S(2)}) %collective-permute-start.4) | collective-permute-done | bytes 98336 | tf_op jit(solution)/shard_map/ppermute | solution.py:311
  70.3 9.9 %collective-permute-start.5 = (f32[48,512]{1,0:T(8,128)S(1)}, f32[48,512]{1,0:T(8,128)S(1)}, u32[]{:S(2)}, u32[]{:S(2)}) collective-permute-start(f32[48,512]{1,0:T(8,128)S(1)} %add.22), channel_id=1, source_target_pairs={{0,1},{1,0},{2,3},{3,2},{4,5},{5,4},{6,7},{7,6},{8,9},{9,8},{10,11... | collective-permute-start | bytes 294920 | tf_op jit(solution)/shard_map/ppermute | solution.py:311
  80.2 0.9 %collective-permute-done.5 = f32[48,512]{1,0:T(8,128)S(1)} collective-permute-done((f32[48,512]{1,0:T(8,128)S(1)}, f32[48,512]{1,0:T(8,128)S(1)}, u32[]{:S(2)}, u32[]{:S(2)}) %collective-permute-start.5) | collective-permute-done | bytes 98336 | tf_op jit(solution)/shard_map/ppermute | solution.py:311
  81.1 0.6 add_convert_fusion
  (8 shorter events, 0.1 us)
Async XLA Ops:
  0.0 12.6 %copy-start.2 = (bf16[512]{0:T(512)(128)(2,1)S(1)}, bf16[512]{0:T(512)(128)(2,1)}, u32[]{:S(2)}) copy-start(bf16[512]{0:T(512)(128)(2,1)} %param.11) | copy-start | bytes 3076
  0.1 38.4 %slice-start = ((s8[6291456]{0:T(1024)(128)(4,1)}), s8[4194304]{0:T(1024)(128)(4,1)S(1)}, s32[]{:S(2)}) async-start(s8[6291456]{0:T(1024)(128)(4,1)} %bitcast.9), calls=%async_computation.4 | async-start | bytes 8388608
  0.1 38.4 %slice-start.1 = ((s8[6291456]{0:T(1024)(128)(4,1)}), s8[2097152]{0:T(1024)(128)(4,1)S(1)}, s32[]{:S(2)}) async-start(s8[6291456]{0:T(1024)(128)(4,1)} %bitcast.9), calls=%async_computation.5 | async-start | bytes 4194304
  0.1 38.4 %copy-start = (bf16[24,1,1024,128]{3,2,1,0:T(8,128)(2,1)S(1)}, bf16[24,1,1024,128]{3,2,1,0:T(8,128)(2,1)}, u32[]{:S(2)}) copy-start(bf16[24,1,1024,128]{3,2,1,0:T(8,128)(2,1)} %param.14) | copy-start | bytes 18874372
  3.2 2.4 %collective-permute-start = (bf16[48,512]{1,0:T(8,128)(2,1)S(1)}, bf16[48,512]{1,0:T(8,128)(2,1)S(1)}, u32[]{:S(2)}, u32[]{:S(2)}) collective-permute-start(bf16[48,512]{1,0:T(8,128)(2,1)S(1)} %get-tuple-element.10), channel_id=1, source_target_pairs={{0,1},{1,0},{2,3},{3,2},{4,5},{5,4},{6,7},{7,6},{8,9},{9,8},{10,11... | collective-permute-start | bytes 147464 | tf_op jit(solution)/shard_map/ppermute | solution.py:311
  5.6 3.3 %collective-permute-start.1 = (bf16[48,512]{1,0:T(8,128)(2,1)S(1)}, bf16[48,512]{1,0:T(8,128)(2,1)S(1)}, u32[]{:S(2)}, u32[]{:S(2)}) collective-permute-start(bf16[48,512]{1,0:T(8,128)(2,1)S(1)} %add.18), channel_id=1, source_target_pairs={{0,2},{1,3},{2,0},{3,1},{4,6},{5,7},{6,4},{7,5},{8,10},{9,11},{10,... | collective-permute-start | bytes 147464 | tf_op jit(solution)/shard_map/ppermute | solution.py:311
  8.9 5.2 %collective-permute-start.2 = (bf16[48,512]{1,0:T(8,128)(2,1)S(1)}, bf16[48,512]{1,0:T(8,128)(2,1)S(1)}, u32[]{:S(2)}, u32[]{:S(2)}) collective-permute-start(bf16[48,512]{1,0:T(8,128)(2,1)S(1)} %add.19), channel_id=1, source_target_pairs={{0,6},{1,7},{2,4},{3,5},{4,2},{5,3},{6,0},{7,1},{8,14},{9,15},{10,... | collective-permute-start | bytes 147464 | tf_op jit(solution)/shard_map/ppermute | solution.py:311
  38.5 22.9 %copy-start.1 = (bf16[1,1024,512]{2,1,0:T(8,128)(2,1)S(1)}, bf16[1,1024,512]{2,1,0:T(8,128)(2,1)}, u32[]{:S(2)}) copy-start(bf16[1,1024,512]{2,1,0:T(8,128)(2,1)} %param.15) | copy-start | bytes 3145732
  61.8 3.8 %collective-permute-start.3 = (f32[48,512]{1,0:T(8,128)S(1)}, f32[48,512]{1,0:T(8,128)S(1)}, u32[]{:S(2)}, u32[]{:S(2)}) collective-permute-start(f32[48,512]{1,0:T(8,128)S(1)} %output.1), channel_id=1, source_target_pairs={{0,2},{1,3},{2,0},{3,1},{4,6},{5,7},{6,4},{7,5},{8,10},{9,11},{10,... | collective-permute-start | bytes 294920 | tf_op jit(solution)/shard_map/ppermute | solution.py:311
  65.6 4.8 %collective-permute-start.4 = (f32[48,512]{1,0:T(8,128)S(1)}, f32[48,512]{1,0:T(8,128)S(1)}, u32[]{:S(2)}, u32[]{:S(2)}) collective-permute-start(f32[48,512]{1,0:T(8,128)S(1)} %add.21), channel_id=1, source_target_pairs={{0,6},{1,7},{2,4},{3,5},{4,2},{5,3},{6,0},{7,1},{8,14},{9,15},{10,... | collective-permute-start | bytes 294920 | tf_op jit(solution)/shard_map/ppermute | solution.py:311
  70.3 10.8 %collective-permute-start.5 = (f32[48,512]{1,0:T(8,128)S(1)}, f32[48,512]{1,0:T(8,128)S(1)}, u32[]{:S(2)}, u32[]{:S(2)}) collective-permute-start(f32[48,512]{1,0:T(8,128)S(1)} %add.22), channel_id=1, source_target_pairs={{0,1},{1,0},{2,3},{3,2},{4,5},{5,4},{6,7},{7,6},{8,9},{9,8},{10,11... | collective-permute-start | bytes 294920 | tf_op jit(solution)/shard_map/ppermute | solution.py:311

commit v4 on v3

--- a/solution.py
+++ b/solution.py
@@ -93,12 +93,12 @@
                 table_ref.at[pl.ds(pl.multiple_of(start, TILE), TILE)],
                 held.at[pl.ds(i * TILE, TILE)],
                 sem,
-            ).start()
+            ).start(priority=1)
 
         found = found + inside.astype(jnp.int32)
         places.append(jnp.where(inside, i * TILE + within, -1))
     w_copy = pltpu.make_async_copy(far_w_ref, w_ref, w_sem)
-    w_copy.start()
+    w_copy.start(priority=1)
 
     me = lax.axis_index("seq")
     near = LANES // (2 * SUB)
@@ -185,7 +185,7 @@
     per_row = 2 * SUB
     near = LANES // per_row
     groups = row_count // near
-    chunk = 256
+    chunk = 512
     me = lax.axis_index("seq")
     lane = lax.broadcasted_iota(jnp.int32, (1, LANES), 1)
     position = lax.broadcasted_iota(jnp.int32, (chunk, LANES), 0)

time: 82.1 us -> 82.1 us (level)
  no operation moved by 1% of the time
where the time goes in v4:
time: 82.1 us; the launch traced here: 81.7 us
  blocking collectives  43.5 us (53%)
  starting transfers between devices  19.2 us (23%)
  waiting for transfers between devices  10.9 us (13%)
  Pallas kernels  7.19 us (9%)
    all_to_all x4, blocking collectives, swap(): return lax.all_to_all(array, axis_name, 0, 0, tiled=True)  43.5 us
    ppermute x6, starting transfers between devices, double(): return array + lax.ppermute(array, axis_name, pairs)  19.2 us
    ppermute x6, waiting for transfers between devices, double(): return array + lax.ppermute(array, axis_name, pairs)  10.9 us
    pallas_call x1, Pallas kernels, body(): pl.pallas_call(functools.partial(pick_kernel, cache_dev), out_shape=[jax....  3.06 us
    pallas_call x1, Pallas kernels, body(): call(attend_kernel, 'attend', ((n_seq, BLOCK, head_dim), jnp.float32), [V...  2.97 us
  transfers between devices with their start and end apart: 6, of which 6 were waited for; matrix products, arithmetic and copies ran while one was open for 0% of the time, Pallas kernels for 0%

profile of v4, /device:TPU:1, one launch (start us, length us, event | category | flops | bytes accessed | tf_op | source)
XLA Modules:
  0.0 81.7 jit_solution(18065733601832919804)
XLA Ops:
  0.0 0.0 copy-start.2
  0.0 0.1 maximum_bitcast_fusion.frequency_ref
  0.1 0.0 slice-start
  0.1 0.0 slice-start.1
  0.1 0.0 copy-start
  0.1 3.1 %pick.1 = (bf16[48,512]{1,0:T(8,128)(2,1)S(1)}, f32[64,128]{1,0:T(8,128)S(1)}, s32[8,128]{1,0:T(8,128)S(1)}, bf16[512,1280]{1,0:T(8,128)(2,1)S(1)}) custom-call(s32[2,24]{1,0:T(2,128)} %ids_ref.1, s32[24]{0:T(128)} %lengths_ref.1, f32[1,128]{1,0:T(1,128)S(1)} %maximum_bitcast_fusion.frequency_ref, bf16[8016,512]{1,0:T(8,128)(2,1)} %table_ref.1, ...), custom_call_target="tpu_custom_call" | custom-call | tf_op jit(solution)/shard_map/pick/pallas_call | solution.py:322
  3.2 1.5 %collective-permute-start = (bf16[48,512]{1,0:T(8,128)(2,1)S(1)}, bf16[48,512]{1,0:T(8,128)(2,1)S(1)}, u32[]{:S(2)}, u32[]{:S(2)}) collective-permute-start(bf16[48,512]{1,0:T(8,128)(2,1)S(1)} %get-tuple-element.10), channel_id=1, source_target_pairs={{0,1},{1,0},{2,3},{3,2},{4,5},{5,4},{6,7},{7,6},{8,9},{9,8},{10,11... | collective-permute-start | bytes 147464 | tf_op jit(solution)/shard_map/ppermute | solution.py:311
  4.7 0.9 %collective-permute-done = bf16[48,512]{1,0:T(8,128)(2,1)S(1)} collective-permute-done((bf16[48,512]{1,0:T(8,128)(2,1)S(1)}, bf16[48,512]{1,0:T(8,128)(2,1)S(1)}, u32[]{:S(2)}, u32[]{:S(2)}) %collective-permute-start) | collective-permute-done | bytes 49184 | tf_op jit(solution)/shard_map/ppermute | solution.py:311
  5.6 1.8 %collective-permute-start.1 = (bf16[48,512]{1,0:T(8,128)(2,1)S(1)}, bf16[48,512]{1,0:T(8,128)(2,1)S(1)}, u32[]{:S(2)}, u32[]{:S(2)}) collective-permute-start(bf16[48,512]{1,0:T(8,128)(2,1)S(1)} %add.18), channel_id=1, source_target_pairs={{0,2},{1,3},{2,0},{3,1},{4,6},{5,7},{6,4},{7,5},{8,10},{9,11},{10,... | collective-permute-start | bytes 147464 | tf_op jit(solution)/shard_map/ppermute | solution.py:311
  7.4 1.5 %collective-permute-done.1 = bf16[48,512]{1,0:T(8,128)(2,1)S(1)} collective-permute-done((bf16[48,512]{1,0:T(8,128)(2,1)S(1)}, bf16[48,512]{1,0:T(8,128)(2,1)S(1)}, u32[]{:S(2)}, u32[]{:S(2)}) %collective-permute-start.1) | collective-permute-done | bytes 49184 | tf_op jit(solution)/shard_map/ppermute | solution.py:311
  8.9 3.7 %collective-permute-start.2 = (bf16[48,512]{1,0:T(8,128)(2,1)S(1)}, bf16[48,512]{1,0:T(8,128)(2,1)S(1)}, u32[]{:S(2)}, u32[]{:S(2)}) collective-permute-start(bf16[48,512]{1,0:T(8,128)(2,1)S(1)} %add.19), channel_id=1, source_target_pairs={{0,6},{1,7},{2,4},{3,5},{4,2},{5,3},{6,0},{7,1},{8,14},{9,15},{10,... | collective-permute-start | bytes 147464 | tf_op jit(solution)/shard_map/ppermute | solution.py:311
  12.6 0.0 copy-done.2
  12.6 1.5 %collective-permute-done.2 = bf16[48,512]{1,0:T(8,128)(2,1)S(1)} collective-permute-done((bf16[48,512]{1,0:T(8,128)(2,1)S(1)}, bf16[48,512]{1,0:T(8,128)(2,1)S(1)}, u32[]{:S(2)}, u32[]{:S(2)}) %collective-permute-start.2) | collective-permute-done | bytes 49184 | tf_op jit(solution)/shard_map/ppermute | solution.py:311
  14.1 0.4 project.1
  14.5 14.2 %all_to_all.20.parts_ref = f32[16,32,128]{2,1,0:T(8,128)S(1)} all-to-all(f32[16,32,128]{2,1,0:T(8,128)S(1)} %bitcast.13), channel_id=1, replica_groups=mesh['seq'=16,'head'=8] {'seq'}, dimensions={0} | all-to-all | bytes 524288 | tf_op jit(solution)/shard_map/all_to_all | solution.py:47
  28.7 0.2 finish.1
  28.9 9.6 %all_to_all.21.rows_ref = bf16[16,32,128]{2,1,0:T(8,128)(2,1)S(1)} all-to-all(bf16[16,32,128]{2,1,0:T(8,128)(2,1)S(1)} %finish.1), channel_id=1, replica_groups=mesh['seq'=16,'head'=8] {'seq'}, dimensions={0} | all-to-all | bytes 262144 | tf_op jit(solution)/shard_map/all_to_all | solution.py:47
  38.5 0.0 slice-done
  38.5 0.0 slice-done.1
  38.5 0.0 copy-done
  38.5 0.0 copy-start.1
  38.6 3.0 %attend.1 = f32[16,32,128]{2,1,0:T(8,128)S(1)} custom-call(s32[8,128]{1,0:T(8,128)S(1)} %get-tuple-element.9.limits_ref, bf16[16,32,128]{2,1,0:T(8,128)(2,1)S(1)} %all_to_all.21.rows_ref, bf16[24,1024,128]{2,1,0:T(8,128)(2,1)S(1)} %bitcast.11, bf16[24,1024,128]{2,1,0:T(8,128)(2,1)S(1)} %bitcast.12), custom_call_target="tpu_custom_call" | custom-call | tf_op jit(solution)/shard_map/attend/pallas_call | solution.py:359
  41.5 10.3 %all_to_all.22.parts_ref = f32[16,32,128]{2,1,0:T(8,128)S(1)} all-to-all(f32[16,32,128]{2,1,0:T(8,128)S(1)} %attend.1), channel_id=1, replica_groups=mesh['seq'=16,'head'=8] {'seq'}, dimensions={0} | all-to-all | bytes 524288 | tf_op jit(solution)/shard_map/all_to_all | solution.py:47
  51.9 0.3 merge.1
  52.2 9.3 %all_to_all.23.attention_ref = bf16[16,8,384]{2,1,0:T(8,128)(2,1)S(1)} all-to-all(bf16[16,8,384]{2,1,0:T(8,128)(2,1)S(1)} %merge.1), channel_id=1, replica_groups=mesh['seq'=16,'head'=8] {'seq'}, dimensions={0} | all-to-all | bytes 196608 | tf_op jit(solution)/shard_map/all_to_all | solution.py:47
  61.4 0.0 copy-done.1
  61.5 0.3 output.1
  61.7 0.0 collective-permute-start.3
  61.7 3.8 %collective-permute-done.3 = f32[48,512]{1,0:T(8,128)S(1)} collective-permute-done((f32[48,512]{1,0:T(8,128)S(1)}, f32[48,512]{1,0:T(8,128)S(1)}, u32[]{:S(2)}, u32[]{:S(2)}) %collective-permute-start.3) | collective-permute-done | bytes 98336 | tf_op jit(solution)/shard_map/ppermute | solution.py:311
  65.5 2.4 %collective-permute-start.4 = (f32[48,512]{1,0:T(8,128)S(1)}, f32[48,512]{1,0:T(8,128)S(1)}, u32[]{:S(2)}, u32[]{:S(2)}) collective-permute-start(f32[48,512]{1,0:T(8,128)S(1)} %add.21), channel_id=1, source_target_pairs={{0,6},{1,7},{2,4},{3,5},{4,2},{5,3},{6,0},{7,1},{8,14},{9,15},{10,... | collective-permute-start | bytes 294920 | tf_op jit(solution)/shard_map/ppermute | solution.py:311
  67.9 2.4 %collective-permute-done.4 = f32[48,512]{1,0:T(8,128)S(1)} collective-permute-done((f32[48,512]{1,0:T(8,128)S(1)}, f32[48,512]{1,0:T(8,128)S(1)}, u32[]{:S(2)}, u32[]{:S(2)}) %collective-permute-start.4) | collective-permute-done | bytes 98336 | tf_op jit(solution)/shard_map/ppermute | solution.py:311
  70.3 9.9 %collective-permute-start.5 = (f32[48,512]{1,0:T(8,128)S(1)}, f32[48,512]{1,0:T(8,128)S(1)}, u32[]{:S(2)}, u32[]{:S(2)}) collective-permute-start(f32[48,512]{1,0:T(8,128)S(1)} %add.22), channel_id=1, source_target_pairs={{0,1},{1,0},{2,3},{3,2},{4,5},{5,4},{6,7},{7,6},{8,9},{9,8},{10,11... | collective-permute-start | bytes 294920 | tf_op jit(solution)/shard_map/ppermute | solution.py:311
  80.2 0.9 %collective-permute-done.5 = f32[48,512]{1,0:T(8,128)S(1)} collective-permute-done((f32[48,512]{1,0:T(8,128)S(1)}, f32[48,512]{1,0:T(8,128)S(1)}, u32[]{:S(2)}, u32[]{:S(2)}) %collective-permute-start.5) | collective-permute-done | bytes 98336 | tf_op jit(solution)/shard_map/ppermute | solution.py:311
  81.1 0.6 add_convert_fusion
  (8 shorter events, 0.1 us)
Async XLA Ops:
  0.0 12.6 %copy-start.2 = (bf16[512]{0:T(512)(128)(2,1)S(1)}, bf16[512]{0:T(512)(128)(2,1)}, u32[]{:S(2)}) copy-start(bf16[512]{0:T(512)(128)(2,1)} %param.11) | copy-start | bytes 3076
  0.1 38.4 %slice-start = ((s8[6291456]{0:T(1024)(128)(4,1)}), s8[4194304]{0:T(1024)(128)(4,1)S(1)}, s32[]{:S(2)}) async-start(s8[6291456]{0:T(1024)(128)(4,1)} %bitcast.9), calls=%async_computation.4 | async-start | bytes 8388608
  0.1 38.4 %slice-start.1 = ((s8[6291456]{0:T(1024)(128)(4,1)}), s8[2097152]{0:T(1024)(128)(4,1)S(1)}, s32[]{:S(2)}) async-start(s8[6291456]{0:T(1024)(128)(4,1)} %bitcast.9), calls=%async_computation.5 | async-start | bytes 4194304
  0.1 38.4 %copy-start = (bf16[24,1,1024,128]{3,2,1,0:T(8,128)(2,1)S(1)}, bf16[24,1,1024,128]{3,2,1,0:T(8,128)(2,1)}, u32[]{:S(2)}) copy-start(bf16[24,1,1024,128]{3,2,1,0:T(8,128)(2,1)} %param.14) | copy-start | bytes 18874372
  3.2 2.4 %collective-permute-start = (bf16[48,512]{1,0:T(8,128)(2,1)S(1)}, bf16[48,512]{1,0:T(8,128)(2,1)S(1)}, u32[]{:S(2)}, u32[]{:S(2)}) collective-permute-start(bf16[48,512]{1,0:T(8,128)(2,1)S(1)} %get-tuple-element.10), channel_id=1, source_target_pairs={{0,1},{1,0},{2,3},{3,2},{4,5},{5,4},{6,7},{7,6},{8,9},{9,8},{10,11... | collective-permute-start | bytes 147464 | tf_op jit(solution)/shard_map/ppermute | solution.py:311
  5.6 3.3 %collective-permute-start.1 = (bf16[48,512]{1,0:T(8,128)(2,1)S(1)}, bf16[48,512]{1,0:T(8,128)(2,1)S(1)}, u32[]{:S(2)}, u32[]{:S(2)}) collective-permute-start(bf16[48,512]{1,0:T(8,128)(2,1)S(1)} %add.18), channel_id=1, source_target_pairs={{0,2},{1,3},{2,0},{3,1},{4,6},{5,7},{6,4},{7,5},{8,10},{9,11},{10,... | collective-permute-start | bytes 147464 | tf_op jit(solution)/shard_map/ppermute | solution.py:311
  8.9 5.1 %collective-permute-start.2 = (bf16[48,512]{1,0:T(8,128)(2,1)S(1)}, bf16[48,512]{1,0:T(8,128)(2,1)S(1)}, u32[]{:S(2)}, u32[]{:S(2)}) collective-permute-start(bf16[48,512]{1,0:T(8,128)(2,1)S(1)} %add.19), channel_id=1, source_target_pairs={{0,6},{1,7},{2,4},{3,5},{4,2},{5,3},{6,0},{7,1},{8,14},{9,15},{10,... | collective-permute-start | bytes 147464 | tf_op jit(solution)/shard_map/ppermute | solution.py:311
  38.5 22.9 %copy-start.1 = (bf16[1,1024,512]{2,1,0:T(8,128)(2,1)S(1)}, bf16[1,1024,512]{2,1,0:T(8,128)(2,1)}, u32[]{:S(2)}) copy-start(bf16[1,1024,512]{2,1,0:T(8,128)(2,1)} %param.15) | copy-start | bytes 3145732
  61.7 3.8 %collective-permute-start.3 = (f32[48,512]{1,0:T(8,128)S(1)}, f32[48,512]{1,0:T(8,128)S(1)}, u32[]{:S(2)}, u32[]{:S(2)}) collective-permute-start(f32[48,512]{1,0:T(8,128)S(1)} %output.1), channel_id=1, source_target_pairs={{0,2},{1,3},{2,0},{3,1},{4,6},{5,7},{6,4},{7,5},{8,10},{9,11},{10,... | collective-permute-start | bytes 294920 | tf_op jit(solution)/shard_map/ppermute | solution.py:311
  65.5 4.8 %collective-permute-start.4 = (f32[48,512]{1,0:T(8,128)S(1)}, f32[48,512]{1,0:T(8,128)S(1)}, u32[]{:S(2)}, u32[]{:S(2)}) collective-permute-start(f32[48,512]{1,0:T(8,128)S(1)} %add.21), channel_id=1, source_target_pairs={{0,6},{1,7},{2,4},{3,5},{4,2},{5,3},{6,0},{7,1},{8,14},{9,15},{10,... | collective-permute-start | bytes 294920 | tf_op jit(solution)/shard_map/ppermute | solution.py:311
  70.3 10.8 %collective-permute-start.5 = (f32[48,512]{1,0:T(8,128)S(1)}, f32[48,512]{1,0:T(8,128)S(1)}, u32[]{:S(2)}, u32[]{:S(2)}) collective-permute-start(f32[48,512]{1,0:T(8,128)S(1)} %add.22), channel_id=1, source_target_pairs={{0,1},{1,0},{2,3},{3,2},{4,5},{5,4},{6,7},{7,6},{8,9},{9,8},{10,11... | collective-permute-start | bytes 294920 | tf_op jit(solution)/shard_map/ppermute | solution.py:311

commit v5 on v4

--- a/solution.py
+++ b/solution.py
@@ -13,6 +13,7 @@
 SUB = 8
 BLOCK = 32
 SPAN = 32
+CORE, NEAR, FAR = 1, 2, 6
 
 rope_base = 500000.0
 epsilon = 1e-05
@@ -137,6 +138,27 @@
     picked = jnp.dot(select, held[...], preferred_element_type=jnp.float32)
     x_ref[...] = picked.astype(jnp.bfloat16)
     w_copy.wait()
+
+
+def fetch_kernel(after_ref, far_ref, near_ref, sem):
+    copy = pltpu.make_async_copy(far_ref, near_ref, sem)
+    copy.start()
+    copy.wait()
+
+
+def fetch(after, array):
+    return pl.pallas_call(
+        fetch_kernel,
+        out_shape=pltpu.VMEM(array.shape, array.dtype),
+        in_specs=[ANY] * 2,
+        out_specs=VMEM,
+        scratch_shapes=[pltpu.SemaphoreType.DMA],
+        cost_estimate=pl.CostEstimate(
+            flops=0, bytes_accessed=2 * array.size * array.dtype.itemsize, transcendentals=0
+        ),
+        compiler_params=pltpu.CompilerParams(vmem_limit_bytes=4 << 20),
+        name="fetch",
+    )(after, in_hbm(array))
 
 
 def project_kernel(x_ref, gain_ref, w_ref, out_ref):
@@ -283,32 +305,49 @@
         out_ref[j] = merged
 
 
-def output_kernel(attention_ref, w_ref, out_ref, held):
-    count, heads, width = attention_ref.shape
-    groups, _, head_dim = held.shape
-    for g in range(groups):
-        part = attention_ref[:, :, g * head_dim : (g + 1) * head_dim]
-        held[g] = part.astype(jnp.float32).reshape(count * heads, head_dim)
-    left = jnp.concatenate(
-        [
-            jnp.concatenate(
-                [
-                    held[g, pl.ds(step * heads + i, count // 2, stride=2 * heads)]
-                    for i in range(heads)
-                ],
-                axis=1,
-            )
-            for step in range(2)
-            for g in range(groups)
-        ],
-        axis=0,
-    )
-    out_ref[...] = jnp.dot(left.astype(jnp.bfloat16), w_ref[...], preferred_element_type=jnp.float32)
-
-
-def double(array, axis_name, mask, size):
-    pairs = [(i, i ^ mask) for i in range(size)]
-    return array + lax.ppermute(array, axis_name, pairs)
+def output_kernel(attention_ref, w_ref, other_w_ref, out_ref, held):
+    groups, lines, head_dim = held.shape
+    heads = attention_ref.shape[1]
+    count = lines // heads
+    mine = lax.axis_index("head") // 4
+
+    def terms(place, weights):
+        for j in range(count):
+            part = attention_ref[2 * j + place].astype(jnp.float32)
+            for g in range(groups):
+                held[g, pl.ds(j * heads, heads)] = part[:, g * head_dim : (g + 1) * head_dim]
+        left = jnp.concatenate(
+            [
+                jnp.concatenate(
+                    [
+                        held[g, pl.ds(step * heads + i, count // 2, stride=2 * heads)]
+                        for i in range(heads)
+                    ],
+                    axis=1,
+                )
+                for step in range(2)
+                for g in range(groups)
+            ],
+            axis=0,
+        )
+        return jnp.dot(left.astype(jnp.bfloat16), weights, preferred_element_type=jnp.float32)
+
+    out_ref[...] = terms(mine, w_ref[...]) + terms(1 - mine, other_w_ref[...])
+
+
+def partner(array, mask, size):
+    return lax.ppermute(array, "head", [(i, i ^ mask) for i in range(size)])
+
+
+def swap_with_pairs(array, n_seq, n_head):
+    groups = [
+        [s * n_head + i for s in range(n_seq) for i in sorted((first, first ^ FAR))]
+        for first in range(n_head)
+        if first < first ^ FAR
+    ]
+    return lax.all_to_all(
+        array, ("seq", "head"), 0, 0, axis_index_groups=groups, tiled=True
+    )
 
 
 def body(token_ids, lengths, embedding, norm_gain, w_qkv, k_cache, v_cache, w_out):
@@ -343,8 +382,11 @@
         in_hbm(embedding),
         in_hbm(w_qkv.reshape(feat, width)),
     )
-    for mask in (1, 2, 6):
-        picked = double(picked, "head", mask, n_head)
+    picked = picked + partner(picked, CORE, n_head)
+    picked = picked + partner(picked, FAR, n_head)
+    w_mine = fetch(picked, w_out[0])
+    w_other = partner(w_mine, FAR, n_head)
+    picked = picked + partner(picked, NEAR, n_head)
     gain = norm_gain.astype(jnp.float32).reshape(1, feat)
 
     partial = call(
@@ -365,20 +407,20 @@
         8,
     )(limits, rows, in_vmem(k_cache[:, 0]), in_vmem(v_cache[:, 0]))
     partial = swap(partial, "seq")
-    attention = call(merge_kernel, "merge", ((n_seq, SUB, own * head_dim), jnp.bfloat16), [VMEM])(
+    attention = call(merge_kernel, "merge", ((2 * n_seq, SUB, own * head_dim), jnp.bfloat16), [VMEM])(
         partial
     )
-    attention = swap(attention, "seq")
+    attention = swap_with_pairs(attention, n_seq, n_head)
 
     terms = call(
         output_kernel,
         "output",
         ((tokens, w_out.shape[2]), jnp.float32),
-        [VMEM] * 2,
+        [VMEM] * 3,
         [pltpu.VMEM((own, n_seq * SUB, head_dim), jnp.float32)],
-    )(attention, in_vmem(w_out[0]))
-    for mask in (2, 6, 1):
-        terms = double(terms, "head", mask, n_head)
+    )(attention, in_vmem(w_mine), in_vmem(w_other))
+    terms = terms + partner(terms, NEAR, n_head)
+    terms = terms + partner(terms, CORE, n_head)
     return terms.astype(jnp.bfloat16).reshape(2, row_count, -1)
 
 

time: 82.1 us -> 83.6 us (1.018)
  blocking collectives: 43.5 us -> 46.3 us
  starting transfers between devices: 19.2 us -> 17.1 us
  Pallas kernels: 7.19 us -> 8.77 us
    all_to_all x0 -> x1, blocking collectives: none -> 12.1 us  [swap_with_pairs(): lax.all_to_all(array, ('seq', 'head'), 0, 0, axis_index_groups=groups, ti...]
    all_to_all x4 -> x3, blocking collectives: 43.5 us -> 34.2 us  [swap(): return lax.all_to_all(array, axis_name, 0, 0, tiled=True)]
    ppermute x6, starting transfers between devices: 19.2 us -> 17.1 us  [partner(): return lax.ppermute(array, 'head', [(i, i ^ mask) for i in range(size)])]
    pallas_call x1 -> x2, Pallas kernels: 0.29 us -> 1.54 us  [the longest x1 1.24 us: fetch(): pl.pallas_call(fetch_kernel, out_shape=pltpu.VMEM(array.shape, array.dtyp...]
  transfers between devices with their start and end apart: 6 -> 6, of which waited for: 6 -> 5; matrix products, arithmetic and copies ran while one was open for 0% -> 0% of each run, Pallas kernels for 0% -> 5%
where the time goes in v5:
time: 83.6 us; the launch traced here: 83.3 us
  blocking collectives  46.3 us (55%)
  starting transfers between devices  17.1 us (20%)
  waiting for transfers between devices  10.3 us (12%)
  Pallas kernels  8.77 us (10%)
    all_to_all x3, blocking collectives, swap(): return lax.all_to_all(array, axis_name, 0, 0, tiled=True)  34.2 us
    ppermute x6, starting transfers between devices, partner(): return lax.ppermute(array, 'head', [(i, i ^ mask) for i in range(size)])  17.1 us
    all_to_all x1, blocking collectives, swap_with_pairs(): lax.all_to_all(array, ('seq', 'head'), 0, 0, axis_index_groups=groups, ti...  12.1 us
    ppermute x6, waiting for transfers between devices, partner(): return lax.ppermute(array, 'head', [(i, i ^ mask) for i in range(size)])  10.3 us
    pallas_call x1, Pallas kernels, body(): pl.pallas_call(functools.partial(pick_kernel, cache_dev), out_shape=[jax....  3.1 us
    pallas_call x1, Pallas kernels, body(): call(attend_kernel, 'attend', ((n_seq, BLOCK, head_dim), jnp.float32), [V...  2.97 us
  transfers between devices with their start and end apart: 6, of which 5 were waited for; matrix products, arithmetic and copies ran while one was open for 0% of the time, Pallas kernels for 5%

profile of v5, /device:TPU:1, one launch (start us, length us, event | category | flops | bytes accessed | tf_op | source)
XLA Modules:
  0.0 83.3 jit_solution(12786914795187283182)
XLA Ops:
  0.0 0.0 copy-start.1
  0.0 0.1 maximum_bitcast_fusion.frequency_ref
  0.1 0.0 slice-start
  0.1 0.0 slice-start.1
  0.1 0.0 copy-start
  0.1 3.1 %pick.1 = (bf16[48,512]{1,0:T(8,128)(2,1)S(1)}, f32[64,128]{1,0:T(8,128)S(1)}, s32[8,128]{1,0:T(8,128)S(1)}, bf16[512,1280]{1,0:T(8,128)(2,1)S(1)}) custom-call(s32[2,24]{1,0:T(2,128)} %ids_ref.1, s32[24]{0:T(128)} %lengths_ref.1, f32[1,128]{1,0:T(1,128)S(1)} %maximum_bitcast_fusion.frequency_ref, bf16[8016,512]{1,0:T(8,128)(2,1)} %table_ref.1, ...), custom_call_target="tpu_custom_call" | custom-call | tf_op jit(solution)/shard_map/pick/pallas_call | solution.py:361
  3.2 1.5 %collective-permute-start = (bf16[48,512]{1,0:T(8,128)(2,1)S(1)}, bf16[48,512]{1,0:T(8,128)(2,1)S(1)}, u32[]{:S(2)}, u32[]{:S(2)}) collective-permute-start(bf16[48,512]{1,0:T(8,128)(2,1)S(1)} %get-tuple-element.10), channel_id=1, source_target_pairs={{0,1},{1,0},{2,3},{3,2},{4,5},{5,4},{6,7},{7,6},{8,9},{9,8},{10,11... | collective-permute-start | bytes 147464 | tf_op jit(solution)/shard_map/ppermute | solution.py:339
  4.7 0.9 %collective-permute-done = bf16[48,512]{1,0:T(8,128)(2,1)S(1)} collective-permute-done((bf16[48,512]{1,0:T(8,128)(2,1)S(1)}, bf16[48,512]{1,0:T(8,128)(2,1)S(1)}, u32[]{:S(2)}, u32[]{:S(2)}) %collective-permute-start) | collective-permute-done | bytes 49184 | tf_op jit(solution)/shard_map/ppermute | solution.py:339
  5.6 3.9 %collective-permute-start.1 = (bf16[48,512]{1,0:T(8,128)(2,1)S(1)}, bf16[48,512]{1,0:T(8,128)(2,1)S(1)}, u32[]{:S(2)}, u32[]{:S(2)}) collective-permute-start(bf16[48,512]{1,0:T(8,128)(2,1)S(1)} %add.15), channel_id=1, source_target_pairs={{0,6},{1,7},{2,4},{3,5},{4,2},{5,3},{6,0},{7,1},{8,14},{9,15},{10,... | collective-permute-start | bytes 147464 | tf_op jit(solution)/shard_map/ppermute | solution.py:339
  9.5 1.5 %collective-permute-done.1 = bf16[48,512]{1,0:T(8,128)(2,1)S(1)} collective-permute-done((bf16[48,512]{1,0:T(8,128)(2,1)S(1)}, bf16[48,512]{1,0:T(8,128)(2,1)S(1)}, u32[]{:S(2)}, u32[]{:S(2)}) %collective-permute-start.1) | collective-permute-done | bytes 49184 | tf_op jit(solution)/shard_map/ppermute | solution.py:339
  11.0 1.2 %fetch.1.w_ref = bf16[1024,512]{1,0:T(8,128)(2,1)S(1)} custom-call(bf16[48,512]{1,0:T(8,128)(2,1)S(1)} %add.16.after_ref, bf16[1024,512]{1,0:T(8,128)(2,1)} %bitcast.16), custom_call_target="tpu_custom_call" | custom-call | bytes 2097152 | tf_op jit(solution)/shard_map/fetch/pallas_call | solution.py:150
  12.2 2.8 %collective-permute-start.3 = (bf16[1024,512]{1,0:T(8,128)(2,1)S(1)}, bf16[1024,512]{1,0:T(8,128)(2,1)S(1)}, u32[]{:S(2)}, u32[]{:S(2)}) collective-permute-start(bf16[1024,512]{1,0:T(8,128)(2,1)S(1)} %fetch.1.w_ref), channel_id=1, source_target_pairs={{0,6},{1,7},{2,4},{3,5},{4,2},{5,3},{6,0},{7,1},{8,14},{9,15},{10,... | collective-permute-start | bytes 3145736 | tf_op jit(solution)/shard_map/ppermute | solution.py:339
  15.0 0.0 collective-permute-start.2
  15.0 0.0 copy-done.1
  15.0 3.2 %collective-permute-done.2 = bf16[48,512]{1,0:T(8,128)(2,1)S(1)} collective-permute-done((bf16[48,512]{1,0:T(8,128)(2,1)S(1)}, bf16[48,512]{1,0:T(8,128)(2,1)S(1)}, u32[]{:S(2)}, u32[]{:S(2)}) %collective-permute-start.2) | collective-permute-done | bytes 49184 | tf_op jit(solution)/shard_map/ppermute | solution.py:339
  18.2 0.4 project.1
  18.6 14.1 %all_to_all.20.parts_ref = f32[16,32,128]{2,1,0:T(8,128)S(1)} all-to-all(f32[16,32,128]{2,1,0:T(8,128)S(1)} %bitcast.13), channel_id=1, replica_groups=mesh['seq'=16,'head'=8] {'seq'}, dimensions={0} | all-to-all | bytes 524288 | tf_op jit(solution)/shard_map/all_to_all | solution.py:48
  32.7 0.2 finish.1
  32.9 9.8 %all_to_all.21.rows_ref = bf16[16,32,128]{2,1,0:T(8,128)(2,1)S(1)} all-to-all(bf16[16,32,128]{2,1,0:T(8,128)(2,1)S(1)} %finish.1), channel_id=1, replica_groups=mesh['seq'=16,'head'=8] {'seq'}, dimensions={0} | all-to-all | bytes 262144 | tf_op jit(solution)/shard_map/all_to_all | solution.py:48
  42.7 0.0 slice-done
  42.7 0.0 slice-done.1
  42.7 0.0 copy-done
  42.7 3.0 %attend.1 = f32[16,32,128]{2,1,0:T(8,128)S(1)} custom-call(s32[8,128]{1,0:T(8,128)S(1)} %get-tuple-element.9.limits_ref, bf16[16,32,128]{2,1,0:T(8,128)(2,1)S(1)} %all_to_all.21.rows_ref, bf16[24,1024,128]{2,1,0:T(8,128)(2,1)S(1)} %bitcast.11, bf16[24,1024,128]{2,1,0:T(8,128)(2,1)S(1)} %bitcast.12), custom_call_target="tpu_custom_call" | custom-call | tf_op jit(solution)/shard_map/attend/pallas_call | solution.py:401
  45.7 10.3 %all_to_all.22.parts_ref = f32[16,32,128]{2,1,0:T(8,128)S(1)} all-to-all(f32[16,32,128]{2,1,0:T(8,128)S(1)} %attend.1), channel_id=1, replica_groups=mesh['seq'=16,'head'=8] {'seq'}, dimensions={0} | all-to-all | bytes 524288 | tf_op jit(solution)/shard_map/all_to_all | solution.py:48
  56.0 0.3 merge.1
  56.3 12.1 %all_to_all.23.attention_ref = bf16[32,8,384]{2,1,0:T(8,128)(2,1)S(1)} all-to-all(bf16[32,8,384]{2,1,0:T(8,128)(2,1)S(1)} %merge.1), channel_id=1, replica_groups={{0,6,8,14,16,22,24,30,32,38,40,46,48,54,56,62,64,70,72,78,80,86,88,94,9..., dimensions={0} | all-to-all | bytes 393216 | tf_op jit(solution)/shard_map/all_to_all | solution.py:348
  68.4 0.0 collective-permute-done.3.other_w_ref
  68.4 0.6 output.1
  69.0 0.0 collective-permute-start.4
  69.0 3.8 %collective-permute-done.4 = f32[48,512]{1,0:T(8,128)S(1)} collective-permute-done((f32[48,512]{1,0:T(8,128)S(1)}, f32[48,512]{1,0:T(8,128)S(1)}, u32[]{:S(2)}, u32[]{:S(2)}) %collective-permute-start.4) | collective-permute-done | bytes 98336 | tf_op jit(solution)/shard_map/ppermute | solution.py:339
  72.8 8.9 %collective-permute-start.5 = (f32[48,512]{1,0:T(8,128)S(1)}, f32[48,512]{1,0:T(8,128)S(1)}, u32[]{:S(2)}, u32[]{:S(2)}) collective-permute-start(f32[48,512]{1,0:T(8,128)S(1)} %add.18), channel_id=1, source_target_pairs={{0,1},{1,0},{2,3},{3,2},{4,5},{5,4},{6,7},{7,6},{8,9},{9,8},{10,11... | collective-permute-start | bytes 294920 | tf_op jit(solution)/shard_map/ppermute | solution.py:339
  81.7 0.9 %collective-permute-done.5 = f32[48,512]{1,0:T(8,128)S(1)} collective-permute-done((f32[48,512]{1,0:T(8,128)S(1)}, f32[48,512]{1,0:T(8,128)S(1)}, u32[]{:S(2)}, u32[]{:S(2)}) %collective-permute-start.5) | collective-permute-done | bytes 98336 | tf_op jit(solution)/shard_map/ppermute | solution.py:339
  82.7 0.6 add_convert_fusion
  (7 shorter events, 0.1 us)
Async XLA Ops:
  0.0 15.0 %copy-start.1 = (bf16[512]{0:T(512)(128)(2,1)S(1)}, bf16[512]{0:T(512)(128)(2,1)}, u32[]{:S(2)}) copy-start(bf16[512]{0:T(512)(128)(2,1)} %param.11) | copy-start | bytes 3076
  0.1 42.6 %slice-start = ((s8[6291456]{0:T(1024)(128)(4,1)}), s8[4194304]{0:T(1024)(128)(4,1)S(1)}, s32[]{:S(2)}) async-start(s8[6291456]{0:T(1024)(128)(4,1)} %bitcast.9), calls=%async_computation.4 | async-start | bytes 8388608
  0.1 42.6 %slice-start.1 = ((s8[6291456]{0:T(1024)(128)(4,1)}), s8[2097152]{0:T(1024)(128)(4,1)S(1)}, s32[]{:S(2)}) async-start(s8[6291456]{0:T(1024)(128)(4,1)} %bitcast.9), calls=%async_computation.5 | async-start | bytes 4194304
  0.1 42.6 %copy-start = (bf16[24,1,1024,128]{3,2,1,0:T(8,128)(2,1)S(1)}, bf16[24,1,1024,128]{3,2,1,0:T(8,128)(2,1)}, u32[]{:S(2)}) copy-start(bf16[24,1,1024,128]{3,2,1,0:T(8,128)(2,1)} %param.14) | copy-start | bytes 18874372
  3.2 2.4 %collective-permute-start = (bf16[48,512]{1,0:T(8,128)(2,1)S(1)}, bf16[48,512]{1,0:T(8,128)(2,1)S(1)}, u32[]{:S(2)}, u32[]{:S(2)}) collective-permute-start(bf16[48,512]{1,0:T(8,128)(2,1)S(1)} %get-tuple-element.10), channel_id=1, source_target_pairs={{0,1},{1,0},{2,3},{3,2},{4,5},{5,4},{6,7},{7,6},{8,9},{9,8},{10,11... | collective-permute-start | bytes 147464 | tf_op jit(solution)/shard_map/ppermute | solution.py:339
  5.6 5.4 %collective-permute-start.1 = (bf16[48,512]{1,0:T(8,128)(2,1)S(1)}, bf16[48,512]{1,0:T(8,128)(2,1)S(1)}, u32[]{:S(2)}, u32[]{:S(2)}) collective-permute-start(bf16[48,512]{1,0:T(8,128)(2,1)S(1)} %add.15), channel_id=1, source_target_pairs={{0,6},{1,7},{2,4},{3,5},{4,2},{5,3},{6,0},{7,1},{8,14},{9,15},{10,... | collective-permute-start | bytes 147464 | tf_op jit(solution)/shard_map/ppermute | solution.py:339
  12.2 56.2 %collective-permute-start.3 = (bf16[1024,512]{1,0:T(8,128)(2,1)S(1)}, bf16[1024,512]{1,0:T(8,128)(2,1)S(1)}, u32[]{:S(2)}, u32[]{:S(2)}) collective-permute-start(bf16[1024,512]{1,0:T(8,128)(2,1)S(1)} %fetch.1.w_ref), channel_id=1, source_target_pairs={{0,6},{1,7},{2,4},{3,5},{4,2},{5,3},{6,0},{7,1},{8,14},{9,15},{10,... | collective-permute-start | bytes 3145736 | tf_op jit(solution)/shard_map/ppermute | solution.py:339
  15.0 3.2 %collective-permute-start.2 = (bf16[48,512]{1,0:T(8,128)(2,1)S(1)}, bf16[48,512]{1,0:T(8,128)(2,1)S(1)}, u32[]{:S(2)}, u32[]{:S(2)}) collective-permute-start(bf16[48,512]{1,0:T(8,128)(2,1)S(1)} %add.16.after_ref), channel_id=1, source_target_pairs={{0,2},{1,3},{2,0},{3,1},{4,6},{5,7},{6,4},{7,5},{8,10},{9,11},{10,... | collective-permute-start | bytes 147464 | tf_op jit(solution)/shard_map/ppermute | solution.py:339
  69.0 3.8 %collective-permute-start.4 = (f32[48,512]{1,0:T(8,128)S(1)}, f32[48,512]{1,0:T(8,128)S(1)}, u32[]{:S(2)}, u32[]{:S(2)}) collective-permute-start(f32[48,512]{1,0:T(8,128)S(1)} %output.1), channel_id=1, source_target_pairs={{0,2},{1,3},{2,0},{3,1},{4,6},{5,7},{6,4},{7,5},{8,10},{9,11},{10,... | collective-permute-start | bytes 294920 | tf_op jit(solution)/shard_map/ppermute | solution.py:339
  72.8 9.9 %collective-permute-start.5 = (f32[48,512]{1,0:T(8,128)S(1)}, f32[48,512]{1,0:T(8,128)S(1)}, u32[]{:S(2)}, u32[]{:S(2)}) collective-permute-start(f32[48,512]{1,0:T(8,128)S(1)} %add.18), channel_id=1, source_target_pairs={{0,1},{1,0},{2,3},{3,2},{4,5},{5,4},{6,7},{7,6},{8,9},{9,8},{10,11... | collective-permute-start | bytes 294920 | tf_op jit(solution)/shard_map/ppermute | solution.py:339

commit v6 on v4

--- a/solution.py
+++ b/solution.py
@@ -185,7 +185,7 @@
     per_row = 2 * SUB
     near = LANES // per_row
     groups = row_count // near
-    chunk = 512
+    chunk = 256
     me = lax.axis_index("seq")
     lane = lax.broadcasted_iota(jnp.int32, (1, LANES), 1)
     position = lax.broadcasted_iota(jnp.int32, (chunk, LANES), 0)
@@ -195,63 +195,74 @@
     new_values = pltpu.roll(new_keys, LANES - groups, 0).astype(jnp.bfloat16)
     new_keys = new_keys.astype(jnp.bfloat16)
 
-    def score(g):
+    chunks = cache_dev // chunk
+    queries, tops, fresh, totals, parts, values = {}, {}, {}, {}, {}, {}
+
+    def begin(g):
         turned = rows[:, g * SUB : (g + 1) * SUB].reshape(count * SUB, head_dim).T
         blocks = [
             jnp.where(lane // per_row == r, turned, 0.0).astype(jnp.bfloat16) for r in range(near)
         ]
-        weights = jnp.concatenate(blocks, axis=0)
-        limit = limits_ref[g : g + 1]
-        fresh = jnp.dot(new_keys, turned.astype(jnp.bfloat16), preferred_element_type=jnp.float32)
+        queries[g] = jnp.concatenate(blocks, axis=0)
+        new = jnp.dot(new_keys, turned.astype(jnp.bfloat16), preferred_element_type=jnp.float32)
         seen = (
             (slot % SUB == g)
             & (slot // per_row == lane // per_row)
             & (slot // SUB <= lane // SUB)
             & (me == 0)
         )
-        fresh = jnp.where(seen, fresh, negative)
-        top = jnp.max(fresh, axis=0, keepdims=True)
-        for c in range(cache_dev // chunk):
-            keys = jnp.concatenate(
-                [k_ref[g * near + r, pl.ds(c * chunk, chunk)] for r in range(near)], axis=1
+        fresh[g] = jnp.where(seen, new, negative)
+        tops[g] = jnp.max(fresh[g], axis=0, keepdims=True)
+
+    def score(g, c):
+        keys = jnp.concatenate(
+            [k_ref[g * near + r, pl.ds(c * chunk, chunk)] for r in range(near)], axis=1
+        )
+        scores = jnp.dot(keys, queries[g], preferred_element_type=jnp.float32)
+        scores = jnp.where(position < limits_ref[g : g + 1] - c * chunk, scores, negative)
+        scores_ref[g, pl.ds(c * chunk, chunk)] = scores
+        tops[g] = jnp.maximum(tops[g], jnp.max(scores, axis=0, keepdims=True))
+
+    def weigh(g, c):
+        if c == 0:
+            fresh[g] = jnp.exp(fresh[g] - tops[g])
+            totals[g] = jnp.sum(fresh[g], axis=0, keepdims=True)
+            parts[g] = []
+        weight = jnp.exp(scores_ref[g, pl.ds(c * chunk, chunk)] - tops[g])
+        totals[g] = totals[g] + jnp.sum(weight, axis=0, keepdims=True)
+        parts[g].append(weight.astype(jnp.bfloat16).T)
+
+    def add_up(g, c):
+        if c == 0:
+            parts[g] = jnp.concatenate(parts[g], axis=1)
+            values[g] = []
+        for r in range(c * near // chunks, (c + 1) * near // chunks):
+            part = parts[g][r * per_row : (r + 1) * per_row]
+            values[g].append(
+                jnp.dot(part, v_ref[g * near + r], preferred_element_type=jnp.float32)
             )
-            scores = jnp.dot(keys, weights, preferred_element_type=jnp.float32)
-            scores = jnp.where(position < limit - c * chunk, scores, negative)
-            scores_ref[g, pl.ds(c * chunk, chunk)] = scores
-            top = jnp.maximum(top, jnp.max(scores, axis=0, keepdims=True))
-        return top, fresh
-
-    def weigh(g, top, fresh):
-        fresh = jnp.exp(fresh - top)
-        total = jnp.sum(fresh, axis=0, keepdims=True)
-        parts = []
-        for c in range(cache_dev // chunk):
-            weight = jnp.exp(scores_ref[g, pl.ds(c * chunk, chunk)] - top)
-            total = total + jnp.sum(weight, axis=0, keepdims=True)
-            parts.append(weight.astype(jnp.bfloat16).T)
-        parts = jnp.concatenate(parts, axis=1)
-        value = jnp.concatenate(
-            [
-                jnp.dot(
-                    parts[r * per_row : (r + 1) * per_row],
-                    v_ref[g * near + r],
-                    preferred_element_type=jnp.float32,
-                )
-                for r in range(near)
-            ],
-            axis=0,
-        ) + jnp.dot(fresh.T.astype(jnp.bfloat16), new_values, preferred_element_type=jnp.float32)
+
+    def end(g):
+        value = jnp.concatenate(values[g], axis=0) + jnp.dot(
+            fresh[g].T.astype(jnp.bfloat16), new_values, preferred_element_type=jnp.float32
+        )
         for j in range(count):
             out_ref[j, pl.ds(g * SUB, SUB)] = value[j * SUB : (j + 1) * SUB]
-        return total
-
-    tops, totals = [], []
-    ready = score(0)
-    for g in range(groups):
-        later = score(g + 1) if g + 1 < groups else None
-        tops.append(ready[0])
-        totals.append(weigh(g, *ready))
-        ready = later
+
+    for g in range(groups + 2):
+        if g < groups:
+            begin(g)
+        for c in range(chunks):
+            if g < groups:
+                score(g, c)
+            if 0 <= g - 1 < groups:
+                weigh(g - 1, c)
+            if 0 <= g - 2:
+                add_up(g - 2, c)
+        if 0 <= g - 2:
+            end(g - 2)
+    tops = [tops[g] for g in range(groups)]
+    totals = [totals[g] for g in range(groups)]
     spare = jnp.zeros((SUB - 2 * groups, LANES), jnp.float32)
     stats = jnp.concatenate(tops + totals + [spare], axis=0)
     for j in range(count):
@@ -343,7 +354,7 @@
         in_hbm(embedding),
         in_hbm(w_qkv.reshape(feat, width)),
     )
-    for mask in (1, 2, 6):
+    for mask in (1, 6, 2):
         picked = double(picked, "head", mask, n_head)
     gain = norm_gain.astype(jnp.float32).reshape(1, feat)
 
@@ -377,7 +388,7 @@
         [VMEM] * 2,
         [pltpu.VMEM((own, n_seq * SUB, head_dim), jnp.float32)],
     )(attention, in_vmem(w_out[0]))
-    for mask in (2, 6, 1):
+    for mask in (6, 2, 1):
         terms = double(terms, "head", mask, n_head)
     return terms.astype(jnp.bfloat16).reshape(2, row_count, -1)
 

time: 82.1 us -> 82.1 us (level)
  waiting for transfers between devices: 10.9 us -> 12.3 us
  starting transfers between devices: 19.2 us -> 17.9 us
    ppermute x6, starting transfers between devices: 19.2 us -> 17.9 us  [double(): return array + lax.ppermute(array, axis_name, pairs)]
    ppermute x6, waiting for transfers between devices: 10.9 us -> 12.3 us  [double(): return array + lax.ppermute(array, axis_name, pairs)]
where the time goes in v6:
time: 82.1 us; the launch traced here: 81.8 us
  blocking collectives  43.5 us (53%)
  starting transfers between devices  17.9 us (22%)
  waiting for transfers between devices  12.3 us (15%)
  Pallas kernels  7.28 us (9%)
    all_to_all x4, blocking collectives, swap(): return lax.all_to_all(array, axis_name, 0, 0, tiled=True)  43.5 us
    ppermute x6, starting transfers between devices, double(): return array + lax.ppermute(array, axis_name, pairs)  17.9 us
    ppermute x6, waiting for transfers between devices, double(): return array + lax.ppermute(array, axis_name, pairs)  12.3 us
    pallas_call x1, Pallas kernels, body(): pl.pallas_call(functools.partial(pick_kernel, cache_dev), out_shape=[jax....  3.08 us
    pallas_call x1, Pallas kernels, body(): call(attend_kernel, 'attend', ((n_seq, BLOCK, head_dim), jnp.float32), [V...  3.04 us
  transfers between devices with their start and end apart: 6, of which 6 were waited for; matrix products, arithmetic and copies ran while one was open for 0% of the time, Pallas kernels for 0%

profile of v6, /device:TPU:1, one launch (start us, length us, event | category | flops | bytes accessed | tf_op | source)
XLA Modules:
  0.0 81.8 jit_solution(507668955170355603)
XLA Ops:
  0.0 0.0 copy-start.2
  0.0 0.1 maximum_bitcast_fusion.frequency_ref
  0.1 0.0 slice-start
  0.1 0.0 slice-start.1
  0.1 0.0 copy-start
  0.1 3.1 %pick.1 = (bf16[48,512]{1,0:T(8,128)(2,1)S(1)}, f32[64,128]{1,0:T(8,128)S(1)}, s32[8,128]{1,0:T(8,128)S(1)}, bf16[512,1280]{1,0:T(8,128)(2,1)S(1)}) custom-call(s32[2,24]{1,0:T(2,128)} %ids_ref.1, s32[24]{0:T(128)} %lengths_ref.1, f32[1,128]{1,0:T(1,128)S(1)} %maximum_bitcast_fusion.frequency_ref, bf16[8016,512]{1,0:T(8,128)(2,1)} %table_ref.1, ...), custom_call_target="tpu_custom_call" | custom-call | tf_op jit(solution)/shard_map/pick/pallas_call | solution.py:333
  3.2 1.5 %collective-permute-start = (bf16[48,512]{1,0:T(8,128)(2,1)S(1)}, bf16[48,512]{1,0:T(8,128)(2,1)S(1)}, u32[]{:S(2)}, u32[]{:S(2)}) collective-permute-start(bf16[48,512]{1,0:T(8,128)(2,1)S(1)} %get-tuple-element.10), channel_id=1, source_target_pairs={{0,1},{1,0},{2,3},{3,2},{4,5},{5,4},{6,7},{7,6},{8,9},{9,8},{10,11... | collective-permute-start | bytes 147464 | tf_op jit(solution)/shard_map/ppermute | solution.py:322
  4.7 0.9 %collective-permute-done = bf16[48,512]{1,0:T(8,128)(2,1)S(1)} collective-permute-done((bf16[48,512]{1,0:T(8,128)(2,1)S(1)}, bf16[48,512]{1,0:T(8,128)(2,1)S(1)}, u32[]{:S(2)}, u32[]{:S(2)}) %collective-permute-start) | collective-permute-done | bytes 49184 | tf_op jit(solution)/shard_map/ppermute | solution.py:322
  5.6 3.9 %collective-permute-start.1 = (bf16[48,512]{1,0:T(8,128)(2,1)S(1)}, bf16[48,512]{1,0:T(8,128)(2,1)S(1)}, u32[]{:S(2)}, u32[]{:S(2)}) collective-permute-start(bf16[48,512]{1,0:T(8,128)(2,1)S(1)} %add.18), channel_id=1, source_target_pairs={{0,6},{1,7},{2,4},{3,5},{4,2},{5,3},{6,0},{7,1},{8,14},{9,15},{10,... | collective-permute-start | bytes 147464 | tf_op jit(solution)/shard_map/ppermute | solution.py:322
  9.5 1.5 %collective-permute-done.1 = bf16[48,512]{1,0:T(8,128)(2,1)S(1)} collective-permute-done((bf16[48,512]{1,0:T(8,128)(2,1)S(1)}, bf16[48,512]{1,0:T(8,128)(2,1)S(1)}, u32[]{:S(2)}, u32[]{:S(2)}) %collective-permute-start.1) | collective-permute-done | bytes 49184 | tf_op jit(solution)/shard_map/ppermute | solution.py:322
  11.0 0.1 collective-permute-start.2
  11.1 0.0 copy-done.2
  11.1 2.9 %collective-permute-done.2 = bf16[48,512]{1,0:T(8,128)(2,1)S(1)} collective-permute-done((bf16[48,512]{1,0:T(8,128)(2,1)S(1)}, bf16[48,512]{1,0:T(8,128)(2,1)S(1)}, u32[]{:S(2)}, u32[]{:S(2)}) %collective-permute-start.2) | collective-permute-done | bytes 49184 | tf_op jit(solution)/shard_map/ppermute | solution.py:322
  14.0 0.4 project.1
  14.4 14.2 %all_to_all.20.parts_ref = f32[16,32,128]{2,1,0:T(8,128)S(1)} all-to-all(f32[16,32,128]{2,1,0:T(8,128)S(1)} %bitcast.13), channel_id=1, replica_groups=mesh['seq'=16,'head'=8] {'seq'}, dimensions={0} | all-to-all | bytes 524288 | tf_op jit(solution)/shard_map/all_to_all | solution.py:47
  28.6 0.2 finish.1
  28.9 9.6 %all_to_all.21.rows_ref = bf16[16,32,128]{2,1,0:T(8,128)(2,1)S(1)} all-to-all(bf16[16,32,128]{2,1,0:T(8,128)(2,1)S(1)} %finish.1), channel_id=1, replica_groups=mesh['seq'=16,'head'=8] {'seq'}, dimensions={0} | all-to-all | bytes 262144 | tf_op jit(solution)/shard_map/all_to_all | solution.py:47
  38.5 0.0 slice-done
  38.5 0.0 slice-done.1
  38.5 0.0 copy-done
  38.5 0.0 copy-start.1
  38.5 3.0 %attend.1 = f32[16,32,128]{2,1,0:T(8,128)S(1)} custom-call(s32[8,128]{1,0:T(8,128)S(1)} %get-tuple-element.9.limits_ref, bf16[16,32,128]{2,1,0:T(8,128)(2,1)S(1)} %all_to_all.21.rows_ref, bf16[24,1024,128]{2,1,0:T(8,128)(2,1)S(1)} %bitcast.11, bf16[24,1024,128]{2,1,0:T(8,128)(2,1)S(1)} %bitcast.12), custom_call_target="tpu_custom_call" | custom-call | tf_op jit(solution)/shard_map/attend/pallas_call | solution.py:370
  41.6 10.3 %all_to_all.22.parts_ref = f32[16,32,128]{2,1,0:T(8,128)S(1)} all-to-all(f32[16,32,128]{2,1,0:T(8,128)S(1)} %attend.1), channel_id=1, replica_groups=mesh['seq'=16,'head'=8] {'seq'}, dimensions={0} | all-to-all | bytes 524288 | tf_op jit(solution)/shard_map/all_to_all | solution.py:47
  51.9 0.3 merge.1
  52.2 9.3 %all_to_all.23.attention_ref = bf16[16,8,384]{2,1,0:T(8,128)(2,1)S(1)} all-to-all(bf16[16,8,384]{2,1,0:T(8,128)(2,1)S(1)} %merge.1), channel_id=1, replica_groups=mesh['seq'=16,'head'=8] {'seq'}, dimensions={0} | all-to-all | bytes 196608 | tf_op jit(solution)/shard_map/all_to_all | solution.py:47
  61.5 0.0 copy-done.1
  61.5 0.3 output.1
  61.8 2.4 %collective-permute-start.3 = (f32[48,512]{1,0:T(8,128)S(1)}, f32[48,512]{1,0:T(8,128)S(1)}, u32[]{:S(2)}, u32[]{:S(2)}) collective-permute-start(f32[48,512]{1,0:T(8,128)S(1)} %output.1), channel_id=1, source_target_pairs={{0,6},{1,7},{2,4},{3,5},{4,2},{5,3},{6,0},{7,1},{8,14},{9,15},{10,... | collective-permute-start | bytes 294920 | tf_op jit(solution)/shard_map/ppermute | solution.py:322
  64.2 2.6 %collective-permute-done.3 = f32[48,512]{1,0:T(8,128)S(1)} collective-permute-done((f32[48,512]{1,0:T(8,128)S(1)}, f32[48,512]{1,0:T(8,128)S(1)}, u32[]{:S(2)}, u32[]{:S(2)}) %collective-permute-start.3) | collective-permute-done | bytes 98336 | tf_op jit(solution)/shard_map/ppermute | solution.py:322
  66.8 0.1 collective-permute-start.4
  66.9 3.5 %collective-permute-done.4 = f32[48,512]{1,0:T(8,128)S(1)} collective-permute-done((f32[48,512]{1,0:T(8,128)S(1)}, f32[48,512]{1,0:T(8,128)S(1)}, u32[]{:S(2)}, u32[]{:S(2)}) %collective-permute-start.4) | collective-permute-done | bytes 98336 | tf_op jit(solution)/shard_map/ppermute | solution.py:322
  70.3 9.9 %collective-permute-start.5 = (f32[48,512]{1,0:T(8,128)S(1)}, f32[48,512]{1,0:T(8,128)S(1)}, u32[]{:S(2)}, u32[]{:S(2)}) collective-permute-start(f32[48,512]{1,0:T(8,128)S(1)} %add.22), channel_id=1, source_target_pairs={{0,1},{1,0},{2,3},{3,2},{4,5},{5,4},{6,7},{7,6},{8,9},{9,8},{10,11... | collective-permute-start | bytes 294920 | tf_op jit(solution)/shard_map/ppermute | solution.py:322
  80.2 0.9 %collective-permute-done.5 = f32[48,512]{1,0:T(8,128)S(1)} collective-permute-done((f32[48,512]{1,0:T(8,128)S(1)}, f32[48,512]{1,0:T(8,128)S(1)}, u32[]{:S(2)}, u32[]{:S(2)}) %collective-permute-start.5) | collective-permute-done | bytes 98336 | tf_op jit(solution)/shard_map/ppermute | solution.py:322
  81.2 0.6 add_convert_fusion
  (8 shorter events, 0.1 us)
Async XLA Ops:
  0.0 11.1 %copy-start.2 = (bf16[512]{0:T(512)(128)(2,1)S(1)}, bf16[512]{0:T(512)(128)(2,1)}, u32[]{:S(2)}) copy-start(bf16[512]{0:T(512)(128)(2,1)} %param.11) | copy-start | bytes 3076
  0.1 38.4 %slice-start = ((s8[6291456]{0:T(1024)(128)(4,1)}), s8[4194304]{0:T(1024)(128)(4,1)S(1)}, s32[]{:S(2)}) async-start(s8[6291456]{0:T(1024)(128)(4,1)} %bitcast.9), calls=%async_computation.4 | async-start | bytes 8388608
  0.1 38.4 %slice-start.1 = ((s8[6291456]{0:T(1024)(128)(4,1)}), s8[2097152]{0:T(1024)(128)(4,1)S(1)}, s32[]{:S(2)}) async-start(s8[6291456]{0:T(1024)(128)(4,1)} %bitcast.9), calls=%async_computation.5 | async-start | bytes 4194304
  0.1 38.4 %copy-start = (bf16[24,1,1024,128]{3,2,1,0:T(8,128)(2,1)S(1)}, bf16[24,1,1024,128]{3,2,1,0:T(8,128)(2,1)}, u32[]{:S(2)}) copy-start(bf16[24,1,1024,128]{3,2,1,0:T(8,128)(2,1)} %param.14) | copy-start | bytes 18874372
  3.2 2.4 %collective-permute-start = (bf16[48,512]{1,0:T(8,128)(2,1)S(1)}, bf16[48,512]{1,0:T(8,128)(2,1)S(1)}, u32[]{:S(2)}, u32[]{:S(2)}) collective-permute-start(bf16[48,512]{1,0:T(8,128)(2,1)S(1)} %get-tuple-element.10), channel_id=1, source_target_pairs={{0,1},{1,0},{2,3},{3,2},{4,5},{5,4},{6,7},{7,6},{8,9},{9,8},{10,11... | collective-permute-start | bytes 147464 | tf_op jit(solution)/shard_map/ppermute | solution.py:322
  5.6 5.4 %collective-permute-start.1 = (bf16[48,512]{1,0:T(8,128)(2,1)S(1)}, bf16[48,512]{1,0:T(8,128)(2,1)S(1)}, u32[]{:S(2)}, u32[]{:S(2)}) collective-permute-start(bf16[48,512]{1,0:T(8,128)(2,1)S(1)} %add.18), channel_id=1, source_target_pairs={{0,6},{1,7},{2,4},{3,5},{4,2},{5,3},{6,0},{7,1},{8,14},{9,15},{10,... | collective-permute-start | bytes 147464 | tf_op jit(solution)/shard_map/ppermute | solution.py:322
  11.0 3.0 %collective-permute-start.2 = (bf16[48,512]{1,0:T(8,128)(2,1)S(1)}, bf16[48,512]{1,0:T(8,128)(2,1)S(1)}, u32[]{:S(2)}, u32[]{:S(2)}) collective-permute-start(bf16[48,512]{1,0:T(8,128)(2,1)S(1)} %add.19), channel_id=1, source_target_pairs={{0,2},{1,3},{2,0},{3,1},{4,6},{5,7},{6,4},{7,5},{8,10},{9,11},{10,... | collective-permute-start | bytes 147464 | tf_op jit(solution)/shard_map/ppermute | solution.py:322
  38.5 23.0 %copy-start.1 = (bf16[1,1024,512]{2,1,0:T(8,128)(2,1)S(1)}, bf16[1,1024,512]{2,1,0:T(8,128)(2,1)}, u32[]{:S(2)}) copy-start(bf16[1,1024,512]{2,1,0:T(8,128)(2,1)} %param.15) | copy-start | bytes 3145732
  61.8 5.0 %collective-permute-start.3 = (f32[48,512]{1,0:T(8,128)S(1)}, f32[48,512]{1,0:T(8,128)S(1)}, u32[]{:S(2)}, u32[]{:S(2)}) collective-permute-start(f32[48,512]{1,0:T(8,128)S(1)} %output.1), channel_id=1, source_target_pairs={{0,6},{1,7},{2,4},{3,5},{4,2},{5,3},{6,0},{7,1},{8,14},{9,15},{10,... | collective-permute-start | bytes 294920 | tf_op jit(solution)/shard_map/ppermute | solution.py:322
  66.8 3.5 %collective-permute-start.4 = (f32[48,512]{1,0:T(8,128)S(1)}, f32[48,512]{1,0:T(8,128)S(1)}, u32[]{:S(2)}, u32[]{:S(2)}) collective-permute-start(f32[48,512]{1,0:T(8,128)S(1)} %add.21), channel_id=1, source_target_pairs={{0,2},{1,3},{2,0},{3,1},{4,6},{5,7},{6,4},{7,5},{8,10},{9,11},{10,... | collective-permute-start | bytes 294920 | tf_op jit(solution)/shard_map/ppermute | solution.py:322
  70.3 10.8 %collective-permute-start.5 = (f32[48,512]{1,0:T(8,128)S(1)}, f32[48,512]{1,0:T(8,128)S(1)}, u32[]{:S(2)}, u32[]{:S(2)}) collective-permute-start(f32[48,512]{1,0:T(8,128)S(1)} %add.22), channel_id=1, source_target_pairs={{0,1},{1,0},{2,3},{3,2},{4,5},{5,4},{6,7},{7,6},{8,9},{9,8},{10,11... | collective-permute-start | bytes 294920 | tf_op jit(solution)/shard_map/ppermute | solution.py:322

commit v7 on v4

--- a/solution.py
+++ b/solution.py
@@ -71,8 +71,8 @@
 
 
 def pick_kernel(
-    cache_dev, ids_ref, lengths_ref, frequency_ref, table_ref, far_w_ref,
-    x_ref, rope_ref, limits_ref, w_ref, held, sem, w_sem,
+    cache_dev, ids_ref, lengths_ref, frequency_ref, table_ref,
+    x_ref, rope_ref, limits_ref, held, sem,
 ):
     vocab_dev, feat = table_ref.shape
     steps, rows = ids_ref.shape
@@ -97,8 +97,6 @@
 
         found = found + inside.astype(jnp.int32)
         places.append(jnp.where(inside, i * TILE + within, -1))
-    w_copy = pltpu.make_async_copy(far_w_ref, w_ref, w_sem)
-    w_copy.start(priority=1)
 
     me = lax.axis_index("seq")
     near = LANES // (2 * SUB)
@@ -136,7 +134,27 @@
     lax.fori_loop(0, found, wait, 0)
     picked = jnp.dot(select, held[...], preferred_element_type=jnp.float32)
     x_ref[...] = picked.astype(jnp.bfloat16)
-    w_copy.wait()
+
+
+def fetch_kernel(after_ref, far_ref, near_ref, sem):
+    copy = pltpu.make_async_copy(far_ref, near_ref, sem)
+    copy.start()
+    copy.wait()
+
+
+def fetch(after, array):
+    return pl.pallas_call(
+        fetch_kernel,
+        out_shape=pltpu.VMEM(array.shape, array.dtype),
+        in_specs=[ANY] * 2,
+        out_specs=VMEM,
+        scratch_shapes=[pltpu.SemaphoreType.DMA],
+        cost_estimate=pl.CostEstimate(
+            flops=0, bytes_accessed=2 * array.size * array.dtype.itemsize, transcendentals=0
+        ),
+        compiler_params=pltpu.CompilerParams(vmem_limit_bytes=4 << 20),
+        name="fetch",
+    )(after, in_hbm(array))
 
 
 def project_kernel(x_ref, gain_ref, w_ref, out_ref):
@@ -319,19 +337,17 @@
     own = tokens // n_seq
     width = w_qkv.shape[2]
 
-    picked, rope, limits, w_near = pl.pallas_call(
+    picked, rope, limits = pl.pallas_call(
         functools.partial(pick_kernel, cache_dev),
         out_shape=[
             jax.ShapeDtypeStruct((tokens, feat), jnp.bfloat16),
             jax.ShapeDtypeStruct((2 * BLOCK, LANES), jnp.float32),
             jax.ShapeDtypeStruct((SUB, LANES), jnp.int32),
-            pltpu.VMEM((feat, width), jnp.bfloat16),
         ],
-        in_specs=[SMEM, SMEM, VMEM, ANY, ANY],
-        out_specs=[VMEM] * 4,
+        in_specs=[SMEM, SMEM, VMEM, ANY],
+        out_specs=[VMEM] * 3,
         scratch_shapes=[
             pltpu.VMEM((tokens * TILE, feat), jnp.bfloat16),
-            pltpu.SemaphoreType.DMA,
             pltpu.SemaphoreType.DMA,
         ],
         compiler_params=pltpu.CompilerParams(vmem_limit_bytes=8 << 20),
@@ -341,8 +357,8 @@
         in_hbm(lengths),
         rope_frequency(head_dim),
         in_hbm(embedding),
-        in_hbm(w_qkv.reshape(feat, width)),
-    )
+    )
+    w_near = fetch(picked, w_qkv.reshape(feat, width))
     for mask in (1, 2, 6):
         picked = double(picked, "head", mask, n_head)
     gain = norm_gain.astype(jnp.float32).reshape(1, feat)

time: 82.1 us -> 81.8 us (level)
  waiting for transfers between devices: 10.9 us -> 9.59 us
  Pallas kernels: 7.19 us -> 8.1 us
    ppermute x6, waiting for transfers between devices: 10.9 us -> 9.59 us  [double(): return array + lax.ppermute(array, axis_name, pairs)]
    pallas_call x0 -> x1, Pallas kernels: none -> 1.32 us  [fetch(): pl.pallas_call(fetch_kernel, out_shape=pltpu.VMEM(array.shape, array.dtyp...]
  transfers between devices with their start and end apart: 6 -> 6, of which waited for: 6 -> 6; matrix products, arithmetic and copies ran while one was open for 0% -> 0% of each run, Pallas kernels for 0% -> 2%
where the time goes in v7:
time: 81.8 us; the launch traced here: 81.3 us
  blocking collectives  43.5 us (53%)
  starting transfers between devices  19.2 us (23%)
  waiting for transfers between devices  9.59 us (12%)
  Pallas kernels  8.1 us (10%)
    all_to_all x4, blocking collectives, swap(): return lax.all_to_all(array, axis_name, 0, 0, tiled=True)  43.5 us
    ppermute x6, starting transfers between devices, double(): return array + lax.ppermute(array, axis_name, pairs)  19.2 us
    ppermute x6, waiting for transfers between devices, double(): return array + lax.ppermute(array, axis_name, pairs)  9.59 us
    pallas_call x1, Pallas kernels, body(): call(attend_kernel, 'attend', ((n_seq, BLOCK, head_dim), jnp.float32), [V...  2.97 us
    pallas_call x1, Pallas kernels, body(): pl.pallas_call(functools.partial(pick_kernel, cache_dev), out_shape=[jax....  2.65 us
  transfers between devices with their start and end apart: 6, of which 6 were waited for; matrix products, arithmetic and copies ran while one was open for 0% of the time, Pallas kernels for 2%

profile of v7, /device:TPU:1, one launch (start us, length us, event | category | flops | bytes accessed | tf_op | source)
XLA Modules:
  0.0 81.3 jit_solution(16997367724634877465)
XLA Ops:
  0.0 0.0 copy-start.2
  0.0 0.0 slice-start
  0.0 0.1 maximum_bitcast_fusion.frequency_ref
  0.1 0.0 slice-start.1
  0.1 0.0 copy-start
  0.1 2.6 %pick.1 = (bf16[48,512]{1,0:T(8,128)(2,1)S(1)}, f32[64,128]{1,0:T(8,128)S(1)}, s32[8,128]{1,0:T(8,128)S(1)}) custom-call(s32[2,24]{1,0:T(2,128)} %ids_ref.1, s32[24]{0:T(128)} %lengths_ref.1, f32[1,128]{1,0:T(1,128)S(1)} %maximum_bitcast_fusion.frequency_ref, bf16[8016,512]{1,0:T(8,128)(2,1)} %table_ref.1), custom_call_target="tpu_custom_call" | custom-call | tf_op jit(solution)/shard_map/pick/pallas_call | solution.py:340
  2.8 1.6 %collective-permute-start = (bf16[48,512]{1,0:T(8,128)(2,1)S(1)}, bf16[48,512]{1,0:T(8,128)(2,1)S(1)}, u32[]{:S(2)}, u32[]{:S(2)}) collective-permute-start(bf16[48,512]{1,0:T(8,128)(2,1)S(1)} %get-tuple-element.9.after_ref), channel_id=1, source_target_pairs={{0,1},{1,0},{2,3},{3,2},{4,5},{5,4},{6,7},{7,6},{8,9},{9,8},{10,11... | collective-permute-start | bytes 147464 | tf_op jit(solution)/shard_map/ppermute | solution.py:329
  4.3 0.9 %collective-permute-done = bf16[48,512]{1,0:T(8,128)(2,1)S(1)} collective-permute-done((bf16[48,512]{1,0:T(8,128)(2,1)S(1)}, bf16[48,512]{1,0:T(8,128)(2,1)S(1)}, u32[]{:S(2)}, u32[]{:S(2)}) %collective-permute-start) | collective-permute-done | bytes 49184 | tf_op jit(solution)/shard_map/ppermute | solution.py:329
  5.2 1.8 %collective-permute-start.1 = (bf16[48,512]{1,0:T(8,128)(2,1)S(1)}, bf16[48,512]{1,0:T(8,128)(2,1)S(1)}, u32[]{:S(2)}, u32[]{:S(2)}) collective-permute-start(bf16[48,512]{1,0:T(8,128)(2,1)S(1)} %add.18), channel_id=1, source_target_pairs={{0,2},{1,3},{2,0},{3,1},{4,6},{5,7},{6,4},{7,5},{8,10},{9,11},{10,... | collective-permute-start | bytes 147464 | tf_op jit(solution)/shard_map/ppermute | solution.py:329
  7.0 1.5 %collective-permute-done.1 = bf16[48,512]{1,0:T(8,128)(2,1)S(1)} collective-permute-done((bf16[48,512]{1,0:T(8,128)(2,1)S(1)}, bf16[48,512]{1,0:T(8,128)(2,1)S(1)}, u32[]{:S(2)}, u32[]{:S(2)}) %collective-permute-start.1) | collective-permute-done | bytes 49184 | tf_op jit(solution)/shard_map/ppermute | solution.py:329
  8.5 3.6 %collective-permute-start.2 = (bf16[48,512]{1,0:T(8,128)(2,1)S(1)}, bf16[48,512]{1,0:T(8,128)(2,1)S(1)}, u32[]{:S(2)}, u32[]{:S(2)}) collective-permute-start(bf16[48,512]{1,0:T(8,128)(2,1)S(1)} %add.19), channel_id=1, source_target_pairs={{0,6},{1,7},{2,4},{3,5},{4,2},{5,3},{6,0},{7,1},{8,14},{9,15},{10,... | collective-permute-start | bytes 147464 | tf_op jit(solution)/shard_map/ppermute | solution.py:329
  12.2 0.0 copy-done.2
  12.2 1.3 %fetch.1.w_ref = bf16[512,1280]{1,0:T(8,128)(2,1)S(1)} custom-call(bf16[48,512]{1,0:T(8,128)(2,1)S(1)} %get-tuple-element.9.after_ref, bf16[512,1280]{1,0:T(8,128)(2,1)} %bitcast.16), custom_call_target="tpu_custom_call" | custom-call | bytes 2621440 | tf_op jit(solution)/shard_map/fetch/pallas_call | solution.py:146
  13.5 0.1 collective-permute-done.2
  13.7 0.4 project.1
  14.0 14.2 %all_to_all.20.parts_ref = f32[16,32,128]{2,1,0:T(8,128)S(1)} all-to-all(f32[16,32,128]{2,1,0:T(8,128)S(1)} %bitcast.13), channel_id=1, replica_groups=mesh['seq'=16,'head'=8] {'seq'}, dimensions={0} | all-to-all | bytes 524288 | tf_op jit(solution)/shard_map/all_to_all | solution.py:47
  28.3 0.2 finish.1
  28.5 9.6 %all_to_all.21.rows_ref = bf16[16,32,128]{2,1,0:T(8,128)(2,1)S(1)} all-to-all(bf16[16,32,128]{2,1,0:T(8,128)(2,1)S(1)} %finish.1), channel_id=1, replica_groups=mesh['seq'=16,'head'=8] {'seq'}, dimensions={0} | all-to-all | bytes 262144 | tf_op jit(solution)/shard_map/all_to_all | solution.py:47
  38.1 0.0 slice-done
  38.1 0.0 slice-done.1
  38.1 0.0 copy-done
  38.1 0.0 copy-start.1
  38.1 3.0 %attend.1 = f32[16,32,128]{2,1,0:T(8,128)S(1)} custom-call(s32[8,128]{1,0:T(8,128)S(1)} %get-tuple-element.8.limits_ref, bf16[16,32,128]{2,1,0:T(8,128)(2,1)S(1)} %all_to_all.21.rows_ref, bf16[24,1024,128]{2,1,0:T(8,128)(2,1)S(1)} %bitcast.11, bf16[24,1024,128]{2,1,0:T(8,128)(2,1)S(1)} %bitcast.12), custom_call_target="tpu_custom_call" | custom-call | tf_op jit(solution)/shard_map/attend/pallas_call | solution.py:375
  41.1 10.3 %all_to_all.22.parts_ref = f32[16,32,128]{2,1,0:T(8,128)S(1)} all-to-all(f32[16,32,128]{2,1,0:T(8,128)S(1)} %attend.1), channel_id=1, replica_groups=mesh['seq'=16,'head'=8] {'seq'}, dimensions={0} | all-to-all | bytes 524288 | tf_op jit(solution)/shard_map/all_to_all | solution.py:47
  51.5 0.3 merge.1
  51.8 9.3 %all_to_all.23.attention_ref = bf16[16,8,384]{2,1,0:T(8,128)(2,1)S(1)} all-to-all(bf16[16,8,384]{2,1,0:T(8,128)(2,1)S(1)} %merge.1), channel_id=1, replica_groups=mesh['seq'=16,'head'=8] {'seq'}, dimensions={0} | all-to-all | bytes 196608 | tf_op jit(solution)/shard_map/all_to_all | solution.py:47
  61.0 0.0 copy-done.1
  61.0 0.3 output.1
  61.3 0.0 collective-permute-start.3
  61.3 3.8 %collective-permute-done.3 = f32[48,512]{1,0:T(8,128)S(1)} collective-permute-done((f32[48,512]{1,0:T(8,128)S(1)}, f32[48,512]{1,0:T(8,128)S(1)}, u32[]{:S(2)}, u32[]{:S(2)}) %collective-permute-start.3) | collective-permute-done | bytes 98336 | tf_op jit(solution)/shard_map/ppermute | solution.py:329
  65.1 2.4 %collective-permute-start.4 = (f32[48,512]{1,0:T(8,128)S(1)}, f32[48,512]{1,0:T(8,128)S(1)}, u32[]{:S(2)}, u32[]{:S(2)}) collective-permute-start(f32[48,512]{1,0:T(8,128)S(1)} %add.21), channel_id=1, source_target_pairs={{0,6},{1,7},{2,4},{3,5},{4,2},{5,3},{6,0},{7,1},{8,14},{9,15},{10,... | collective-permute-start | bytes 294920 | tf_op jit(solution)/shard_map/ppermute | solution.py:329
  67.5 2.4 %collective-permute-done.4 = f32[48,512]{1,0:T(8,128)S(1)} collective-permute-done((f32[48,512]{1,0:T(8,128)S(1)}, f32[48,512]{1,0:T(8,128)S(1)}, u32[]{:S(2)}, u32[]{:S(2)}) %collective-permute-start.4) | collective-permute-done | bytes 98336 | tf_op jit(solution)/shard_map/ppermute | solution.py:329
  69.9 9.9 %collective-permute-start.5 = (f32[48,512]{1,0:T(8,128)S(1)}, f32[48,512]{1,0:T(8,128)S(1)}, u32[]{:S(2)}, u32[]{:S(2)}) collective-permute-start(f32[48,512]{1,0:T(8,128)S(1)} %add.22), channel_id=1, source_target_pairs={{0,1},{1,0},{2,3},{3,2},{4,5},{5,4},{6,7},{7,6},{8,9},{9,8},{10,11... | collective-permute-start | bytes 294920 | tf_op jit(solution)/shard_map/ppermute | solution.py:329
  79.8 0.9 %collective-permute-done.5 = f32[48,512]{1,0:T(8,128)S(1)} collective-permute-done((f32[48,512]{1,0:T(8,128)S(1)}, f32[48,512]{1,0:T(8,128)S(1)}, u32[]{:S(2)}, u32[]{:S(2)}) %collective-permute-start.5) | collective-permute-done | bytes 98336 | tf_op jit(solution)/shard_map/ppermute | solution.py:329
  80.7 0.6 add_convert_fusion
  (8 shorter events, 0.1 us)
Async XLA Ops:
  0.0 12.2 %copy-start.2 = (bf16[512]{0:T(512)(128)(2,1)S(1)}, bf16[512]{0:T(512)(128)(2,1)}, u32[]{:S(2)}) copy-start(bf16[512]{0:T(512)(128)(2,1)} %param.11) | copy-start | bytes 3076
  0.0 38.1 %slice-start = ((s8[6291456]{0:T(1024)(128)(4,1)}), s8[4194304]{0:T(1024)(128)(4,1)S(1)}, s32[]{:S(2)}) async-start(s8[6291456]{0:T(1024)(128)(4,1)} %bitcast.9), calls=%async_computation.4 | async-start | bytes 8388608
  0.1 38.0 %slice-start.1 = ((s8[6291456]{0:T(1024)(128)(4,1)}), s8[2097152]{0:T(1024)(128)(4,1)S(1)}, s32[]{:S(2)}) async-start(s8[6291456]{0:T(1024)(128)(4,1)} %bitcast.9), calls=%async_computation.5 | async-start | bytes 4194304
  0.1 38.0 %copy-start = (bf16[24,1,1024,128]{3,2,1,0:T(8,128)(2,1)S(1)}, bf16[24,1,1024,128]{3,2,1,0:T(8,128)(2,1)}, u32[]{:S(2)}) copy-start(bf16[24,1,1024,128]{3,2,1,0:T(8,128)(2,1)} %param.14) | copy-start | bytes 18874372
  2.8 2.4 %collective-permute-start = (bf16[48,512]{1,0:T(8,128)(2,1)S(1)}, bf16[48,512]{1,0:T(8,128)(2,1)S(1)}, u32[]{:S(2)}, u32[]{:S(2)}) collective-permute-start(bf16[48,512]{1,0:T(8,128)(2,1)S(1)} %get-tuple-element.9.after_ref), channel_id=1, source_target_pairs={{0,1},{1,0},{2,3},{3,2},{4,5},{5,4},{6,7},{7,6},{8,9},{9,8},{10,11... | collective-permute-start | bytes 147464 | tf_op jit(solution)/shard_map/ppermute | solution.py:329
  5.2 3.3 %collective-permute-start.1 = (bf16[48,512]{1,0:T(8,128)(2,1)S(1)}, bf16[48,512]{1,0:T(8,128)(2,1)S(1)}, u32[]{:S(2)}, u32[]{:S(2)}) collective-permute-start(bf16[48,512]{1,0:T(8,128)(2,1)S(1)} %add.18), channel_id=1, source_target_pairs={{0,2},{1,3},{2,0},{3,1},{4,6},{5,7},{6,4},{7,5},{8,10},{9,11},{10,... | collective-permute-start | bytes 147464 | tf_op jit(solution)/shard_map/ppermute | solution.py:329
  8.5 5.1 %collective-permute-start.2 = (bf16[48,512]{1,0:T(8,128)(2,1)S(1)}, bf16[48,512]{1,0:T(8,128)(2,1)S(1)}, u32[]{:S(2)}, u32[]{:S(2)}) collective-permute-start(bf16[48,512]{1,0:T(8,128)(2,1)S(1)} %add.19), channel_id=1, source_target_pairs={{0,6},{1,7},{2,4},{3,5},{4,2},{5,3},{6,0},{7,1},{8,14},{9,15},{10,... | collective-permute-start | bytes 147464 | tf_op jit(solution)/shard_map/ppermute | solution.py:329
  38.1 22.9 %copy-start.1 = (bf16[1,1024,512]{2,1,0:T(8,128)(2,1)S(1)}, bf16[1,1024,512]{2,1,0:T(8,128)(2,1)}, u32[]{:S(2)}) copy-start(bf16[1,1024,512]{2,1,0:T(8,128)(2,1)} %param.15) | copy-start | bytes 3145732
  61.3 3.8 %collective-permute-start.3 = (f32[48,512]{1,0:T(8,128)S(1)}, f32[48,512]{1,0:T(8,128)S(1)}, u32[]{:S(2)}, u32[]{:S(2)}) collective-permute-start(f32[48,512]{1,0:T(8,128)S(1)} %output.1), channel_id=1, source_target_pairs={{0,2},{1,3},{2,0},{3,1},{4,6},{5,7},{6,4},{7,5},{8,10},{9,11},{10,... | collective-permute-start | bytes 294920 | tf_op jit(solution)/shard_map/ppermute | solution.py:329
  65.1 4.8 %collective-permute-start.4 = (f32[48,512]{1,0:T(8,128)S(1)}, f32[48,512]{1,0:T(8,128)S(1)}, u32[]{:S(2)}, u32[]{:S(2)}) collective-permute-start(f32[48,512]{1,0:T(8,128)S(1)} %add.21), channel_id=1, source_target_pairs={{0,6},{1,7},{2,4},{3,5},{4,2},{5,3},{6,0},{7,1},{8,14},{9,15},{10,... | collective-permute-start | bytes 294920 | tf_op jit(solution)/shard_map/ppermute | solution.py:329
  69.9 10.8 %collective-permute-start.5 = (f32[48,512]{1,0:T(8,128)S(1)}, f32[48,512]{1,0:T(8,128)S(1)}, u32[]{:S(2)}, u32[]{:S(2)}) collective-permute-start(f32[48,512]{1,0:T(8,128)S(1)} %add.22), channel_id=1, source_target_pairs={{0,1},{1,0},{2,3},{3,2},{4,5},{5,4},{6,7},{7,6},{8,9},{9,8},{10,11... | collective-permute-start | bytes 294920 | tf_op jit(solution)/shard_map/ppermute | solution.py:329

commit v8 on v7

--- a/solution.py
+++ b/solution.py
@@ -70,10 +70,7 @@
     )
 
 
-def pick_kernel(
-    cache_dev, ids_ref, lengths_ref, frequency_ref, table_ref,
-    x_ref, rope_ref, limits_ref, held, sem,
-):
+def pick_kernel(ids_ref, table_ref, x_ref, held, sem):
     vocab_dev, feat = table_ref.shape
     steps, rows = ids_ref.shape
     tokens = steps * rows
@@ -98,6 +95,29 @@
         found = found + inside.astype(jnp.int32)
         places.append(jnp.where(inside, i * TILE + within, -1))
 
+    near = LANES // (2 * SUB)
+    row = lax.broadcasted_iota(jnp.int32, (tokens, 1), 0)
+    choice = jnp.full((tokens, 1), -1, jnp.int32)
+    for i in range(tokens):
+        step, r = i // rows, i % rows
+        choice = jnp.where(row == r // near * 2 * near + r % near * 2 + step, places[i], choice)
+    column = lax.broadcasted_iota(jnp.int32, (tokens, tokens * TILE), 1)
+    select = jnp.where(column == choice, 1.0, 0.0).astype(jnp.bfloat16)
+    def wait(i, carry):
+        pltpu.make_async_copy(table_ref.at[pl.ds(0, TILE)], held.at[pl.ds(0, TILE)], sem).wait()
+        return carry
+
+    lax.fori_loop(0, found, wait, 0)
+    picked = jnp.dot(select, held[...], preferred_element_type=jnp.float32)
+    x_ref[...] = picked.astype(jnp.bfloat16)
+
+
+def prepare_kernel(
+    cache_dev, after_ref, lengths_ref, frequency_ref, far_w_ref, rope_ref, limits_ref, w_ref, sem
+):
+    copy = pltpu.make_async_copy(far_w_ref, w_ref, sem)
+    copy.start()
+    rows = lengths_ref.shape[0]
     me = lax.axis_index("seq")
     near = LANES // (2 * SUB)
     sub = lax.broadcasted_iota(jnp.int32, (SUB, LANES), 0)
@@ -119,42 +139,26 @@
     first_half = lax.broadcasted_iota(jnp.int32, (block, LANES), 1) < LANES // 2
     rope_ref[:block] = jnp.where(turned, cosine, 1.0)
     rope_ref[block:] = jnp.where(turned, jnp.where(first_half, -sine, sine), 0.0)
-
-    row = lax.broadcasted_iota(jnp.int32, (tokens, 1), 0)
-    choice = jnp.full((tokens, 1), -1, jnp.int32)
-    for i in range(tokens):
-        step, r = i // rows, i % rows
-        choice = jnp.where(row == r // near * 2 * near + r % near * 2 + step, places[i], choice)
-    column = lax.broadcasted_iota(jnp.int32, (tokens, tokens * TILE), 1)
-    select = jnp.where(column == choice, 1.0, 0.0).astype(jnp.bfloat16)
-    def wait(i, carry):
-        pltpu.make_async_copy(table_ref.at[pl.ds(0, TILE)], held.at[pl.ds(0, TILE)], sem).wait()
-        return carry
-
-    lax.fori_loop(0, found, wait, 0)
-    picked = jnp.dot(select, held[...], preferred_element_type=jnp.float32)
-    x_ref[...] = picked.astype(jnp.bfloat16)
-
-
-def fetch_kernel(after_ref, far_ref, near_ref, sem):
-    copy = pltpu.make_async_copy(far_ref, near_ref, sem)
-    copy.start()
     copy.wait()
 
 
-def fetch(after, array):
+def prepare(after, lengths, frequency, w, cache_dev):
     return pl.pallas_call(
-        fetch_kernel,
-        out_shape=pltpu.VMEM(array.shape, array.dtype),
-        in_specs=[ANY] * 2,
-        out_specs=VMEM,
+        functools.partial(prepare_kernel, cache_dev),
+        out_shape=[
+            jax.ShapeDtypeStruct((2 * BLOCK, LANES), jnp.float32),
+            jax.ShapeDtypeStruct((SUB, LANES), jnp.int32),
+            pltpu.VMEM(w.shape, w.dtype),
+        ],
+        in_specs=[ANY, SMEM, VMEM, ANY],
+        out_specs=[VMEM] * 3,
         scratch_shapes=[pltpu.SemaphoreType.DMA],
         cost_estimate=pl.CostEstimate(
-            flops=0, bytes_accessed=2 * array.size * array.dtype.itemsize, transcendentals=0
+            flops=0, bytes_accessed=2 * w.size * w.dtype.itemsize, transcendentals=0
         ),
         compiler_params=pltpu.CompilerParams(vmem_limit_bytes=4 << 20),
-        name="fetch",
-    )(after, in_hbm(array))
+        name="prepare",
+    )(after, in_hbm(lengths), frequency, in_hbm(w))
 
 
 def project_kernel(x_ref, gain_ref, w_ref, out_ref):
@@ -337,28 +341,17 @@
     own = tokens // n_seq
     width = w_qkv.shape[2]
 
-    picked, rope, limits = pl.pallas_call(
-        functools.partial(pick_kernel, cache_dev),
-        out_shape=[
-            jax.ShapeDtypeStruct((tokens, feat), jnp.bfloat16),
-            jax.ShapeDtypeStruct((2 * BLOCK, LANES), jnp.float32),
-            jax.ShapeDtypeStruct((SUB, LANES), jnp.int32),
-        ],
-        in_specs=[SMEM, SMEM, VMEM, ANY],
-        out_specs=[VMEM] * 3,
-        scratch_shapes=[
-            pltpu.VMEM((tokens * TILE, feat), jnp.bfloat16),
-            pltpu.SemaphoreType.DMA,
-        ],
-        compiler_params=pltpu.CompilerParams(vmem_limit_bytes=8 << 20),
-        name="pick",
-    )(
-        in_hbm(token_ids),
-        in_hbm(lengths),
-        rope_frequency(head_dim),
-        in_hbm(embedding),
-    )
-    w_near = fetch(picked, w_qkv.reshape(feat, width))
+    picked = call(
+        pick_kernel,
+        "pick",
+        ((tokens, feat), jnp.bfloat16),
+        [SMEM, ANY],
+        [pltpu.VMEM((tokens * TILE, feat), jnp.bfloat16), pltpu.SemaphoreType.DMA],
+        8,
+    )(in_hbm(token_ids), in_hbm(embedding))
+    rope, limits, w_near = prepare(
+        picked, lengths, rope_frequency(head_dim), w_qkv.reshape(feat, width), cache_dev
+    )
     for mask in (1, 2, 6):
         picked = double(picked, "head", mask, n_head)
     gain = norm_gain.astype(jnp.float32).reshape(1, feat)

time: 81.8 us -> 81.6 us (level)
  starting transfers between devices: 19.2 us -> 18.2 us
    ppermute x6, starting transfers between devices: 19.2 us -> 18.2 us  [double(): return array + lax.ppermute(array, axis_name, pairs)]
  transfers between devices with their start and end apart: 6 -> 6, of which waited for: 6 -> 5; matrix products, arithmetic and copies ran while one was open for 0% -> 0% of each run, Pallas kernels for 2% -> 2%
where the time goes in v8:
time: 81.6 us; the launch traced here: 81.2 us
  blocking collectives  43.5 us (53%)
  starting transfers between devices  18.2 us (22%)
  waiting for transfers between devices  10.1 us (12%)
  Pallas kernels  8.6 us (11%)
    all_to_all x4, blocking collectives, swap(): return lax.all_to_all(array, axis_name, 0, 0, tiled=True)  43.5 us
    ppermute x6, starting transfers between devices, double(): return array + lax.ppermute(array, axis_name, pairs)  18.2 us
    ppermute x6, waiting for transfers between devices, double(): return array + lax.ppermute(array, axis_name, pairs)  10.1 us
    pallas_call x1, Pallas kernels, body(): call(attend_kernel, 'attend', ((n_seq, BLOCK, head_dim), jnp.float32), [V...  2.97 us
    pallas_call x1, Pallas kernels, body(): call(pick_kernel, 'pick', ((tokens, feat), jnp.bfloat16), [SMEM, ANY], [p...  2.49 us
    pallas_call x1, Pallas kernels, prepare(): pl.pallas_call(functools.partial(prepare_kernel, cache_dev), out_shape=[j...  1.99 us
  transfers between devices with their start and end apart: 6, of which 5 were waited for; matrix products, arithmetic and copies ran while one was open for 0% of the time, Pallas kernels for 2%

profile of v8, /device:TPU:1, one launch (start us, length us, event | category | flops | bytes accessed | tf_op | source)
XLA Modules:
  0.0 81.2 jit_solution(6221696737274149172)
XLA Ops:
  0.0 0.0 copy-start.3
  0.0 0.0 copy-start.1
  0.0 0.0 copy-start
  0.0 2.5 %pick.1.after_ref = bf16[48,512]{1,0:T(8,128)(2,1)S(1)} custom-call(s32[2,24]{1,0:T(2,128)} %ids_ref.1, bf16[8016,512]{1,0:T(8,128)(2,1)} %table_ref.1), custom_call_target="tpu_custom_call" | custom-call | tf_op jit(solution)/shard_map/pick/pallas_call | solution.py:344
  2.5 1.7 %collective-permute-start = (bf16[48,512]{1,0:T(8,128)(2,1)S(1)}, bf16[48,512]{1,0:T(8,128)(2,1)S(1)}, u32[]{:S(2)}, u32[]{:S(2)}) collective-permute-start(bf16[48,512]{1,0:T(8,128)(2,1)S(1)} %pick.1.after_ref), channel_id=1, source_target_pairs={{0,1},{1,0},{2,3},{3,2},{4,5},{5,4},{6,7},{7,6},{8,9},{9,8},{10,11... | collective-permute-start | bytes 147464 | tf_op jit(solution)/shard_map/ppermute | solution.py:333
  4.2 0.9 %collective-permute-done = bf16[48,512]{1,0:T(8,128)(2,1)S(1)} collective-permute-done((bf16[48,512]{1,0:T(8,128)(2,1)S(1)}, bf16[48,512]{1,0:T(8,128)(2,1)S(1)}, u32[]{:S(2)}, u32[]{:S(2)}) %collective-permute-start) | collective-permute-done | bytes 49184 | tf_op jit(solution)/shard_map/ppermute | solution.py:333
  5.1 1.7 %collective-permute-start.1 = (bf16[48,512]{1,0:T(8,128)(2,1)S(1)}, bf16[48,512]{1,0:T(8,128)(2,1)S(1)}, u32[]{:S(2)}, u32[]{:S(2)}) collective-permute-start(bf16[48,512]{1,0:T(8,128)(2,1)S(1)} %add.18), channel_id=1, source_target_pairs={{0,2},{1,3},{2,0},{3,1},{4,6},{5,7},{6,4},{7,5},{8,10},{9,11},{10,... | collective-permute-start | bytes 147464 | tf_op jit(solution)/shard_map/ppermute | solution.py:333
  6.8 1.5 %collective-permute-done.1 = bf16[48,512]{1,0:T(8,128)(2,1)S(1)} collective-permute-done((bf16[48,512]{1,0:T(8,128)(2,1)S(1)}, bf16[48,512]{1,0:T(8,128)(2,1)S(1)}, u32[]{:S(2)}, u32[]{:S(2)}) %collective-permute-start.1) | collective-permute-done | bytes 49184 | tf_op jit(solution)/shard_map/ppermute | solution.py:333
  8.3 3.7 %collective-permute-start.2 = (bf16[48,512]{1,0:T(8,128)(2,1)S(1)}, bf16[48,512]{1,0:T(8,128)(2,1)S(1)}, u32[]{:S(2)}, u32[]{:S(2)}) collective-permute-start(bf16[48,512]{1,0:T(8,128)(2,1)S(1)} %add.19), channel_id=1, source_target_pairs={{0,6},{1,7},{2,4},{3,5},{4,2},{5,3},{6,0},{7,1},{8,14},{9,15},{10,... | collective-permute-start | bytes 147464 | tf_op jit(solution)/shard_map/ppermute | solution.py:333
  12.0 0.1 maximum_bitcast_fusion.frequency_ref
  12.1 0.0 copy-done.3
  12.1 2.0 %prepare.1 = (f32[64,128]{1,0:T(8,128)S(1)}, s32[8,128]{1,0:T(8,128)S(1)}, bf16[512,1280]{1,0:T(8,128)(2,1)S(1)}) custom-call(bf16[48,512]{1,0:T(8,128)(2,1)S(1)} %pick.1.after_ref, s32[24]{0:T(128)} %lengths_ref.1, f32[1,128]{1,0:T(1,128)S(1)} %maximum_bitcast_fusion.frequency_ref, bf16[512,1280]{1,0:T(8,128)(2,1)} %bitcast.14), custom_call_target="tpu_custom_call" | custom-call | bytes 2621440 | tf_op jit(solution)/shard_map/prepare/pallas_call | solution.py:146
  14.1 0.0 collective-permute-done.2
  14.1 0.4 project.1
  14.5 14.1 %all_to_all.20.parts_ref = f32[16,32,128]{2,1,0:T(8,128)S(1)} all-to-all(f32[16,32,128]{2,1,0:T(8,128)S(1)} %bitcast.11), channel_id=1, replica_groups=mesh['seq'=16,'head'=8] {'seq'}, dimensions={0} | all-to-all | bytes 524288 | tf_op jit(solution)/shard_map/all_to_all | solution.py:47
  28.6 0.2 finish.1
  28.8 9.8 %all_to_all.21.rows_ref = bf16[16,32,128]{2,1,0:T(8,128)(2,1)S(1)} all-to-all(bf16[16,32,128]{2,1,0:T(8,128)(2,1)S(1)} %finish.1), channel_id=1, replica_groups=mesh['seq'=16,'head'=8] {'seq'}, dimensions={0} | all-to-all | bytes 262144 | tf_op jit(solution)/shard_map/all_to_all | solution.py:47
  38.6 0.0 copy-done.1
  38.6 0.0 copy-done
  38.6 0.0 copy-start.2
  38.6 3.0 %attend.1 = f32[16,32,128]{2,1,0:T(8,128)S(1)} custom-call(s32[8,128]{1,0:T(8,128)S(1)} %get-tuple-element.8.limits_ref, bf16[16,32,128]{2,1,0:T(8,128)(2,1)S(1)} %all_to_all.21.rows_ref, bf16[24,1024,128]{2,1,0:T(8,128)(2,1)S(1)} %bitcast.9, bf16[24,1024,128]{2,1,0:T(8,128)(2,1)S(1)} %bitcast.10), custom_call_target="tpu_custom_call" | custom-call | tf_op jit(solution)/shard_map/attend/pallas_call | solution.py:368
  41.6 10.3 %all_to_all.22.parts_ref = f32[16,32,128]{2,1,0:T(8,128)S(1)} all-to-all(f32[16,32,128]{2,1,0:T(8,128)S(1)} %attend.1), channel_id=1, replica_groups=mesh['seq'=16,'head'=8] {'seq'}, dimensions={0} | all-to-all | bytes 524288 | tf_op jit(solution)/shard_map/all_to_all | solution.py:47
  51.9 0.3 merge.1
  52.2 9.3 %all_to_all.23.attention_ref = bf16[16,8,384]{2,1,0:T(8,128)(2,1)S(1)} all-to-all(bf16[16,8,384]{2,1,0:T(8,128)(2,1)S(1)} %merge.1), channel_id=1, replica_groups=mesh['seq'=16,'head'=8] {'seq'}, dimensions={0} | all-to-all | bytes 196608 | tf_op jit(solution)/shard_map/all_to_all | solution.py:47
  61.5 0.0 copy-done.2
  61.5 0.3 output.1
  61.8 0.0 collective-permute-start.3
  61.8 3.8 %collective-permute-done.3 = f32[48,512]{1,0:T(8,128)S(1)} collective-permute-done((f32[48,512]{1,0:T(8,128)S(1)}, f32[48,512]{1,0:T(8,128)S(1)}, u32[]{:S(2)}, u32[]{:S(2)}) %collective-permute-start.3) | collective-permute-done | bytes 98336 | tf_op jit(solution)/shard_map/ppermute | solution.py:333
  65.6 1.7 %collective-permute-start.4 = (f32[48,512]{1,0:T(8,128)S(1)}, f32[48,512]{1,0:T(8,128)S(1)}, u32[]{:S(2)}, u32[]{:S(2)}) collective-permute-start(f32[48,512]{1,0:T(8,128)S(1)} %add.21), channel_id=1, source_target_pairs={{0,6},{1,7},{2,4},{3,5},{4,2},{5,3},{6,0},{7,1},{8,14},{9,15},{10,... | collective-permute-start | bytes 294920 | tf_op jit(solution)/shard_map/ppermute | solution.py:333
  67.3 3.0 %collective-permute-done.4 = f32[48,512]{1,0:T(8,128)S(1)} collective-permute-done((f32[48,512]{1,0:T(8,128)S(1)}, f32[48,512]{1,0:T(8,128)S(1)}, u32[]{:S(2)}, u32[]{:S(2)}) %collective-permute-start.4) | collective-permute-done | bytes 98336 | tf_op jit(solution)/shard_map/ppermute | solution.py:333
  70.4 9.3 %collective-permute-start.5 = (f32[48,512]{1,0:T(8,128)S(1)}, f32[48,512]{1,0:T(8,128)S(1)}, u32[]{:S(2)}, u32[]{:S(2)}) collective-permute-start(f32[48,512]{1,0:T(8,128)S(1)} %add.22), channel_id=1, source_target_pairs={{0,1},{1,0},{2,3},{3,2},{4,5},{5,4},{6,7},{7,6},{8,9},{9,8},{10,11... | collective-permute-start | bytes 294920 | tf_op jit(solution)/shard_map/ppermute | solution.py:333
  79.6 0.9 %collective-permute-done.5 = f32[48,512]{1,0:T(8,128)S(1)} collective-permute-done((f32[48,512]{1,0:T(8,128)S(1)}, f32[48,512]{1,0:T(8,128)S(1)}, u32[]{:S(2)}, u32[]{:S(2)}) %collective-permute-start.5) | collective-permute-done | bytes 98336 | tf_op jit(solution)/shard_map/ppermute | solution.py:333
  80.6 0.6 add_convert_fusion
  (7 shorter events, 0.1 us)
Async XLA Ops:
  0.0 12.1 %copy-start.3 = (bf16[512]{0:T(512)(128)(2,1)S(1)}, bf16[512]{0:T(512)(128)(2,1)}, u32[]{:S(2)}) copy-start(bf16[512]{0:T(512)(128)(2,1)} %param.11) | copy-start | bytes 3076
  0.0 38.6 %copy-start.1 = (bf16[24,1,1024,128]{3,2,1,0:T(8,128)(2,1)S(1)}, bf16[24,1,1024,128]{3,2,1,0:T(8,128)(2,1)}, u32[]{:S(2)}) copy-start(bf16[24,1,1024,128]{3,2,1,0:T(8,128)(2,1)} %param.14) | copy-start | bytes 18874372
  0.0 38.6 %copy-start = (bf16[24,1,1024,128]{3,2,1,0:T(8,128)(2,1)S(1)}, bf16[24,1,1024,128]{3,2,1,0:T(8,128)(2,1)}, u32[]{:S(2)}) copy-start(bf16[24,1,1024,128]{3,2,1,0:T(8,128)(2,1)} %param.13) | copy-start | bytes 18874372
  2.5 2.6 %collective-permute-start = (bf16[48,512]{1,0:T(8,128)(2,1)S(1)}, bf16[48,512]{1,0:T(8,128)(2,1)S(1)}, u32[]{:S(2)}, u32[]{:S(2)}) collective-permute-start(bf16[48,512]{1,0:T(8,128)(2,1)S(1)} %pick.1.after_ref), channel_id=1, source_target_pairs={{0,1},{1,0},{2,3},{3,2},{4,5},{5,4},{6,7},{7,6},{8,9},{9,8},{10,11... | collective-permute-start | bytes 147464 | tf_op jit(solution)/shard_map/ppermute | solution.py:333
  5.1 3.2 %collective-permute-start.1 = (bf16[48,512]{1,0:T(8,128)(2,1)S(1)}, bf16[48,512]{1,0:T(8,128)(2,1)S(1)}, u32[]{:S(2)}, u32[]{:S(2)}) collective-permute-start(bf16[48,512]{1,0:T(8,128)(2,1)S(1)} %add.18), channel_id=1, source_target_pairs={{0,2},{1,3},{2,0},{3,1},{4,6},{5,7},{6,4},{7,5},{8,10},{9,11},{10,... | collective-permute-start | bytes 147464 | tf_op jit(solution)/shard_map/ppermute | solution.py:333
  8.3 5.8 %collective-permute-start.2 = (bf16[48,512]{1,0:T(8,128)(2,1)S(1)}, bf16[48,512]{1,0:T(8,128)(2,1)S(1)}, u32[]{:S(2)}, u32[]{:S(2)}) collective-permute-start(bf16[48,512]{1,0:T(8,128)(2,1)S(1)} %add.19), channel_id=1, source_target_pairs={{0,6},{1,7},{2,4},{3,5},{4,2},{5,3},{6,0},{7,1},{8,14},{9,15},{10,... | collective-permute-start | bytes 147464 | tf_op jit(solution)/shard_map/ppermute | solution.py:333
  38.6 22.9 %copy-start.2 = (bf16[1,1024,512]{2,1,0:T(8,128)(2,1)S(1)}, bf16[1,1024,512]{2,1,0:T(8,128)(2,1)}, u32[]{:S(2)}) copy-start(bf16[1,1024,512]{2,1,0:T(8,128)(2,1)} %param.15) | copy-start | bytes 3145732
  61.8 3.8 %collective-permute-start.3 = (f32[48,512]{1,0:T(8,128)S(1)}, f32[48,512]{1,0:T(8,128)S(1)}, u32[]{:S(2)}, u32[]{:S(2)}) collective-permute-start(f32[48,512]{1,0:T(8,128)S(1)} %output.1), channel_id=1, source_target_pairs={{0,2},{1,3},{2,0},{3,1},{4,6},{5,7},{6,4},{7,5},{8,10},{9,11},{10,... | collective-permute-start | bytes 294920 | tf_op jit(solution)/shard_map/ppermute | solution.py:333
  65.6 4.8 %collective-permute-start.4 = (f32[48,512]{1,0:T(8,128)S(1)}, f32[48,512]{1,0:T(8,128)S(1)}, u32[]{:S(2)}, u32[]{:S(2)}) collective-permute-start(f32[48,512]{1,0:T(8,128)S(1)} %add.21), channel_id=1, source_target_pairs={{0,6},{1,7},{2,4},{3,5},{4,2},{5,3},{6,0},{7,1},{8,14},{9,15},{10,... | collective-permute-start | bytes 294920 | tf_op jit(solution)/shard_map/ppermute | solution.py:333
  70.4 10.2 %collective-permute-start.5 = (f32[48,512]{1,0:T(8,128)S(1)}, f32[48,512]{1,0:T(8,128)S(1)}, u32[]{:S(2)}, u32[]{:S(2)}) collective-permute-start(f32[48,512]{1,0:T(8,128)S(1)} %add.22), channel_id=1, source_target_pairs={{0,1},{1,0},{2,3},{3,2},{4,5},{5,4},{6,7},{7,6},{8,9},{9,8},{10,11... | collective-permute-start | bytes 294920 | tf_op jit(solution)/shard_map/ppermute | solution.py:333

commit v9 on v7

--- a/solution.py
+++ b/solution.py
@@ -197,7 +197,9 @@
         out_ref[j] = turned
 
 
-def attend_kernel(limits_ref, rows_ref, k_ref, v_ref, out_ref, scores_ref):
+def attend_kernel(
+    limits_ref, rows_ref, k_ref, v_ref, out_ref, scores_ref, held_ref, stats_ref
+):
     row_count, cache_dev, head_dim = k_ref.shape
     count = rows_ref.shape[0]
     per_row = 2 * SUB
@@ -208,18 +210,20 @@
     lane = lax.broadcasted_iota(jnp.int32, (1, LANES), 1)
     position = lax.broadcasted_iota(jnp.int32, (chunk, LANES), 0)
     slot = lax.broadcasted_iota(jnp.int32, (LANES, LANES), 0)
-    rows = rows_ref[...].astype(jnp.float32)
-    new_keys = rows[:, groups * SUB :].reshape(count * SUB, head_dim)
+    held_ref[...] = rows_ref[...].astype(jnp.float32)
+    new_keys = held_ref[:, groups * SUB :].reshape(count * SUB, head_dim)
     new_values = pltpu.roll(new_keys, LANES - groups, 0).astype(jnp.bfloat16)
     new_keys = new_keys.astype(jnp.bfloat16)
-
-    def score(g):
-        turned = rows[:, g * SUB : (g + 1) * SUB].reshape(count * SUB, head_dim).T
+    stats_ref[...] = jnp.zeros_like(stats_ref)
+
+    def attend_group(g, carry):
+        own_rows = pl.ds(pl.multiple_of(g * SUB, SUB), SUB)
+        turned = held_ref[:, own_rows].reshape(count * SUB, head_dim).T
         blocks = [
             jnp.where(lane // per_row == r, turned, 0.0).astype(jnp.bfloat16) for r in range(near)
         ]
         weights = jnp.concatenate(blocks, axis=0)
-        limit = limits_ref[g : g + 1]
+        limit = limits_ref[pl.ds(g, 1)]
         fresh = jnp.dot(new_keys, turned.astype(jnp.bfloat16), preferred_element_type=jnp.float32)
         seen = (
             (slot % SUB == g)
@@ -235,16 +239,13 @@
             )
             scores = jnp.dot(keys, weights, preferred_element_type=jnp.float32)
             scores = jnp.where(position < limit - c * chunk, scores, negative)
-            scores_ref[g, pl.ds(c * chunk, chunk)] = scores
+            scores_ref[pl.ds(c * chunk, chunk)] = scores
             top = jnp.maximum(top, jnp.max(scores, axis=0, keepdims=True))
-        return top, fresh
-
-    def weigh(g, top, fresh):
         fresh = jnp.exp(fresh - top)
         total = jnp.sum(fresh, axis=0, keepdims=True)
         parts = []
         for c in range(cache_dev // chunk):
-            weight = jnp.exp(scores_ref[g, pl.ds(c * chunk, chunk)] - top)
+            weight = jnp.exp(scores_ref[pl.ds(c * chunk, chunk)] - top)
             total = total + jnp.sum(weight, axis=0, keepdims=True)
             parts.append(weight.astype(jnp.bfloat16).T)
         parts = jnp.concatenate(parts, axis=1)
@@ -260,18 +261,13 @@
             axis=0,
         ) + jnp.dot(fresh.T.astype(jnp.bfloat16), new_values, preferred_element_type=jnp.float32)
         for j in range(count):
-            out_ref[j, pl.ds(g * SUB, SUB)] = value[j * SUB : (j + 1) * SUB]
-        return total
-
-    tops, totals = [], []
-    ready = score(0)
-    for g in range(groups):
-        later = score(g + 1) if g + 1 < groups else None
-        tops.append(ready[0])
-        totals.append(weigh(g, *ready))
-        ready = later
-    spare = jnp.zeros((SUB - 2 * groups, LANES), jnp.float32)
-    stats = jnp.concatenate(tops + totals + [spare], axis=0)
+            out_ref[j, own_rows] = value[j * SUB : (j + 1) * SUB]
+        stats_ref[pl.ds(g, 1)] = top
+        stats_ref[pl.ds(groups + g, 1)] = total
+        return carry
+
+    lax.fori_loop(0, groups, attend_group, 0)
+    stats = stats_ref[...]
     for j in range(count):
         turn = (LANES - SUB * j) % LANES
         out_ref[j, pl.ds(groups * SUB, SUB)] = pltpu.roll(stats, turn, 1) if turn else stats
@@ -377,7 +373,11 @@
         "attend",
         ((n_seq, BLOCK, head_dim), jnp.float32),
         [VMEM] * 4,
-        [pltpu.VMEM((own, cache_dev, LANES), jnp.float32)],
+        [
+            pltpu.VMEM((cache_dev, LANES), jnp.float32),
+            pltpu.VMEM((n_seq, BLOCK, head_dim), jnp.float32),
+            pltpu.VMEM((SUB, LANES), jnp.float32),
+        ],
         8,
     )(limits, rows, in_vmem(k_cache[:, 0]), in_vmem(v_cache[:, 0]))
     partial = swap(partial, "seq")

time: 81.8 us -> 83 us (1.015)
  Pallas kernels: 8.1 us -> 9.05 us
    pallas_call x1, Pallas kernels: 2.97 us -> 4.23 us  [body(): call(attend_kernel, 'attend', ((n_seq, BLOCK, head_dim), jnp.float32), [V...]
where the time goes in v9:
time: 83 us; the launch traced here: 82.7 us
  blocking collectives  43.5 us (52%)
  starting transfers between devices  19.6 us (24%)
  waiting for transfers between devices  9.6 us (12%)
  Pallas kernels  9.05 us (11%)
    all_to_all x4, blocking collectives, swap(): return lax.all_to_all(array, axis_name, 0, 0, tiled=True)  43.5 us
    ppermute x6, starting transfers between devices, double(): return array + lax.ppermute(array, axis_name, pairs)  19.6 us
    ppermute x6, waiting for transfers between devices, double(): return array + lax.ppermute(array, axis_name, pairs)  9.6 us
    pallas_call x1, Pallas kernels, body(): call(attend_kernel, 'attend', ((n_seq, BLOCK, head_dim), jnp.float32), [V...  4.23 us
    pallas_call x1, Pallas kernels, body(): pl.pallas_call(functools.partial(pick_kernel, cache_dev), out_shape=[jax....  2.33 us
  transfers between devices with their start and end apart: 6, of which 6 were waited for; matrix products, arithmetic and copies ran while one was open for 0% of the time, Pallas kernels for 2%

profile of v9, /device:TPU:1, one launch (start us, length us, event | category | flops | bytes accessed | tf_op | source)
XLA Modules:
  0.0 82.7 jit_solution(4082291430795308717)
XLA Ops:
  0.0 0.0 copy-start.2
  0.0 0.0 slice-start
  0.0 0.1 maximum_bitcast_fusion.frequency_ref
  0.1 0.0 slice-start.1
  0.1 0.0 copy-start
  0.1 2.3 %pick.1 = (bf16[48,512]{1,0:T(8,128)(2,1)S(1)}, f32[64,128]{1,0:T(8,128)S(1)}, s32[8,128]{1,0:T(8,128)S(1)}) custom-call(s32[2,24]{1,0:T(2,128)} %ids_ref.1, s32[24]{0:T(128)} %lengths_ref.1, f32[1,128]{1,0:T(1,128)S(1)} %maximum_bitcast_fusion.frequency_ref, bf16[8016,512]{1,0:T(8,128)(2,1)} %table_ref.1), custom_call_target="tpu_custom_call" | custom-call | tf_op jit(solution)/shard_map/pick/pallas_call | solution.py:336
  2.4 1.9 %collective-permute-start = (bf16[48,512]{1,0:T(8,128)(2,1)S(1)}, bf16[48,512]{1,0:T(8,128)(2,1)S(1)}, u32[]{:S(2)}, u32[]{:S(2)}) collective-permute-start(bf16[48,512]{1,0:T(8,128)(2,1)S(1)} %get-tuple-element.9.after_ref), channel_id=1, source_target_pairs={{0,1},{1,0},{2,3},{3,2},{4,5},{5,4},{6,7},{7,6},{8,9},{9,8},{10,11... | collective-permute-start | bytes 147464 | tf_op jit(solution)/shard_map/ppermute | solution.py:325
  4.3 0.9 %collective-permute-done = bf16[48,512]{1,0:T(8,128)(2,1)S(1)} collective-permute-done((bf16[48,512]{1,0:T(8,128)(2,1)S(1)}, bf16[48,512]{1,0:T(8,128)(2,1)S(1)}, u32[]{:S(2)}, u32[]{:S(2)}) %collective-permute-start) | collective-permute-done | bytes 49184 | tf_op jit(solution)/shard_map/ppermute | solution.py:325
  5.2 1.7 %collective-permute-start.1 = (bf16[48,512]{1,0:T(8,128)(2,1)S(1)}, bf16[48,512]{1,0:T(8,128)(2,1)S(1)}, u32[]{:S(2)}, u32[]{:S(2)}) collective-permute-start(bf16[48,512]{1,0:T(8,128)(2,1)S(1)} %add.18), channel_id=1, source_target_pairs={{0,2},{1,3},{2,0},{3,1},{4,6},{5,7},{6,4},{7,5},{8,10},{9,11},{10,... | collective-permute-start | bytes 147464 | tf_op jit(solution)/shard_map/ppermute | solution.py:325
  7.0 1.5 %collective-permute-done.1 = bf16[48,512]{1,0:T(8,128)(2,1)S(1)} collective-permute-done((bf16[48,512]{1,0:T(8,128)(2,1)S(1)}, bf16[48,512]{1,0:T(8,128)(2,1)S(1)}, u32[]{:S(2)}, u32[]{:S(2)}) %collective-permute-start.1) | collective-permute-done | bytes 49184 | tf_op jit(solution)/shard_map/ppermute | solution.py:325
  8.5 3.7 %collective-permute-start.2 = (bf16[48,512]{1,0:T(8,128)(2,1)S(1)}, bf16[48,512]{1,0:T(8,128)(2,1)S(1)}, u32[]{:S(2)}, u32[]{:S(2)}) collective-permute-start(bf16[48,512]{1,0:T(8,128)(2,1)S(1)} %add.19), channel_id=1, source_target_pairs={{0,6},{1,7},{2,4},{3,5},{4,2},{5,3},{6,0},{7,1},{8,14},{9,15},{10,... | collective-permute-start | bytes 147464 | tf_op jit(solution)/shard_map/ppermute | solution.py:325
  12.2 0.0 copy-done.2
  12.2 1.3 %fetch.1.w_ref = bf16[512,1280]{1,0:T(8,128)(2,1)S(1)} custom-call(bf16[48,512]{1,0:T(8,128)(2,1)S(1)} %get-tuple-element.9.after_ref, bf16[512,1280]{1,0:T(8,128)(2,1)} %bitcast.16), custom_call_target="tpu_custom_call" | custom-call | bytes 2621440 | tf_op jit(solution)/shard_map/fetch/pallas_call | solution.py:146
  13.6 0.1 collective-permute-done.2
  13.7 0.4 project.1
  14.1 14.2 %all_to_all.20.parts_ref = f32[16,32,128]{2,1,0:T(8,128)S(1)} all-to-all(f32[16,32,128]{2,1,0:T(8,128)S(1)} %bitcast.13), channel_id=1, replica_groups=mesh['seq'=16,'head'=8] {'seq'}, dimensions={0} | all-to-all | bytes 524288 | tf_op jit(solution)/shard_map/all_to_all | solution.py:47
  28.3 0.2 finish.1
  28.5 9.6 %all_to_all.21.rows_ref = bf16[16,32,128]{2,1,0:T(8,128)(2,1)S(1)} all-to-all(bf16[16,32,128]{2,1,0:T(8,128)(2,1)S(1)} %finish.1), channel_id=1, replica_groups=mesh['seq'=16,'head'=8] {'seq'}, dimensions={0} | all-to-all | bytes 262144 | tf_op jit(solution)/shard_map/all_to_all | solution.py:47
  38.2 0.0 slice-done
  38.2 0.0 slice-done.1
  38.2 0.0 copy-done
  38.2 0.0 copy-start.1
  38.2 4.2 %attend.1 = f32[16,32,128]{2,1,0:T(8,128)S(1)} custom-call(s32[8,128]{1,0:T(8,128)S(1)} %get-tuple-element.8.limits_ref, bf16[16,32,128]{2,1,0:T(8,128)(2,1)S(1)} %all_to_all.21.rows_ref, bf16[24,1024,128]{2,1,0:T(8,128)(2,1)S(1)} %bitcast.11, bf16[24,1024,128]{2,1,0:T(8,128)(2,1)S(1)} %bitcast.12), custom_call_target="tpu_custom_call" | custom-call | tf_op jit(solution)/shard_map/attend/pallas_call | solution.py:371
  42.5 10.3 %all_to_all.22.parts_ref = f32[16,32,128]{2,1,0:T(8,128)S(1)} all-to-all(f32[16,32,128]{2,1,0:T(8,128)S(1)} %attend.1), channel_id=1, replica_groups=mesh['seq'=16,'head'=8] {'seq'}, dimensions={0} | all-to-all | bytes 524288 | tf_op jit(solution)/shard_map/all_to_all | solution.py:47
  52.8 0.3 merge.1
  53.1 9.3 %all_to_all.23.attention_ref = bf16[16,8,384]{2,1,0:T(8,128)(2,1)S(1)} all-to-all(bf16[16,8,384]{2,1,0:T(8,128)(2,1)S(1)} %merge.1), channel_id=1, replica_groups=mesh['seq'=16,'head'=8] {'seq'}, dimensions={0} | all-to-all | bytes 196608 | tf_op jit(solution)/shard_map/all_to_all | solution.py:47
  62.4 0.0 copy-done.1
  62.4 0.3 output.1
  62.6 0.0 collective-permute-start.3
  62.7 3.8 %collective-permute-done.3 = f32[48,512]{1,0:T(8,128)S(1)} collective-permute-done((f32[48,512]{1,0:T(8,128)S(1)}, f32[48,512]{1,0:T(8,128)S(1)}, u32[]{:S(2)}, u32[]{:S(2)}) %collective-permute-start.3) | collective-permute-done | bytes 98336 | tf_op jit(solution)/shard_map/ppermute | solution.py:325
  66.4 2.4 %collective-permute-start.4 = (f32[48,512]{1,0:T(8,128)S(1)}, f32[48,512]{1,0:T(8,128)S(1)}, u32[]{:S(2)}, u32[]{:S(2)}) collective-permute-start(f32[48,512]{1,0:T(8,128)S(1)} %add.21), channel_id=1, source_target_pairs={{0,6},{1,7},{2,4},{3,5},{4,2},{5,3},{6,0},{7,1},{8,14},{9,15},{10,... | collective-permute-start | bytes 294920 | tf_op jit(solution)/shard_map/ppermute | solution.py:325
  68.8 2.4 %collective-permute-done.4 = f32[48,512]{1,0:T(8,128)S(1)} collective-permute-done((f32[48,512]{1,0:T(8,128)S(1)}, f32[48,512]{1,0:T(8,128)S(1)}, u32[]{:S(2)}, u32[]{:S(2)}) %collective-permute-start.4) | collective-permute-done | bytes 98336 | tf_op jit(solution)/shard_map/ppermute | solution.py:325
  71.2 9.9 %collective-permute-start.5 = (f32[48,512]{1,0:T(8,128)S(1)}, f32[48,512]{1,0:T(8,128)S(1)}, u32[]{:S(2)}, u32[]{:S(2)}) collective-permute-start(f32[48,512]{1,0:T(8,128)S(1)} %add.22), channel_id=1, source_target_pairs={{0,1},{1,0},{2,3},{3,2},{4,5},{5,4},{6,7},{7,6},{8,9},{9,8},{10,11... | collective-permute-start | bytes 294920 | tf_op jit(solution)/shard_map/ppermute | solution.py:325
  81.1 0.9 %collective-permute-done.5 = f32[48,512]{1,0:T(8,128)S(1)} collective-permute-done((f32[48,512]{1,0:T(8,128)S(1)}, f32[48,512]{1,0:T(8,128)S(1)}, u32[]{:S(2)}, u32[]{:S(2)}) %collective-permute-start.5) | collective-permute-done | bytes 98336 | tf_op jit(solution)/shard_map/ppermute | solution.py:325
  82.0 0.6 add_convert_fusion
  (8 shorter events, 0.1 us)
Async XLA Ops:
  0.0 12.2 %copy-start.2 = (bf16[512]{0:T(512)(128)(2,1)S(1)}, bf16[512]{0:T(512)(128)(2,1)}, u32[]{:S(2)}) copy-start(bf16[512]{0:T(512)(128)(2,1)} %param.11) | copy-start | bytes 3076
  0.0 38.2 %slice-start = ((s8[6291456]{0:T(1024)(128)(4,1)}), s8[4194304]{0:T(1024)(128)(4,1)S(1)}, s32[]{:S(2)}) async-start(s8[6291456]{0:T(1024)(128)(4,1)} %bitcast.9), calls=%async_computation.4 | async-start | bytes 8388608
  0.1 38.1 %slice-start.1 = ((s8[6291456]{0:T(1024)(128)(4,1)}), s8[2097152]{0:T(1024)(128)(4,1)S(1)}, s32[]{:S(2)}) async-start(s8[6291456]{0:T(1024)(128)(4,1)} %bitcast.9), calls=%async_computation.5 | async-start | bytes 4194304
  0.1 38.1 %copy-start = (bf16[24,1,1024,128]{3,2,1,0:T(8,128)(2,1)S(1)}, bf16[24,1,1024,128]{3,2,1,0:T(8,128)(2,1)}, u32[]{:S(2)}) copy-start(bf16[24,1,1024,128]{3,2,1,0:T(8,128)(2,1)} %param.14) | copy-start | bytes 18874372
  2.4 2.8 %collective-permute-start = (bf16[48,512]{1,0:T(8,128)(2,1)S(1)}, bf16[48,512]{1,0:T(8,128)(2,1)S(1)}, u32[]{:S(2)}, u32[]{:S(2)}) collective-permute-start(bf16[48,512]{1,0:T(8,128)(2,1)S(1)} %get-tuple-element.9.after_ref), channel_id=1, source_target_pairs={{0,1},{1,0},{2,3},{3,2},{4,5},{5,4},{6,7},{7,6},{8,9},{9,8},{10,11... | collective-permute-start | bytes 147464 | tf_op jit(solution)/shard_map/ppermute | solution.py:325
  5.2 3.2 %collective-permute-start.1 = (bf16[48,512]{1,0:T(8,128)(2,1)S(1)}, bf16[48,512]{1,0:T(8,128)(2,1)S(1)}, u32[]{:S(2)}, u32[]{:S(2)}) collective-permute-start(bf16[48,512]{1,0:T(8,128)(2,1)S(1)} %add.18), channel_id=1, source_target_pairs={{0,2},{1,3},{2,0},{3,1},{4,6},{5,7},{6,4},{7,5},{8,10},{9,11},{10,... | collective-permute-start | bytes 147464 | tf_op jit(solution)/shard_map/ppermute | solution.py:325
  8.5 5.2 %collective-permute-start.2 = (bf16[48,512]{1,0:T(8,128)(2,1)S(1)}, bf16[48,512]{1,0:T(8,128)(2,1)S(1)}, u32[]{:S(2)}, u32[]{:S(2)}) collective-permute-start(bf16[48,512]{1,0:T(8,128)(2,1)S(1)} %add.19), channel_id=1, source_target_pairs={{0,6},{1,7},{2,4},{3,5},{4,2},{5,3},{6,0},{7,1},{8,14},{9,15},{10,... | collective-permute-start | bytes 147464 | tf_op jit(solution)/shard_map/ppermute | solution.py:325
  38.2 24.2 %copy-start.1 = (bf16[1,1024,512]{2,1,0:T(8,128)(2,1)S(1)}, bf16[1,1024,512]{2,1,0:T(8,128)(2,1)}, u32[]{:S(2)}) copy-start(bf16[1,1024,512]{2,1,0:T(8,128)(2,1)} %param.15) | copy-start | bytes 3145732
  62.6 3.8 %collective-permute-start.3 = (f32[48,512]{1,0:T(8,128)S(1)}, f32[48,512]{1,0:T(8,128)S(1)}, u32[]{:S(2)}, u32[]{:S(2)}) collective-permute-start(f32[48,512]{1,0:T(8,128)S(1)} %output.1), channel_id=1, source_target_pairs={{0,2},{1,3},{2,0},{3,1},{4,6},{5,7},{6,4},{7,5},{8,10},{9,11},{10,... | collective-permute-start | bytes 294920 | tf_op jit(solution)/shard_map/ppermute | solution.py:325
  66.4 4.8 %collective-permute-start.4 = (f32[48,512]{1,0:T(8,128)S(1)}, f32[48,512]{1,0:T(8,128)S(1)}, u32[]{:S(2)}, u32[]{:S(2)}) collective-permute-start(f32[48,512]{1,0:T(8,128)S(1)} %add.21), channel_id=1, source_target_pairs={{0,6},{1,7},{2,4},{3,5},{4,2},{5,3},{6,0},{7,1},{8,14},{9,15},{10,... | collective-permute-start | bytes 294920 | tf_op jit(solution)/shard_map/ppermute | solution.py:325
  71.2 10.8 %collective-permute-start.5 = (f32[48,512]{1,0:T(8,128)S(1)}, f32[48,512]{1,0:T(8,128)S(1)}, u32[]{:S(2)}, u32[]{:S(2)}) collective-permute-start(f32[48,512]{1,0:T(8,128)S(1)} %add.22), channel_id=1, source_target_pairs={{0,1},{1,0},{2,3},{3,2},{4,5},{5,4},{6,7},{7,6},{8,9},{9,8},{10,11... | collective-permute-start | bytes 294920 | tf_op jit(solution)/shard_map/ppermute | solution.py:325

commit v10 on v7

--- a/solution.py
+++ b/solution.py
@@ -13,6 +13,7 @@
 SUB = 8
 BLOCK = 32
 SPAN = 32
+HALF = 4
 
 rope_base = 500000.0
 epsilon = 1e-05
@@ -260,7 +261,9 @@
             axis=0,
         ) + jnp.dot(fresh.T.astype(jnp.bfloat16), new_values, preferred_element_type=jnp.float32)
         for j in range(count):
-            out_ref[j, pl.ds(g * SUB, SUB)] = value[j * SUB : (j + 1) * SUB]
+            for h in range(2):
+                start = j * SUB + h * HALF
+                out_ref[j, 2 * g + h] = value[start : start + HALF]
         return total
 
     tops, totals = [], []
@@ -270,31 +273,39 @@
         tops.append(ready[0])
         totals.append(weigh(g, *ready))
         ready = later
-    spare = jnp.zeros((SUB - 2 * groups, LANES), jnp.float32)
-    stats = jnp.concatenate(tops + totals + [spare], axis=0)
+    spare = jnp.zeros((SUB - groups, LANES), jnp.float32)
+    tops = jnp.concatenate(tops + [spare], axis=0)
+    totals = pltpu.roll(jnp.concatenate(totals + [spare], axis=0), SUB, 1)
     for j in range(count):
         turn = (LANES - SUB * j) % LANES
-        out_ref[j, pl.ds(groups * SUB, SUB)] = pltpu.roll(stats, turn, 1) if turn else stats
+        both = jnp.where(
+            lane < SUB,
+            pltpu.roll(tops, turn, 1) if turn else tops,
+            pltpu.roll(totals, turn, 1) if turn else totals,
+        )
+        out_ref[j, 2 * groups] = both[:HALF]
 
 
 def merge_kernel(parts_ref, out_ref):
-    count, rows, head_dim = parts_ref.shape
-    groups = rows // SUB - 1
-    stats = parts_ref[:, groups * SUB :]
+    count, pieces, _, head_dim = parts_ref.shape
+    groups = pieces // 2
+    stats = [parts_ref[j, 2 * groups] for j in range(count)]
     top = stats[0]
     for j in range(1, count):
         top = jnp.maximum(top, stats[j])
-    factors = [jnp.exp(stats[j] - top) for j in range(count)]
-    denominator = factors[0] * pltpu.roll(stats[0], SUB - groups, 0)
-    for j in range(1, count):
-        denominator = denominator + factors[j] * pltpu.roll(stats[j], SUB - groups, 0)
-    shares = jnp.concatenate([factor / denominator for factor in factors], axis=0).T[:SUB]
+    factors = [jnp.exp(jnp.minimum(stats[j] - top, 0.0)) for j in range(count)]
+    denominator = jnp.zeros((HALF, head_dim), jnp.float32)
+    for j in range(count):
+        denominator = denominator + factors[j] * pltpu.roll(stats[j], head_dim - SUB, 1)
+    shares = jnp.concatenate([factor / denominator for factor in factors], axis=0)
+    shares = jnp.concatenate([shares, jnp.zeros_like(shares)], axis=0).T[:SUB]
     merged = []
     for g in range(groups):
         total = jnp.zeros((SUB, head_dim), jnp.float32)
         for j in range(count):
-            column = j * SUB + g
-            total = total + parts_ref[j, pl.ds(g * SUB, SUB)] * shares[:, column : column + 1]
+            column = j * HALF + g
+            part = jnp.concatenate([parts_ref[j, 2 * g], parts_ref[j, 2 * g + 1]], axis=0)
+            total = total + part * shares[:, column : column + 1]
         merged.append(total)
     merged = jnp.concatenate(merged, axis=1).astype(jnp.bfloat16)
     for j in range(out_ref.shape[0]):
@@ -375,7 +386,7 @@
     partial = call(
         attend_kernel,
         "attend",
-        ((n_seq, BLOCK, head_dim), jnp.float32),
+        ((n_seq, 2 * own + 1, HALF, head_dim), jnp.float32),
         [VMEM] * 4,
         [pltpu.VMEM((own, cache_dev, LANES), jnp.float32)],
         8,

time: 81.8 us -> 81.6 us (level)
  no operation moved by 1% of the time
where the time goes in v10:
time: 81.6 us; the launch traced here: 81.1 us
  blocking collectives  43.3 us (53%)
  starting transfers between devices  19.1 us (23%)
  waiting for transfers between devices  9.58 us (12%)
  Pallas kernels  8.18 us (10%)
    all_to_all x4, blocking collectives, swap(): return lax.all_to_all(array, axis_name, 0, 0, tiled=True)  43.3 us
    ppermute x6, starting transfers between devices, double(): return array + lax.ppermute(array, axis_name, pairs)  19.1 us
    ppermute x6, waiting for transfers between devices, double(): return array + lax.ppermute(array, axis_name, pairs)  9.58 us
    pallas_call x1, Pallas kernels, body(): call(attend_kernel, 'attend', ((n_seq, 2 * own + 1, HALF, head_dim), jnp....  2.98 us
    pallas_call x1, Pallas kernels, body(): pl.pallas_call(functools.partial(pick_kernel, cache_dev), out_shape=[jax....  2.67 us
  transfers between devices with their start and end apart: 6, of which 6 were waited for; matrix products, arithmetic and copies ran while one was open for 0% of the time, Pallas kernels for 2%

profile of v10, /device:TPU:1, one launch (start us, length us, event | category | flops | bytes accessed | tf_op | source)
XLA Modules:
  0.0 81.1 jit_solution(1691695001841628622)
XLA Ops:
  0.0 0.0 copy-start.2
  0.0 0.0 slice-start
  0.0 0.1 maximum_bitcast_fusion.frequency_ref
  0.1 0.0 slice-start.1
  0.1 0.0 copy-start
  0.1 2.7 %pick.1 = (bf16[48,512]{1,0:T(8,128)(2,1)S(1)}, f32[64,128]{1,0:T(8,128)S(1)}, s32[8,128]{1,0:T(8,128)S(1)}) custom-call(s32[2,24]{1,0:T(2,128)} %ids_ref.1, s32[24]{0:T(128)} %lengths_ref.1, f32[1,128]{1,0:T(1,128)S(1)} %maximum_bitcast_fusion.frequency_ref, bf16[8016,512]{1,0:T(8,128)(2,1)} %table_ref.1), custom_call_target="tpu_custom_call" | custom-call | tf_op jit(solution)/shard_map/pick/pallas_call | solution.py:351
  2.8 1.6 %collective-permute-start = (bf16[48,512]{1,0:T(8,128)(2,1)S(1)}, bf16[48,512]{1,0:T(8,128)(2,1)S(1)}, u32[]{:S(2)}, u32[]{:S(2)}) collective-permute-start(bf16[48,512]{1,0:T(8,128)(2,1)S(1)} %get-tuple-element.9.after_ref), channel_id=1, source_target_pairs={{0,1},{1,0},{2,3},{3,2},{4,5},{5,4},{6,7},{7,6},{8,9},{9,8},{10,11... | collective-permute-start | bytes 147464 | tf_op jit(solution)/shard_map/ppermute | solution.py:340
  4.4 0.9 %collective-permute-done = bf16[48,512]{1,0:T(8,128)(2,1)S(1)} collective-permute-done((bf16[48,512]{1,0:T(8,128)(2,1)S(1)}, bf16[48,512]{1,0:T(8,128)(2,1)S(1)}, u32[]{:S(2)}, u32[]{:S(2)}) %collective-permute-start) | collective-permute-done | bytes 49184 | tf_op jit(solution)/shard_map/ppermute | solution.py:340
  5.3 1.8 %collective-permute-start.1 = (bf16[48,512]{1,0:T(8,128)(2,1)S(1)}, bf16[48,512]{1,0:T(8,128)(2,1)S(1)}, u32[]{:S(2)}, u32[]{:S(2)}) collective-permute-start(bf16[48,512]{1,0:T(8,128)(2,1)S(1)} %add.18), channel_id=1, source_target_pairs={{0,2},{1,3},{2,0},{3,1},{4,6},{5,7},{6,4},{7,5},{8,10},{9,11},{10,... | collective-permute-start | bytes 147464 | tf_op jit(solution)/shard_map/ppermute | solution.py:340
  7.1 1.5 %collective-permute-done.1 = bf16[48,512]{1,0:T(8,128)(2,1)S(1)} collective-permute-done((bf16[48,512]{1,0:T(8,128)(2,1)S(1)}, bf16[48,512]{1,0:T(8,128)(2,1)S(1)}, u32[]{:S(2)}, u32[]{:S(2)}) %collective-permute-start.1) | collective-permute-done | bytes 49184 | tf_op jit(solution)/shard_map/ppermute | solution.py:340
  8.6 3.4 %collective-permute-start.2 = (bf16[48,512]{1,0:T(8,128)(2,1)S(1)}, bf16[48,512]{1,0:T(8,128)(2,1)S(1)}, u32[]{:S(2)}, u32[]{:S(2)}) collective-permute-start(bf16[48,512]{1,0:T(8,128)(2,1)S(1)} %add.19), channel_id=1, source_target_pairs={{0,6},{1,7},{2,4},{3,5},{4,2},{5,3},{6,0},{7,1},{8,14},{9,15},{10,... | collective-permute-start | bytes 147464 | tf_op jit(solution)/shard_map/ppermute | solution.py:340
  12.0 0.0 copy-done.2
  12.0 1.3 %fetch.1.w_ref = bf16[512,1280]{1,0:T(8,128)(2,1)S(1)} custom-call(bf16[48,512]{1,0:T(8,128)(2,1)S(1)} %get-tuple-element.9.after_ref, bf16[512,1280]{1,0:T(8,128)(2,1)} %bitcast.16), custom_call_target="tpu_custom_call" | custom-call | bytes 2621440 | tf_op jit(solution)/shard_map/fetch/pallas_call | solution.py:147
  13.3 0.1 collective-permute-done.2
  13.5 0.4 project.1
  13.9 14.2 %all_to_all.20.parts_ref = f32[16,32,128]{2,1,0:T(8,128)S(1)} all-to-all(f32[16,32,128]{2,1,0:T(8,128)S(1)} %bitcast.13), channel_id=1, replica_groups=mesh['seq'=16,'head'=8] {'seq'}, dimensions={0} | all-to-all | bytes 524288 | tf_op jit(solution)/shard_map/all_to_all | solution.py:48
  28.1 0.2 finish.1
  28.3 9.6 %all_to_all.21.rows_ref = bf16[16,32,128]{2,1,0:T(8,128)(2,1)S(1)} all-to-all(bf16[16,32,128]{2,1,0:T(8,128)(2,1)S(1)} %finish.1), channel_id=1, replica_groups=mesh['seq'=16,'head'=8] {'seq'}, dimensions={0} | all-to-all | bytes 262144 | tf_op jit(solution)/shard_map/all_to_all | solution.py:48
  38.0 0.0 slice-done
  38.0 0.0 slice-done.1
  38.0 0.0 copy-done
  38.0 0.0 copy-start.1
  38.0 3.0 %attend.1 = f32[16,7,4,128]{3,2,1,0:T(4,128)S(1)} custom-call(s32[8,128]{1,0:T(8,128)S(1)} %get-tuple-element.8.limits_ref, bf16[16,32,128]{2,1,0:T(8,128)(2,1)S(1)} %all_to_all.21.rows_ref, bf16[24,1024,128]{2,1,0:T(8,128)(2,1)S(1)} %bitcast.11, bf16[24,1024,128]{2,1,0:T(8,128)(2,1)S(1)} %bitcast.12), custom_call_target="tpu_custom_call" | custom-call | tf_op jit(solution)/shard_map/attend/pallas_call | solution.py:386
  41.0 10.2 %all_to_all.22.parts_ref = f32[16,7,4,128]{3,2,1,0:T(4,128)S(1)} all-to-all(f32[16,7,4,128]{3,2,1,0:T(4,128)S(1)} %attend.1), channel_id=1, replica_groups=mesh['seq'=16,'head'=8] {'seq'}, dimensions={0} | all-to-all | bytes 458752 | tf_op jit(solution)/shard_map/all_to_all | solution.py:48
  51.1 0.3 merge.1
  51.5 9.3 %all_to_all.23.attention_ref = bf16[16,8,384]{2,1,0:T(8,128)(2,1)S(1)} all-to-all(bf16[16,8,384]{2,1,0:T(8,128)(2,1)S(1)} %merge.1), channel_id=1, replica_groups=mesh['seq'=16,'head'=8] {'seq'}, dimensions={0} | all-to-all | bytes 196608 | tf_op jit(solution)/shard_map/all_to_all | solution.py:48
  60.8 0.0 copy-done.1
  60.8 0.3 output.1
  61.1 0.0 collective-permute-start.3
  61.1 3.8 %collective-permute-done.3 = f32[48,512]{1,0:T(8,128)S(1)} collective-permute-done((f32[48,512]{1,0:T(8,128)S(1)}, f32[48,512]{1,0:T(8,128)S(1)}, u32[]{:S(2)}, u32[]{:S(2)}) %collective-permute-start.3) | collective-permute-done | bytes 98336 | tf_op jit(solution)/shard_map/ppermute | solution.py:340
  64.9 2.4 %collective-permute-start.4 = (f32[48,512]{1,0:T(8,128)S(1)}, f32[48,512]{1,0:T(8,128)S(1)}, u32[]{:S(2)}, u32[]{:S(2)}) collective-permute-start(f32[48,512]{1,0:T(8,128)S(1)} %add.21), channel_id=1, source_target_pairs={{0,6},{1,7},{2,4},{3,5},{4,2},{5,3},{6,0},{7,1},{8,14},{9,15},{10,... | collective-permute-start | bytes 294920 | tf_op jit(solution)/shard_map/ppermute | solution.py:340
  67.2 2.4 %collective-permute-done.4 = f32[48,512]{1,0:T(8,128)S(1)} collective-permute-done((f32[48,512]{1,0:T(8,128)S(1)}, f32[48,512]{1,0:T(8,128)S(1)}, u32[]{:S(2)}, u32[]{:S(2)}) %collective-permute-start.4) | collective-permute-done | bytes 98336 | tf_op jit(solution)/shard_map/ppermute | solution.py:340
  69.6 9.9 %collective-permute-start.5 = (f32[48,512]{1,0:T(8,128)S(1)}, f32[48,512]{1,0:T(8,128)S(1)}, u32[]{:S(2)}, u32[]{:S(2)}) collective-permute-start(f32[48,512]{1,0:T(8,128)S(1)} %add.22), channel_id=1, source_target_pairs={{0,1},{1,0},{2,3},{3,2},{4,5},{5,4},{6,7},{7,6},{8,9},{9,8},{10,11... | collective-permute-start | bytes 294920 | tf_op jit(solution)/shard_map/ppermute | solution.py:340
  79.5 0.9 %collective-permute-done.5 = f32[48,512]{1,0:T(8,128)S(1)} collective-permute-done((f32[48,512]{1,0:T(8,128)S(1)}, f32[48,512]{1,0:T(8,128)S(1)}, u32[]{:S(2)}, u32[]{:S(2)}) %collective-permute-start.5) | collective-permute-done | bytes 98336 | tf_op jit(solution)/shard_map/ppermute | solution.py:340
  80.5 0.6 add_convert_fusion
  (8 shorter events, 0.1 us)
Async XLA Ops:
  0.0 12.0 %copy-start.2 = (bf16[512]{0:T(512)(128)(2,1)S(1)}, bf16[512]{0:T(512)(128)(2,1)}, u32[]{:S(2)}) copy-start(bf16[512]{0:T(512)(128)(2,1)} %param.11) | copy-start | bytes 3076
  0.0 38.0 %slice-start = ((s8[6291456]{0:T(1024)(128)(4,1)}), s8[4194304]{0:T(1024)(128)(4,1)S(1)}, s32[]{:S(2)}) async-start(s8[6291456]{0:T(1024)(128)(4,1)} %bitcast.9), calls=%async_computation.4 | async-start | bytes 8388608
  0.1 37.9 %slice-start.1 = ((s8[6291456]{0:T(1024)(128)(4,1)}), s8[2097152]{0:T(1024)(128)(4,1)S(1)}, s32[]{:S(2)}) async-start(s8[6291456]{0:T(1024)(128)(4,1)} %bitcast.9), calls=%async_computation.5 | async-start | bytes 4194304
  0.1 37.9 %copy-start = (bf16[24,1,1024,128]{3,2,1,0:T(8,128)(2,1)S(1)}, bf16[24,1,1024,128]{3,2,1,0:T(8,128)(2,1)}, u32[]{:S(2)}) copy-start(bf16[24,1,1024,128]{3,2,1,0:T(8,128)(2,1)} %param.14) | copy-start | bytes 18874372
  2.8 2.5 %collective-permute-start = (bf16[48,512]{1,0:T(8,128)(2,1)S(1)}, bf16[48,512]{1,0:T(8,128)(2,1)S(1)}, u32[]{:S(2)}, u32[]{:S(2)}) collective-permute-start(bf16[48,512]{1,0:T(8,128)(2,1)S(1)} %get-tuple-element.9.after_ref), channel_id=1, source_target_pairs={{0,1},{1,0},{2,3},{3,2},{4,5},{5,4},{6,7},{7,6},{8,9},{9,8},{10,11... | collective-permute-start | bytes 147464 | tf_op jit(solution)/shard_map/ppermute | solution.py:340
  5.3 3.3 %collective-permute-start.1 = (bf16[48,512]{1,0:T(8,128)(2,1)S(1)}, bf16[48,512]{1,0:T(8,128)(2,1)S(1)}, u32[]{:S(2)}, u32[]{:S(2)}) collective-permute-start(bf16[48,512]{1,0:T(8,128)(2,1)S(1)} %add.18), channel_id=1, source_target_pairs={{0,2},{1,3},{2,0},{3,1},{4,6},{5,7},{6,4},{7,5},{8,10},{9,11},{10,... | collective-permute-start | bytes 147464 | tf_op jit(solution)/shard_map/ppermute | solution.py:340
  8.6 4.9 %collective-permute-start.2 = (bf16[48,512]{1,0:T(8,128)(2,1)S(1)}, bf16[48,512]{1,0:T(8,128)(2,1)S(1)}, u32[]{:S(2)}, u32[]{:S(2)}) collective-permute-start(bf16[48,512]{1,0:T(8,128)(2,1)S(1)} %add.19), channel_id=1, source_target_pairs={{0,6},{1,7},{2,4},{3,5},{4,2},{5,3},{6,0},{7,1},{8,14},{9,15},{10,... | collective-permute-start | bytes 147464 | tf_op jit(solution)/shard_map/ppermute | solution.py:340
  38.0 22.8 %copy-start.1 = (bf16[1,1024,512]{2,1,0:T(8,128)(2,1)S(1)}, bf16[1,1024,512]{2,1,0:T(8,128)(2,1)}, u32[]{:S(2)}) copy-start(bf16[1,1024,512]{2,1,0:T(8,128)(2,1)} %param.15) | copy-start | bytes 3145732
  61.1 3.8 %collective-permute-start.3 = (f32[48,512]{1,0:T(8,128)S(1)}, f32[48,512]{1,0:T(8,128)S(1)}, u32[]{:S(2)}, u32[]{:S(2)}) collective-permute-start(f32[48,512]{1,0:T(8,128)S(1)} %output.1), channel_id=1, source_target_pairs={{0,2},{1,3},{2,0},{3,1},{4,6},{5,7},{6,4},{7,5},{8,10},{9,11},{10,... | collective-permute-start | bytes 294920 | tf_op jit(solution)/shard_map/ppermute | solution.py:340
  64.9 4.8 %collective-permute-start.4 = (f32[48,512]{1,0:T(8,128)S(1)}, f32[48,512]{1,0:T(8,128)S(1)}, u32[]{:S(2)}, u32[]{:S(2)}) collective-permute-start(f32[48,512]{1,0:T(8,128)S(1)} %add.21), channel_id=1, source_target_pairs={{0,6},{1,7},{2,4},{3,5},{4,2},{5,3},{6,0},{7,1},{8,14},{9,15},{10,... | collective-permute-start | bytes 294920 | tf_op jit(solution)/shard_map/ppermute | solution.py:340
  69.6 10.8 %collective-permute-start.5 = (f32[48,512]{1,0:T(8,128)S(1)}, f32[48,512]{1,0:T(8,128)S(1)}, u32[]{:S(2)}, u32[]{:S(2)}) collective-permute-start(f32[48,512]{1,0:T(8,128)S(1)} %add.22), channel_id=1, source_target_pairs={{0,1},{1,0},{2,3},{3,2},{4,5},{5,4},{6,7},{7,6},{8,9},{9,8},{10,11... | collective-permute-start | bytes 294920 | tf_op jit(solution)/shard_map/ppermute | solution.py:340

commit v11 on v8

--- a/solution.py
+++ b/solution.py
@@ -13,6 +13,7 @@
 SUB = 8
 BLOCK = 32
 SPAN = 32
+HALF = 4
 
 rope_base = 500000.0
 epsilon = 1e-05
@@ -264,7 +265,9 @@
             axis=0,
         ) + jnp.dot(fresh.T.astype(jnp.bfloat16), new_values, preferred_element_type=jnp.float32)
         for j in range(count):
-            out_ref[j, pl.ds(g * SUB, SUB)] = value[j * SUB : (j + 1) * SUB]
+            for h in range(2):
+                start = j * SUB + h * HALF
+                out_ref[j, 2 * g + h] = value[start : start + HALF]
         return total
 
     tops, totals = [], []
@@ -274,31 +277,39 @@
         tops.append(ready[0])
         totals.append(weigh(g, *ready))
         ready = later
-    spare = jnp.zeros((SUB - 2 * groups, LANES), jnp.float32)
-    stats = jnp.concatenate(tops + totals + [spare], axis=0)
+    spare = jnp.zeros((SUB - groups, LANES), jnp.float32)
+    tops = jnp.concatenate(tops + [spare], axis=0)
+    totals = pltpu.roll(jnp.concatenate(totals + [spare], axis=0), SUB, 1)
     for j in range(count):
         turn = (LANES - SUB * j) % LANES
-        out_ref[j, pl.ds(groups * SUB, SUB)] = pltpu.roll(stats, turn, 1) if turn else stats
+        both = jnp.where(
+            lane < SUB,
+            pltpu.roll(tops, turn, 1) if turn else tops,
+            pltpu.roll(totals, turn, 1) if turn else totals,
+        )
+        out_ref[j, 2 * groups] = both[:HALF]
 
 
 def merge_kernel(parts_ref, out_ref):
-    count, rows, head_dim = parts_ref.shape
-    groups = rows // SUB - 1
-    stats = parts_ref[:, groups * SUB :]
+    count, pieces, _, head_dim = parts_ref.shape
+    groups = pieces // 2
+    stats = [parts_ref[j, 2 * groups] for j in range(count)]
     top = stats[0]
     for j in range(1, count):
         top = jnp.maximum(top, stats[j])
-    factors = [jnp.exp(stats[j] - top) for j in range(count)]
-    denominator = factors[0] * pltpu.roll(stats[0], SUB - groups, 0)
-    for j in range(1, count):
-        denominator = denominator + factors[j] * pltpu.roll(stats[j], SUB - groups, 0)
-    shares = jnp.concatenate([factor / denominator for factor in factors], axis=0).T[:SUB]
+    factors = [jnp.exp(jnp.minimum(stats[j] - top, 0.0)) for j in range(count)]
+    denominator = jnp.zeros((HALF, head_dim), jnp.float32)
+    for j in range(count):
+        denominator = denominator + factors[j] * pltpu.roll(stats[j], head_dim - SUB, 1)
+    shares = jnp.concatenate([factor / denominator for factor in factors], axis=0)
+    shares = jnp.concatenate([shares, jnp.zeros_like(shares)], axis=0).T[:SUB]
     merged = []
     for g in range(groups):
         total = jnp.zeros((SUB, head_dim), jnp.float32)
         for j in range(count):
-            column = j * SUB + g
-            total = total + parts_ref[j, pl.ds(g * SUB, SUB)] * shares[:, column : column + 1]
+            column = j * HALF + g
+            part = jnp.concatenate([parts_ref[j, 2 * g], parts_ref[j, 2 * g + 1]], axis=0)
+            total = total + part * shares[:, column : column + 1]
         merged.append(total)
     merged = jnp.concatenate(merged, axis=1).astype(jnp.bfloat16)
     for j in range(out_ref.shape[0]):
@@ -368,7 +379,7 @@
     partial = call(
         attend_kernel,
         "attend",
-        ((n_seq, BLOCK, head_dim), jnp.float32),
+        ((n_seq, 2 * own + 1, HALF, head_dim), jnp.float32),
         [VMEM] * 4,
         [pltpu.VMEM((own, cache_dev, LANES), jnp.float32)],
         8,

time: 81.6 us -> 81.4 us (level)
  no operation moved by 1% of the time
where the time goes in v11:
time: 81.4 us; the launch traced here: 80.9 us
  blocking collectives  43.3 us (53%)
  starting transfers between devices  17.8 us (22%)
  waiting for transfers between devices  10.1 us (12%)
  Pallas kernels  8.76 us (11%)
    all_to_all x4, blocking collectives, swap(): return lax.all_to_all(array, axis_name, 0, 0, tiled=True)  43.3 us
    ppermute x6, starting transfers between devices, double(): return array + lax.ppermute(array, axis_name, pairs)  17.8 us
    ppermute x6, waiting for transfers between devices, double(): return array + lax.ppermute(array, axis_name, pairs)  10.1 us
    pallas_call x1, Pallas kernels, body(): call(attend_kernel, 'attend', ((n_seq, 2 * own + 1, HALF, head_dim), jnp....  2.97 us
    pallas_call x1, Pallas kernels, body(): call(pick_kernel, 'pick', ((tokens, feat), jnp.bfloat16), [SMEM, ANY], [p...  2.59 us
    pallas_call x1, Pallas kernels, prepare(): pl.pallas_call(functools.partial(prepare_kernel, cache_dev), out_shape=[j...  1.99 us
  transfers between devices with their start and end apart: 6, of which 5 were waited for; matrix products, arithmetic and copies ran while one was open for 0% of the time, Pallas kernels for 2%

profile of v11, /device:TPU:1, one launch (start us, length us, event | category | flops | bytes accessed | tf_op | source)
XLA Modules:
  0.0 80.9 jit_solution(6602207295088425439)
XLA Ops:
  0.0 0.0 copy-start.3
  0.0 0.0 copy-start.1
  0.0 0.0 copy-start
  0.0 2.6 %pick.1.after_ref = bf16[48,512]{1,0:T(8,128)(2,1)S(1)} custom-call(s32[2,24]{1,0:T(2,128)} %ids_ref.1, bf16[8016,512]{1,0:T(8,128)(2,1)} %table_ref.1), custom_call_target="tpu_custom_call" | custom-call | tf_op jit(solution)/shard_map/pick/pallas_call | solution.py:355
  2.6 1.6 %collective-permute-start = (bf16[48,512]{1,0:T(8,128)(2,1)S(1)}, bf16[48,512]{1,0:T(8,128)(2,1)S(1)}, u32[]{:S(2)}, u32[]{:S(2)}) collective-permute-start(bf16[48,512]{1,0:T(8,128)(2,1)S(1)} %pick.1.after_ref), channel_id=1, source_target_pairs={{0,1},{1,0},{2,3},{3,2},{4,5},{5,4},{6,7},{7,6},{8,9},{9,8},{10,11... | collective-permute-start | bytes 147464 | tf_op jit(solution)/shard_map/ppermute | solution.py:344
  4.2 0.9 %collective-permute-done = bf16[48,512]{1,0:T(8,128)(2,1)S(1)} collective-permute-done((bf16[48,512]{1,0:T(8,128)(2,1)S(1)}, bf16[48,512]{1,0:T(8,128)(2,1)S(1)}, u32[]{:S(2)}, u32[]{:S(2)}) %collective-permute-start) | collective-permute-done | bytes 49184 | tf_op jit(solution)/shard_map/ppermute | solution.py:344
  5.1 1.7 %collective-permute-start.1 = (bf16[48,512]{1,0:T(8,128)(2,1)S(1)}, bf16[48,512]{1,0:T(8,128)(2,1)S(1)}, u32[]{:S(2)}, u32[]{:S(2)}) collective-permute-start(bf16[48,512]{1,0:T(8,128)(2,1)S(1)} %add.18), channel_id=1, source_target_pairs={{0,2},{1,3},{2,0},{3,1},{4,6},{5,7},{6,4},{7,5},{8,10},{9,11},{10,... | collective-permute-start | bytes 147464 | tf_op jit(solution)/shard_map/ppermute | solution.py:344
  6.9 1.5 %collective-permute-done.1 = bf16[48,512]{1,0:T(8,128)(2,1)S(1)} collective-permute-done((bf16[48,512]{1,0:T(8,128)(2,1)S(1)}, bf16[48,512]{1,0:T(8,128)(2,1)S(1)}, u32[]{:S(2)}, u32[]{:S(2)}) %collective-permute-start.1) | collective-permute-done | bytes 49184 | tf_op jit(solution)/shard_map/ppermute | solution.py:344
  8.3 3.5 %collective-permute-start.2 = (bf16[48,512]{1,0:T(8,128)(2,1)S(1)}, bf16[48,512]{1,0:T(8,128)(2,1)S(1)}, u32[]{:S(2)}, u32[]{:S(2)}) collective-permute-start(bf16[48,512]{1,0:T(8,128)(2,1)S(1)} %add.19), channel_id=1, source_target_pairs={{0,6},{1,7},{2,4},{3,5},{4,2},{5,3},{6,0},{7,1},{8,14},{9,15},{10,... | collective-permute-start | bytes 147464 | tf_op jit(solution)/shard_map/ppermute | solution.py:344
  11.8 0.1 maximum_bitcast_fusion.frequency_ref
  11.9 0.0 copy-done.3
  11.9 2.0 %prepare.1 = (f32[64,128]{1,0:T(8,128)S(1)}, s32[8,128]{1,0:T(8,128)S(1)}, bf16[512,1280]{1,0:T(8,128)(2,1)S(1)}) custom-call(bf16[48,512]{1,0:T(8,128)(2,1)S(1)} %pick.1.after_ref, s32[24]{0:T(128)} %lengths_ref.1, f32[1,128]{1,0:T(1,128)S(1)} %maximum_bitcast_fusion.frequency_ref, bf16[512,1280]{1,0:T(8,128)(2,1)} %bitcast.14), custom_call_target="tpu_custom_call" | custom-call | bytes 2621440 | tf_op jit(solution)/shard_map/prepare/pallas_call | solution.py:147
  13.9 0.0 collective-permute-done.2
  13.9 0.4 project.1
  14.3 14.1 %all_to_all.20.parts_ref = f32[16,32,128]{2,1,0:T(8,128)S(1)} all-to-all(f32[16,32,128]{2,1,0:T(8,128)S(1)} %bitcast.11), channel_id=1, replica_groups=mesh['seq'=16,'head'=8] {'seq'}, dimensions={0} | all-to-all | bytes 524288 | tf_op jit(solution)/shard_map/all_to_all | solution.py:48
  28.4 0.2 finish.1
  28.6 9.8 %all_to_all.21.rows_ref = bf16[16,32,128]{2,1,0:T(8,128)(2,1)S(1)} all-to-all(bf16[16,32,128]{2,1,0:T(8,128)(2,1)S(1)} %finish.1), channel_id=1, replica_groups=mesh['seq'=16,'head'=8] {'seq'}, dimensions={0} | all-to-all | bytes 262144 | tf_op jit(solution)/shard_map/all_to_all | solution.py:48
  38.4 0.0 copy-done.1
  38.4 0.0 copy-done
  38.4 0.0 copy-start.2
  38.4 3.0 %attend.1 = f32[16,7,4,128]{3,2,1,0:T(4,128)S(1)} custom-call(s32[8,128]{1,0:T(8,128)S(1)} %get-tuple-element.8.limits_ref, bf16[16,32,128]{2,1,0:T(8,128)(2,1)S(1)} %all_to_all.21.rows_ref, bf16[24,1024,128]{2,1,0:T(8,128)(2,1)S(1)} %bitcast.9, bf16[24,1024,128]{2,1,0:T(8,128)(2,1)S(1)} %bitcast.10), custom_call_target="tpu_custom_call" | custom-call | tf_op jit(solution)/shard_map/attend/pallas_call | solution.py:379
  41.4 10.2 %all_to_all.22.parts_ref = f32[16,7,4,128]{3,2,1,0:T(4,128)S(1)} all-to-all(f32[16,7,4,128]{3,2,1,0:T(4,128)S(1)} %attend.1), channel_id=1, replica_groups=mesh['seq'=16,'head'=8] {'seq'}, dimensions={0} | all-to-all | bytes 458752 | tf_op jit(solution)/shard_map/all_to_all | solution.py:48
  51.5 0.3 merge.1
  51.9 9.3 %all_to_all.23.attention_ref = bf16[16,8,384]{2,1,0:T(8,128)(2,1)S(1)} all-to-all(bf16[16,8,384]{2,1,0:T(8,128)(2,1)S(1)} %merge.1), channel_id=1, replica_groups=mesh['seq'=16,'head'=8] {'seq'}, dimensions={0} | all-to-all | bytes 196608 | tf_op jit(solution)/shard_map/all_to_all | solution.py:48
  61.2 0.0 copy-done.2
  61.2 0.3 output.1
  61.5 0.0 collective-permute-start.3
  61.5 3.8 %collective-permute-done.3 = f32[48,512]{1,0:T(8,128)S(1)} collective-permute-done((f32[48,512]{1,0:T(8,128)S(1)}, f32[48,512]{1,0:T(8,128)S(1)}, u32[]{:S(2)}, u32[]{:S(2)}) %collective-permute-start.3) | collective-permute-done | bytes 98336 | tf_op jit(solution)/shard_map/ppermute | solution.py:344
  65.3 1.7 %collective-permute-start.4 = (f32[48,512]{1,0:T(8,128)S(1)}, f32[48,512]{1,0:T(8,128)S(1)}, u32[]{:S(2)}, u32[]{:S(2)}) collective-permute-start(f32[48,512]{1,0:T(8,128)S(1)} %add.21), channel_id=1, source_target_pairs={{0,6},{1,7},{2,4},{3,5},{4,2},{5,3},{6,0},{7,1},{8,14},{9,15},{10,... | collective-permute-start | bytes 294920 | tf_op jit(solution)/shard_map/ppermute | solution.py:344
  67.0 3.0 %collective-permute-done.4 = f32[48,512]{1,0:T(8,128)S(1)} collective-permute-done((f32[48,512]{1,0:T(8,128)S(1)}, f32[48,512]{1,0:T(8,128)S(1)}, u32[]{:S(2)}, u32[]{:S(2)}) %collective-permute-start.4) | collective-permute-done | bytes 98336 | tf_op jit(solution)/shard_map/ppermute | solution.py:344
  70.1 9.3 %collective-permute-start.5 = (f32[48,512]{1,0:T(8,128)S(1)}, f32[48,512]{1,0:T(8,128)S(1)}, u32[]{:S(2)}, u32[]{:S(2)}) collective-permute-start(f32[48,512]{1,0:T(8,128)S(1)} %add.22), channel_id=1, source_target_pairs={{0,1},{1,0},{2,3},{3,2},{4,5},{5,4},{6,7},{7,6},{8,9},{9,8},{10,11... | collective-permute-start | bytes 294920 | tf_op jit(solution)/shard_map/ppermute | solution.py:344
  79.3 0.9 %collective-permute-done.5 = f32[48,512]{1,0:T(8,128)S(1)} collective-permute-done((f32[48,512]{1,0:T(8,128)S(1)}, f32[48,512]{1,0:T(8,128)S(1)}, u32[]{:S(2)}, u32[]{:S(2)}) %collective-permute-start.5) | collective-permute-done | bytes 98336 | tf_op jit(solution)/shard_map/ppermute | solution.py:344
  80.3 0.6 add_convert_fusion
  (7 shorter events, 0.1 us)
Async XLA Ops:
  0.0 11.9 %copy-start.3 = (bf16[512]{0:T(512)(128)(2,1)S(1)}, bf16[512]{0:T(512)(128)(2,1)}, u32[]{:S(2)}) copy-start(bf16[512]{0:T(512)(128)(2,1)} %param.11) | copy-start | bytes 3076
  0.0 38.4 %copy-start.1 = (bf16[24,1,1024,128]{3,2,1,0:T(8,128)(2,1)S(1)}, bf16[24,1,1024,128]{3,2,1,0:T(8,128)(2,1)}, u32[]{:S(2)}) copy-start(bf16[24,1,1024,128]{3,2,1,0:T(8,128)(2,1)} %param.14) | copy-start | bytes 18874372
  0.0 38.4 %copy-start = (bf16[24,1,1024,128]{3,2,1,0:T(8,128)(2,1)S(1)}, bf16[24,1,1024,128]{3,2,1,0:T(8,128)(2,1)}, u32[]{:S(2)}) copy-start(bf16[24,1,1024,128]{3,2,1,0:T(8,128)(2,1)} %param.13) | copy-start | bytes 18874372
  2.6 2.5 %collective-permute-start = (bf16[48,512]{1,0:T(8,128)(2,1)S(1)}, bf16[48,512]{1,0:T(8,128)(2,1)S(1)}, u32[]{:S(2)}, u32[]{:S(2)}) collective-permute-start(bf16[48,512]{1,0:T(8,128)(2,1)S(1)} %pick.1.after_ref), channel_id=1, source_target_pairs={{0,1},{1,0},{2,3},{3,2},{4,5},{5,4},{6,7},{7,6},{8,9},{9,8},{10,11... | collective-permute-start | bytes 147464 | tf_op jit(solution)/shard_map/ppermute | solution.py:344
  5.1 3.2 %collective-permute-start.1 = (bf16[48,512]{1,0:T(8,128)(2,1)S(1)}, bf16[48,512]{1,0:T(8,128)(2,1)S(1)}, u32[]{:S(2)}, u32[]{:S(2)}) collective-permute-start(bf16[48,512]{1,0:T(8,128)(2,1)S(1)} %add.18), channel_id=1, source_target_pairs={{0,2},{1,3},{2,0},{3,1},{4,6},{5,7},{6,4},{7,5},{8,10},{9,11},{10,... | collective-permute-start | bytes 147464 | tf_op jit(solution)/shard_map/ppermute | solution.py:344
  8.3 5.6 %collective-permute-start.2 = (bf16[48,512]{1,0:T(8,128)(2,1)S(1)}, bf16[48,512]{1,0:T(8,128)(2,1)S(1)}, u32[]{:S(2)}, u32[]{:S(2)}) collective-permute-start(bf16[48,512]{1,0:T(8,128)(2,1)S(1)} %add.19), channel_id=1, source_target_pairs={{0,6},{1,7},{2,4},{3,5},{4,2},{5,3},{6,0},{7,1},{8,14},{9,15},{10,... | collective-permute-start | bytes 147464 | tf_op jit(solution)/shard_map/ppermute | solution.py:344
  38.4 22.8 %copy-start.2 = (bf16[1,1024,512]{2,1,0:T(8,128)(2,1)S(1)}, bf16[1,1024,512]{2,1,0:T(8,128)(2,1)}, u32[]{:S(2)}) copy-start(bf16[1,1024,512]{2,1,0:T(8,128)(2,1)} %param.15) | copy-start | bytes 3145732
  61.5 3.8 %collective-permute-start.3 = (f32[48,512]{1,0:T(8,128)S(1)}, f32[48,512]{1,0:T(8,128)S(1)}, u32[]{:S(2)}, u32[]{:S(2)}) collective-permute-start(f32[48,512]{1,0:T(8,128)S(1)} %output.1), channel_id=1, source_target_pairs={{0,2},{1,3},{2,0},{3,1},{4,6},{5,7},{6,4},{7,5},{8,10},{9,11},{10,... | collective-permute-start | bytes 294920 | tf_op jit(solution)/shard_map/ppermute | solution.py:344
  65.3 4.8 %collective-permute-start.4 = (f32[48,512]{1,0:T(8,128)S(1)}, f32[48,512]{1,0:T(8,128)S(1)}, u32[]{:S(2)}, u32[]{:S(2)}) collective-permute-start(f32[48,512]{1,0:T(8,128)S(1)} %add.21), channel_id=1, source_target_pairs={{0,6},{1,7},{2,4},{3,5},{4,2},{5,3},{6,0},{7,1},{8,14},{9,15},{10,... | collective-permute-start | bytes 294920 | tf_op jit(solution)/shard_map/ppermute | solution.py:344
  70.1 10.2 %collective-permute-start.5 = (f32[48,512]{1,0:T(8,128)S(1)}, f32[48,512]{1,0:T(8,128)S(1)}, u32[]{:S(2)}, u32[]{:S(2)}) collective-permute-start(f32[48,512]{1,0:T(8,128)S(1)} %add.22), channel_id=1, source_target_pairs={{0,1},{1,0},{2,3},{3,2},{4,5},{5,4},{6,7},{7,6},{8,9},{9,8},{10,11... | collective-permute-start | bytes 294920 | tf_op jit(solution)/shard_map/ppermute | solution.py:344
